TPU v7x, 256 devices: a whole 4x4x8 slice. The times are simulated.
256 devices in a mesh: ctx: 32 (over x, y, core), head: 8 (over z).
Axes of the slice: x: 4, y: 4, z: 8, core: 2. Of those that a mesh axis runs over, the one named last changes fastest.
Arguments:
- queries: bfloat16 [8192, 4096], P('ctx', 'head'), may hold values from -6 to 6
- keys_in: bfloat16 [8192, 4096], P('ctx', 'head'), may hold values from -6 to 6
- values: bfloat16 [8192, 4096], P('ctx', 'head'), may hold values from -12 to 12
- norm_gain: float32 [4096], P('head'), may hold values from 0.25 to 1.75
- out_grad: bfloat16 [8192, 4096], P('ctx', 'head'), may hold values from -6 to 6
Outputs:
- normed: bfloat16 [8192, 4096], P('ctx', 'head')
- query_grad: bfloat16 [8192, 4096], P('ctx', 'head')
- key_grad: bfloat16 [8192, 4096], P('ctx', 'head')
- value_grad: bfloat16 [8192, 4096], P('ctx', 'head')
- gain_grad: float32 [4096], P('head')
All inputs are finite; a program needn't handle non-finite values.
Results may differ from a plain program's by a relative error of at most 0.02.
The roundings to bfloat16 on the way count: a program that leaves them out, or rounds other values in their place, can miss the bound.
Values may be sent and summed in bfloat16 or wider, within the bound.
No kernel may reach another device: no remote copies, remote signals or barrier semaphores. Data moves between devices by JAX's collectives and lax.ppermute only.
A program may use at most 64 MiB of HBM per device.

v0:
```python
import jax
import jax.numpy as jnp
from jax import lax
from jax.sharding import PartitionSpec as P

DH = 128
M = 256
ITERS = 2


HIGH_PRECISION = lax.Precision.HIGHEST
EPS = 1e-06


def newton_inverse(matrix):
    column_total = jnp.max(jnp.sum(matrix, axis=-2), axis=-1)
    factor = lax.stop_gradient(1.0 / column_total)
    approx = jnp.swapaxes(matrix, -1, -2) * factor[..., None, None]
    identity_m = jnp.eye(matrix.shape[-1], dtype=jnp.float32)
    for sweep_index in range(ITERS):
        product = jnp.einsum("...ij,...jk->...ik", matrix, approx, precision=HIGH_PRECISION)
        inner_term = 7.0 * identity_m - product
        inner_term = 15.0 * identity_m - jnp.einsum(
            "...ij,...jk->...ik", product, inner_term, precision=HIGH_PRECISION
        )
        inner_term = 13.0 * identity_m - jnp.einsum(
            "...ij,...jk->...ik", product, inner_term, precision=HIGH_PRECISION
        )
        approx = 0.25 * jnp.einsum(
            "...ij,...jk->...ik", approx, inner_term, precision=HIGH_PRECISION
        )
    return approx


def mix_weights(kernel_two, context):
    return jnp.einsum(
        "...ij,...jk->...ik", newton_inverse(kernel_two), context, precision=HIGH_PRECISION
    )


def local_means(tokens_block, land_dev, seg_len):
    summed = jnp.sum(
        tokens_block.reshape(land_dev, seg_len, tokens_block.shape[1]).astype(jnp.float32), axis=1
    )
    return (summed / seg_len).astype(jnp.bfloat16)


def spread_rows(per_token, per_land, seg_len):
    land_dev = per_land.shape[1]
    shaped = per_token.reshape(land_dev, seg_len, per_token.shape[1], per_token.shape[2])
    landmark_part = jnp.transpose(per_land, (1, 0, 2)) / seg_len
    total = shaped + landmark_part[:, None]
    return total.reshape(per_token.shape[0], per_token.shape[1] * per_token.shape[2]).astype(
        jnp.bfloat16
    )


def on_device(queries, keys_in, values, norm_gain, out_grad):
    tok_rows, width_dev = queries.shape
    heads_dev = width_dev // DH
    land_dev = M // lax.axis_size("ctx")
    seg_len = tok_rows // land_dev
    feature_total = width_dev * lax.axis_size("head")
    scale_q = DH ** (-0.5)
    query_per_head = queries.reshape(tok_rows, heads_dev, DH)
    key_per_head = keys_in.reshape(tok_rows, heads_dev, DH)
    value_per_head = values.reshape(tok_rows, heads_dev, DH)
    own_q = local_means(queries, land_dev, seg_len)
    own_k = local_means(keys_in, land_dev, seg_len)
    land_q, land_k = (
        lax.all_gather(own_q, "ctx", axis=0, tiled=True),
        lax.all_gather(own_k, "ctx", axis=0, tiled=True),
    )
    landmark_query_heads = land_q.reshape(M, heads_dev, DH)
    landmark_key_heads = land_k.reshape(M, heads_dev, DH)
    kernel_one = jax.nn.softmax(
        jnp.einsum(
            "yci,pci->ycp", query_per_head, landmark_key_heads, preferred_element_type=jnp.float32
        )
        * scale_q,
        axis=-1,
    )
    kernel_first_batched = kernel_one.astype(jnp.bfloat16)
    kernel_two = jax.nn.softmax(
        jnp.einsum(
            "tix,uix->itu",
            landmark_query_heads,
            landmark_key_heads,
            preferred_element_type=jnp.float32,
        )
        * scale_q,
        axis=-1,
    )
    score_three = (
        jnp.einsum(
            "rqi,oqi->qro", landmark_query_heads, key_per_head, preferred_element_type=jnp.float32
        )
        * scale_q
    )
    row_top = lax.pmax(jnp.max(score_three, axis=-1), "ctx")
    exp_three = jnp.exp(score_three - row_top[..., None])
    exp_third_batched = exp_three.astype(jnp.bfloat16)
    local_weighted = jnp.einsum(
        "xrz,zxg->xrg", exp_third_batched, value_per_head, preferred_element_type=jnp.float32
    )
    totals, weighted = lax.psum((jnp.sum(exp_three, axis=-1), local_weighted), "ctx")
    context = weighted / totals[..., None]
    mixing_batched = mix_weights(kernel_two, context).astype(jnp.bfloat16)
    output = jnp.einsum(
        "pzj,zji->pzi", kernel_first_batched, mixing_batched, preferred_element_type=jnp.float32
    ).reshape(tok_rows, width_dev)
    square_sum = lax.psum(jnp.sum(output * output, axis=-1), "head")
    root_inv = lax.rsqrt(square_sum / feature_total + EPS)
    normed = (output * root_inv[:, None] * norm_gain).astype(jnp.bfloat16)
    grad_float = out_grad.astype(jnp.float32)
    scaled_grad = grad_float * norm_gain
    slope_sum = lax.psum(jnp.sum(scaled_grad * output, axis=-1), "head")
    slope_dot = slope_sum * root_inv / feature_total
    d_output = (
        root_inv[:, None] * (scaled_grad - output * (root_inv * slope_dot)[:, None])
    ).astype(jnp.bfloat16)
    output_grad_heads = d_output.reshape(tok_rows, heads_dev, DH)
    local_mixing = jnp.einsum(
        "pxe,pxb->xeb", kernel_first_batched, output_grad_heads, preferred_element_type=jnp.float32
    )
    local_gain = jnp.sum(grad_float * output * root_inv[:, None], axis=0)
    grad_mixing, gain_grad = lax.psum((local_mixing, local_gain), "ctx")
    gradient_kernel_first = jnp.einsum(
        "nqa,qia->nqi", output_grad_heads, mixing_batched, preferred_element_type=jnp.float32
    )
    gradient_score_first = (
        kernel_one
        * (
            gradient_kernel_first
            - jnp.sum(kernel_one * gradient_kernel_first, axis=-1, keepdims=True)
        )
    ).astype(jnp.bfloat16)
    query_one = (
        jnp.einsum(
            "fcv,vcq->fcq",
            gradient_score_first,
            landmark_key_heads,
            preferred_element_type=jnp.float32,
        )
        * scale_q
    )
    keyland_one = (
        jnp.einsum(
            "pxe,pxb->xeb", gradient_score_first, query_per_head, preferred_element_type=jnp.float32
        )
        * scale_q
    )
    unused, pull_back = jax.vjp(mix_weights, kernel_two, context)
    grad_ktwo, grad_context = pull_back(grad_mixing)
    gradient_score_second = kernel_two * (
        grad_ktwo - jnp.sum(kernel_two * grad_ktwo, axis=-1, keepdims=True)
    )
    queryland_two = (
        jnp.einsum(
            "sec,csq->seq",
            gradient_score_second,
            landmark_key_heads.astype(jnp.float32),
            precision=HIGH_PRECISION,
        )
        * scale_q
    )
    keyland_two = (
        jnp.einsum(
            "gsi,sge->gie",
            gradient_score_second,
            landmark_query_heads.astype(jnp.float32),
            precision=HIGH_PRECISION,
        )
        * scale_q
    )
    grad_totals = -jnp.sum(grad_context * context, axis=-1) / totals
    weighted_gradient = (grad_context / totals[..., None]).astype(jnp.bfloat16)
    grad_exp = (
        jnp.einsum(
            "ygn,vyn->ygv", weighted_gradient, value_per_head, preferred_element_type=jnp.float32
        )
        + grad_totals[..., None]
    )
    gradient_score_third = (exp_three * grad_exp).astype(jnp.bfloat16)
    value_grad = (
        jnp.einsum(
            "lir,lif->rlf", exp_third_batched, weighted_gradient, preferred_element_type=jnp.float32
        )
        .astype(jnp.bfloat16)
        .reshape(tok_rows, width_dev)
    )
    queryland_three = (
        jnp.einsum(
            "xrz,zxg->xrg", gradient_score_third, key_per_head, preferred_element_type=jnp.float32
        )
        * scale_q
    )
    key_three = (
        jnp.einsum(
            "grj,rgs->jgs",
            gradient_score_third,
            landmark_query_heads,
            preferred_element_type=jnp.float32,
        )
        * scale_q
    )
    first_row = lax.axis_index("ctx") * land_dev
    key_whole, query_whole = (
        lax.psum(keyland_one.astype(jnp.bfloat16), "ctx").astype(jnp.float32),
        lax.psum(queryland_three.astype(jnp.bfloat16), "ctx").astype(jnp.float32),
    )
    key_own = lax.dynamic_slice_in_dim(key_whole, first_row, land_dev, 1)
    query_own = lax.dynamic_slice_in_dim(query_whole, first_row, land_dev, 1)
    query_land = lax.dynamic_slice_in_dim(queryland_two, first_row, land_dev, 1) + query_own
    key_land = key_own + lax.dynamic_slice_in_dim(keyland_two, first_row, land_dev, 1)
    query_grad = spread_rows(query_one, query_land, seg_len)
    key_grad = spread_rows(key_three, key_land, seg_len)
    return (normed, query_grad, key_grad, value_grad, gain_grad)


def solution(mesh):
    return jax.shard_map(
        on_device,
        mesh=mesh,
        in_specs=(
            P("ctx", "head"),
            P("ctx", "head"),
            P("ctx", "head"),
            P("head"),
            P("ctx", "head"),
        ),
        out_specs=(
            P("ctx", "head"),
            P("ctx", "head"),
            P("ctx", "head"),
            P("ctx", "head"),
            P("head"),
        ),
        check_vma=False,
    )
```

profile of v0, /device:TPU:1, one launch (start us, length us, event | category | flops | bytes accessed | tf_op | source)
XLA Modules:
  0.0 549.7 jit_solution(12470979238231249681)
XLA Ops:
  8.3 26.4 %all_gather.6 = bf16[256,512]{1,0:T(8,128)(2,1)S(1)} all-gather(bf16[8,512]{1,0:T(8,128)(2,1)S(1)} %multiply_convert_fusion.3), channel_id=1, replica_groups=mesh['ctx'=32,'head'=8] {'ctx'}, dimensions={0}, use_global_device_ids=true | all-gather | bytes 270336 | tf_op jit(solution)/shard_map/all_gather | solution.py:71
  36.1 62.2 %pmax.7 = f32[4,256]{1,0:T(4,128)S(1)} all-reduce(f32[4,256]{1,0:T(4,128)S(1)} %get-tuple-element.33), channel_id=1, replica_groups=mesh['ctx'=32,'head'=8] {'ctx'}, use_global_device_ids=true, to_apply=%region_7.0 | all-reduce | flops 1024 | bytes 8192 | tf_op jit(solution)/shard_map/pmax | solution.py:100
  100.9 24.9 %all_gather.7 = bf16[256,512]{1,0:T(8,128)(2,1)S(1)} all-gather(bf16[8,512]{1,0:T(8,128)(2,1)S(1)} %multiply_convert_fusion.2), channel_id=1, replica_groups=mesh['ctx'=32,'head'=8] {'ctx'}, dimensions={0}, use_global_device_ids=true | all-gather | bytes 270336 | tf_op jit(solution)/shard_map/all_gather | solution.py:72
  129.4 4.8 online-softmax
  134.3 2.8 fusion.11
  139.3 3.2 convolution_multiply_fusion.2
  142.4 4.7 online-softmax.1
  147.1 2.8 fusion.17
  152.2 2.1 convolution_multiply_fusion.1
  154.3 62.2 %psum.57 = f32[4,256]{1,0:T(4,128)S(1)} all-reduce(f32[4,256]{1,0:T(4,128)S(1)} %fusion.38), channel_id=1, replica_groups=mesh['ctx'=32,'head'=8] {'ctx'}, use_global_device_ids=true, to_apply=%region_10.0 | all-reduce | flops 1024 | bytes 8192 | tf_op jit(solution)/shard_map/psum | solution.py:106
  216.5 2.5 fusion.116
  219.0 3.2 convolution_convert_fusion.1
  222.2 2.7 fusion.49
  224.9 16.5 %psum.58 = f32[256]{0:T(256)S(1)} all-reduce(f32[256]{0:T(256)S(1)} %get-tuple-element.37), channel_id=1, replica_groups=mesh['ctx'=32,'head'=8] {'head'}, use_global_device_ids=true, to_apply=%region_14.0 | all-reduce | flops 256 | bytes 2048 | tf_op jit(solution)/shard_map/psum | solution.py:112
  241.4 2.1 copy.164
  245.5 10.7 %psum.59 = f32[256]{0:T(256)S(1)} all-reduce(f32[256]{0:T(256)S(1)} %get-tuple-element.26), channel_id=1, replica_groups=mesh['ctx'=32,'head'=8] {'head'}, use_global_device_ids=true, to_apply=%region_16.0 | all-reduce | flops 256 | bytes 2048 | tf_op jit(solution)/shard_map/psum | solution.py:117
  256.2 2.1 fusion.59
  258.3 2.7 fusion.60
  266.9 72.9 %psum.63 = f32[512]{0:T(512)} all-reduce(f32[512]{0:T(512)S(1)} %get-tuple-element.25), channel_id=1, replica_groups=mesh['ctx'=32,'head'=8] {'ctx'}, use_global_device_ids=true, to_apply=%region_24.0 | all-reduce | flops 512 | bytes 4096 | tf_op jit(solution)/shard_map/psum | solution.py:127
  339.7 2.1 fusion.32
  341.8 36.4 %all-reduce.7.cloned.1.call-done = f32[4,256,128]{2,1,0:T(8,128)} async-done(((f32[4,256,128]{2,1,0:T(8,128)}), f32[4,256,128]{2,1,0:T(8,128)}) %all-reduce.7.cloned.1.call-update) | async-done | bytes 524304 | tf_op jit(solution)/shard_map/psum | solution.py:127
  378.3 2.4 convolution_multiply_fusion
  389.9 2.2 fusion.122
  392.0 2.3 fusion.26
  394.4 2.2 fusion.125
  398.0 2.1 fusion.124
  407.8 2.3 convolution_multiply_fusion.7
  411.2 3.1 fusion.25
  416.4 3.8 fusion.23
  420.3 2.4 multiply_reduce_fusion
  426.4 2.1 fusion.58
  428.5 110.3 %all-reduce.9.cloned.1.call-done = (bf16[4,256,128]{2,1,0:T(8,128)(2,1)}, bf16[4,256,128]{2,1,0:T(8,128)(2,1)}) async-done(((bf16[4,256,128]{2,1,0:T(8,128)(2,1)}, bf16[4,256,128]{2,1,0:T(8,128)(2,1)}), (bf16[4,256,128]{2,1,0:T(8,128)(2,1)}, bf16[4,256,128]{2,1,0:T(8,128)(2,1)})) %all-reduce.9.cloned.1.call-update) | async-done | bytes 524304 | tf_op jit(solution)/shard_map/psum | solution.py:210
  (145 shorter events, 49.8 us)
Async XLA Ops:
  7.2 91.2 %copy-start = (bf16[256,512]{1,0:T(8,128)(2,1)S(1)}, bf16[256,512]{1,0:T(8,128)(2,1)}, u32[]{:S(2)}) copy-start(bf16[256,512]{1,0:T(8,128)(2,1)} %param.7) | copy-start | bytes 786436
  7.2 211.8 %all-reduce.5.cloned.1.call-start = ((), (), s32[]{:S(2)}) async-start(), calls=%async_computation | async-start | bytes 1048576 | tf_op jit(solution)/shard_map/psum | solution.py:106
  34.9 91.2 %copy-start.23 = (bf16[256,512]{0,1:T(8,128)(2,1)}, bf16[256,512]{0,1:T(8,128)(2,1)S(1)}, u32[]{:S(2)}) copy-start(bf16[256,512]{0,1:T(8,128)(2,1)S(1)} %copy.149) | copy-start | bytes 786436
  36.1 64.4 %copy-start.13 = (f32[4,256,256]{2,1,0:T(8,128)}, f32[4,256,256]{2,1,0:T(8,128)S(1)}, u32[]{:S(2)}) copy-start(f32[4,256,256]{2,1,0:T(8,128)S(1)} %get-tuple-element.34) | copy-start | bytes 3145732
  99.6 278.7 %all-reduce.7.cloned.1.call-start = ((), (), s32[]{:S(2)}) async-start(), calls=%async_computation.1 | async-start | bytes 1048576 | tf_op jit(solution)/shard_map/psum | solution.py:127
  99.7 37.3 %copy-start.28 = (f32[256,256]{1,0:T(8,128)}, f32[256,256]{1,0:T(8,128)S(1)}, u32[]{:S(2)}) copy-start(f32[256,256]{1,0:T(8,128)S(1)} %fusion.75) | copy-start | bytes 786436
  129.4 4.8 copy-start.15
  134.2 2.8 copy-start.1
  137.1 2.2 copy-start.4
  142.4 4.7 copy-start.16
  147.1 2.8 copy-start.2
  147.1 2.9 copy-start.29
  150.0 2.2 copy-start.6
  261.0 277.8 %all-reduce.9.cloned.1.call-start = ((), (), s32[]{:S(2)}) async-start(), calls=%async_computation.2 | async-start | bytes 1048576 | tf_op jit(solution)/shard_map/psum | solution.py:210
  261.0 1.8 copy-start.34
  378.3 2.4 copy-start.12
  381.8 1.9 copy-start.10
  384.9 1.9 copy-start.17
  389.9 2.2 copy-start.5
  392.0 2.4 copy-start.22
  396.6 1.4 copy-start.8
  400.1 1.9 copy-start.20
  400.1 1.9 copy-start.38
  400.1 1.9 copy-start.39
  402.0 2.1 copy-start.14
  405.5 1.3 copy-start.36
  407.8 2.3 copy-start.18
  407.8 2.3 copy-start.19
  414.3 1.9 copy-start.32
  416.4 3.9 copy-start.33
  416.4 3.9 copy-start.37
  420.3 3.4 copy-start.24
  (14 other events, 13.5 us)
Sparse Core Ops, SparseCore 0:
  99.7 114.3 all-reduce.4
  261.1 117.1 all-reduce.6
  425.6 113.2 all-reduce.8
where the time goes:
time: 556 us; the launch traced here: 550 us
  blocking collectives  276 us (50%)
  waiting for transfers between devices  147 us (26%)
  matrix products  76.4 us (14%)
  local copies, waits for them, and re-layouts  16.4 us (3%)
  between operations  14.6 us (3%)
  other arithmetic  10.1 us (2%)
  Pallas kernels  9.49 us (2%)
    psum x1, waiting for transfers between devices, on_device(): lax.psum(queryland_three.astype(jnp.bfloat16), 'ctx').astype(jnp.float32)  110 us
    psum x1, blocking collectives, on_device(): grad_mixing, gain_grad = lax.psum((local_mixing, local_gain), 'ctx')  72.9 us
    pmax x1, blocking collectives, on_device(): row_top = lax.pmax(jnp.max(score_three, axis=-1), 'ctx')  62.2 us
    psum x1, blocking collectives, on_device(): lax.psum((jnp.sum(exp_three, axis=-1), local_weighted), 'ctx')  62.2 us
    psum x1, waiting for transfers between devices, on_device(): grad_mixing, gain_grad = lax.psum((local_mixing, local_gain), 'ctx')  36.4 us
    all_gather x1, blocking collectives, on_device(): lax.all_gather(own_q, 'ctx', axis=0, tiled=True)  26.4 us
    all_gather x1, blocking collectives, on_device(): lax.all_gather(own_k, 'ctx', axis=0, tiled=True)  24.9 us
    dot_general x12, matrix products, newton_inverse(): jnp.einsum('...ij,...jk->...ik', product, inner_term, precision=HIGH_PREC...  22.3 us
  transfers between devices with their start and end apart: 3, of which 2 were waited for; matrix products, arithmetic and copies ran while one was open for 5% of the time, Pallas kernels for 2%

commit v1 on v0

v1 whole, which is shorter than its diff:
```python
import jax
import jax.numpy as jnp
from jax import lax
from jax.sharding import PartitionSpec as P

DH = 128
M = 256
EPS = 1e-06
HIGHEST = lax.Precision.HIGHEST
F32 = jnp.float32
BF16 = jnp.bfloat16
SCALE = DH ** (-0.5)


def exact(a, b, dims=(((1,), (0,)), ((), ()))):
    return lax.dot_general(a, b, dims, precision=HIGHEST, preferred_element_type=F32)


def exchange(parts, axis):
    return lax.all_to_all(parts, axis, 0, 0)


def spread(mine, axis):
    count = lax.axis_size(axis)
    return exchange(jnp.broadcast_to(mine[None], (count,) + mine.shape), axis)


def high_low(x):
    high = x.astype(BF16).astype(F32)
    return high, x - high


def landmark_means(tokens_block, seg_len):
    summed = jnp.sum(
        tokens_block.reshape(-1, seg_len, tokens_block.shape[1]).astype(F32), axis=1
    )
    return (summed / seg_len).astype(BF16)


def cubic(x, p):
    two = 7.0 * x - exact(x, p)
    four = 15.0 * x - exact(two, p)
    return 13.0 * x - exact(four, p), (x, two, four)


def cubic_back(grad, saved, p):
    x, two, four = saved
    d_five = -grad
    d_four = exact(d_five, p)
    d_three = -d_four
    d_two = exact(d_three, p)
    d_one = -d_two
    d_x = 13.0 * grad + 15.0 * d_four + 7.0 * d_two + exact(d_one, p)
    d_p = exact(
        jnp.concatenate([four, two, x], 0),
        jnp.concatenate([d_five, d_three, d_one], 0),
        (((0,), (0,)), ((), ())),
    )
    return d_x, d_p


def inverse_setup(lq, lk):
    ktwo = jax.nn.softmax(
        lax.dot_general(lq, lk, (((1,), (1,)), ((), ())), preferred_element_type=F32) * SCALE,
        axis=-1,
    )
    factor = 1.0 / jnp.max(jnp.sum(ktwo, axis=0))
    p0 = factor * exact(ktwo, ktwo, (((1,), (1,)), ((), ())))
    eye = jnp.eye(M, dtype=F32)
    h1 = 7.0 * eye - p0
    h2 = 15.0 * eye - exact(p0, h1)
    h3 = 13.0 * eye - exact(p0, h2)
    p1 = 0.25 * exact(p0, h3)
    return ktwo, factor, p0, p1, (h1, h2, h3)


def on_device(queries, keys_in, values, norm_gain, out_grad):
    tok, width_dev = queries.shape
    heads = width_dev // DH
    n_ctx = lax.axis_size("ctx")
    per_head = n_ctx // heads
    cols = DH // per_head
    land_dev = M // n_ctx
    seg_len = tok // land_dev
    feature_total = width_dev * lax.axis_size("head")
    my_head = lax.axis_index("ctx") // per_head

    q3 = queries.reshape(tok, heads, DH)
    k3 = keys_in.reshape(tok, heads, DH)
    v3 = values.reshape(tok, heads, DH)

    own = jnp.concatenate(
        [landmark_means(queries, seg_len), landmark_means(keys_in, seg_len)], axis=1
    )
    land = spread(own, "ctx").reshape(M, 2 * width_dev)
    lq = land[:, :width_dev].reshape(M, heads, DH)
    lk = land[:, width_dev:].reshape(M, heads, DH)

    score_three = jnp.einsum("thd,lhd->htl", k3, lq, preferred_element_type=F32) * SCALE
    shift = jnp.max(score_three, axis=1).astype(BF16).astype(F32)
    exp_local = jnp.exp(score_three - shift[:, None])
    tot_high, tot_low = high_low(jnp.sum(exp_local, axis=1))
    weighted = jnp.einsum(
        "thd,htl->hdl", v3, exp_local.astype(BF16), preferred_element_type=F32
    )
    stats = jnp.stack([shift, tot_high, tot_low], axis=1)
    stats = jnp.pad(stats, ((0, 0), (0, 5), (0, 0)))
    stats = jnp.broadcast_to(stats[:, None], (heads, per_head, 8, M))
    parts = jnp.concatenate([weighted.reshape(heads, per_head, cols, M), stats], axis=2)
    got = exchange(parts.reshape(n_ctx, cols + 8, M).astype(BF16), "ctx").astype(F32)

    my_lq = lax.dynamic_slice_in_dim(land, my_head * DH, DH, 1)
    my_lk = lax.dynamic_slice_in_dim(land, width_dev + my_head * DH, DH, 1)
    ktwo, factor, p0, p1, hs = inverse_setup(my_lq, my_lk)

    shifts = got[:, cols]
    top = jnp.max(shifts, axis=0)
    fade = jnp.exp(shifts - top)
    totals = jnp.sum(fade * (got[:, cols + 1] + got[:, cols + 2]), axis=0)
    context = jnp.sum(fade[:, None] * got[:, :cols], axis=0) / totals

    inner, saved_inner = cubic(context, p1)
    outer, saved_outer = cubic(inner, p0)
    my_mixing = (factor / 16.0) * exact(outer, ktwo)
    mixing = spread(my_mixing.astype(BF16), "ctx").reshape(heads, DH, M)

    kernel_one = jax.nn.softmax(
        jnp.einsum("thd,lhd->htl", q3, lk, preferred_element_type=F32) * SCALE, axis=-1
    )
    kernel_one_b = kernel_one.astype(BF16)
    output = jnp.einsum(
        "htl,hdl->thd", kernel_one_b, mixing, preferred_element_type=F32
    ).reshape(tok, width_dev)
    grad_float = out_grad.astype(F32)
    scaled_grad = grad_float * norm_gain
    sums = jnp.stack(
        [jnp.sum(output * output, axis=-1), jnp.sum(scaled_grad * output, axis=-1)]
    )
    sums = jnp.sum(spread(sums, "head"), axis=0)
    root_inv = lax.rsqrt(sums[0] / feature_total + EPS)[:, None]
    slope_dot = sums[1][:, None] * root_inv / feature_total
    normed = (output * root_inv * norm_gain).astype(BF16)
    d_output = (root_inv * (scaled_grad - output * (root_inv * slope_dot))).astype(BF16)
    local_gain = jnp.sum(grad_float * output * root_inv, axis=0)
    d3 = d_output.reshape(tok, heads, DH)

    local_mixing = jnp.einsum("thd,htl->hdl", d3, kernel_one_b, preferred_element_type=F32)
    gain_row = jnp.concatenate(high_low(local_gain.reshape(heads, 1, DH)), axis=2)
    gain_row = jnp.pad(gain_row, ((0, 0), (0, 7), (0, 0)))
    gain_row = jnp.broadcast_to(gain_row[:, None], (heads, per_head, 8, M))
    parts = jnp.concatenate(
        [local_mixing.reshape(heads, per_head, cols, M), gain_row], axis=2
    )
    got = exchange(parts.reshape(n_ctx, cols + 8, M).astype(BF16), "ctx").astype(F32)
    got = jnp.sum(got, axis=0)
    g_mixing = got[:cols]
    gain_high, gain_low = high_low(got[cols : cols + 1, :DH] + got[cols : cols + 1, DH:])

    g_kernel = jnp.einsum("thd,hdl->htl", d3, mixing, preferred_element_type=F32)
    g_sone = (
        kernel_one * (g_kernel - jnp.sum(kernel_one * g_kernel, axis=-1, keepdims=True))
    ).astype(BF16)
    query_one = jnp.einsum("htl,lhd->thd", g_sone, lk, preferred_element_type=F32) * SCALE
    keyland = jnp.einsum("htl,thd->hld", g_sone, q3, preferred_element_type=F32) * SCALE

    d_outer = (factor / 16.0) * exact(g_mixing, ktwo, (((1,), (1,)), ((), ())))
    d_inner, d_p0 = cubic_back(d_outer, saved_outer, p0)
    g_context, d_p1 = cubic_back(d_inner, saved_inner, p1)
    g_weighted = g_context / totals
    gt_high, gt_low = high_low(-jnp.sum(g_context * context, axis=0, keepdims=True) / totals)
    mine = jnp.concatenate(
        [
            g_weighted,
            gt_high,
            gt_low,
            jnp.concatenate([gain_high, gain_low], axis=1),
            top[None],
            jnp.zeros((4, M), F32),
        ],
        axis=0,
    )
    got = spread(mine.astype(BF16), "ctx").reshape(heads, per_head, cols + 8, M)
    g_weighted_b = got[:, :, :cols].reshape(heads, DH, M)
    rows = got[:, :, cols:].astype(F32)
    g_totals = jnp.sum(rows[:, :, 0] + rows[:, :, 1], axis=1)
    gain_grad = (rows[:, 0, 2, :DH] + rows[:, 0, 2, DH:]).reshape(width_dev)
    tops = rows[:, 0, 3]

    h1, h2, h3 = hs
    d_h3 = 0.25 * exact(p0, d_p1)
    d_h2 = -exact(p0, d_h3)
    d_h1 = -exact(p0, d_h2)
    d_p0 = d_p0 + 0.25 * exact(d_p1, h3) - exact(d_h3, h2) - exact(d_h2, h1) - d_h1
    d_ktwo = (factor / 16.0) * exact(
        outer, g_mixing, (((0,), (0,)), ((), ()))
    ) + factor * exact(d_p0 + d_p0.T, ktwo)
    g_stwo = ktwo * (d_ktwo - jnp.sum(ktwo * d_ktwo, axis=-1, keepdims=True))
    queryland_two = exact(g_stwo, my_lk.astype(F32)) * SCALE
    keyland_two = exact(g_stwo, my_lq.astype(F32), (((0,), (0,)), ((), ()))) * SCALE

    exp_three = jnp.exp(score_three - tops[:, None])
    g_exp = (
        jnp.einsum("thd,hdl->htl", v3, g_weighted_b, preferred_element_type=F32)
        + g_totals[:, None]
    )
    g_sthree = (exp_three * g_exp).astype(BF16)
    value_grad = (
        jnp.einsum(
            "htl,hdl->thd", exp_three.astype(BF16), g_weighted_b, preferred_element_type=F32
        )
        .astype(BF16)
        .reshape(tok, width_dev)
    )
    queryland = jnp.einsum("htl,thd->hld", g_sthree, k3, preferred_element_type=F32) * SCALE
    key_three = jnp.einsum("htl,lhd->thd", g_sthree, lq, preferred_element_type=F32) * SCALE

    mine_here = (jnp.arange(heads) == my_head)[:, None, None]
    queryland = queryland + jnp.where(mine_here, queryland_two[None], 0.0)
    keyland = keyland + jnp.where(mine_here, keyland_two[None], 0.0)
    both = jnp.concatenate([queryland, keyland], axis=0).astype(BF16)
    both = jnp.transpose(both, (1, 0, 2)).reshape(n_ctx, land_dev, 2 * width_dev)
    landed = jnp.sum(exchange(both, "ctx").astype(F32), axis=0) / seg_len

    def finish(per_token, per_land):
        total = per_token.reshape(land_dev, seg_len, width_dev) + per_land[:, None]
        return total.reshape(tok, width_dev).astype(BF16)

    query_grad = finish(query_one, landed[:, :width_dev])
    key_grad = finish(key_three, landed[:, width_dev:])
    return (normed, query_grad, key_grad, value_grad, gain_grad)


def solution(mesh):
    return jax.shard_map(
        on_device,
        mesh=mesh,
        in_specs=(
            P("ctx", "head"),
            P("ctx", "head"),
            P("ctx", "head"),
            P("head"),
            P("ctx", "head"),
        ),
        out_specs=(
            P("ctx", "head"),
            P("ctx", "head"),
            P("ctx", "head"),
            P("ctx", "head"),
            P("head"),
        ),
        check_vma=False,
    )
```

time: 556 us -> 150 us (0.27)
  blocking collectives: 276 us -> 0 us
  waiting for transfers between devices: 147 us -> 56.4 us
  matrix products: 76.4 us -> 24.1 us
  starting transfers between devices: 0.12 us -> 38.2 us
  between operations: 14.6 us -> 2.19 us
  Pallas kernels: 9.49 us -> 0 us
    psum x4 -> x0, blocking collectives: 162 us -> none  [the longest x1 72.9 us: on_device(): grad_mixing, gain_grad = lax.psum((local_mixing, local_gain), 'ctx')]
    psum x3 -> x0, waiting for transfers between devices: 147 us -> none  [the longest x1 110 us: on_device(): lax.psum(queryland_three.astype(jnp.bfloat16), 'ctx').astype(jnp.float32)]
    pmax x1 -> x0, blocking collectives: 62.2 us -> none  [on_device(): row_top = lax.pmax(jnp.max(score_three, axis=-1), 'ctx')]
    all_to_all x0 -> x7, waiting for transfers between devices: none -> 56.4 us  [exchange(): return lax.all_to_all(parts, axis, 0, 0)]
    all_gather x2 -> x0, blocking collectives: 51.4 us -> none  [the longest x1 26.4 us: on_device(): lax.all_gather(own_q, 'ctx', axis=0, tiled=True)]
    dot_general x39 -> x42, matrix products: 73.8 us -> 22.6 us  [the longest x30 11.2 us: exact(): lax.dot_general(a, b, dims, precision=HIGHEST, preferred_element_type=F32)]
    all_to_all x0 -> x7, starting transfers between devices: none -> 38.2 us  [exchange(): return lax.all_to_all(parts, axis, 0, 0)]
    unnamed x2 -> x0, Pallas kernels: 9.49 us -> none
  transfers between devices with their start and end apart: 3 -> 7, of which waited for: 2 -> 7; matrix products, arithmetic and copies ran while one was open for 5% -> 7% of each run, Pallas kernels for 2% -> 0%
where the time goes in v1:
time: 150 us; the launch traced here: 149 us
  waiting for transfers between devices  56.4 us (38%)
  starting transfers between devices  38.2 us (25%)
  matrix products  24.1 us (16%)
  local copies, waits for them, and re-layouts  16.2 us (11%)
  other arithmetic  12 us (8%)
  between operations  2.19 us (1%)
    all_to_all x7, waiting for transfers between devices, exchange(): return lax.all_to_all(parts, axis, 0, 0)  56.4 us
    all_to_all x7, starting transfers between devices, exchange(): return lax.all_to_all(parts, axis, 0, 0)  38.2 us
    dot_general x30, matrix products, exact(): lax.dot_general(a, b, dims, precision=HIGHEST, preferred_element_type=F32)  11.2 us
    unnamed x54, local copies, waits for them, and re-layouts  5.75 us
    dot_general x1, matrix products, on_device(): jnp.einsum('htl,hdl->thd', kernel_one_b, mixing, preferred_element_type=F32)  3.74 us
    broadcast_in_dim x4, local copies, waits for them, and re-layouts, spread(): return exchange(jnp.broadcast_to(mine[None], (count,) + mine.shape), axis)  3.01 us
  transfers between devices with their start and end apart: 7, of which 7 were waited for; matrix products, arithmetic and copies ran while one was open for 7% of the time, Pallas kernels for 0%

profile of v1, /device:TPU:1, one launch (start us, length us, event | category | flops | bytes accessed | tf_op | source)
XLA Modules:
  0.0 149.1 jit_solution(13217614532600093207)
XLA Ops:
  0.7 1.1 convert_reduce_fusion.2
  1.8 0.8 broadcast_in_dim.36
  2.7 8.6 %all-to-all-start = ((bf16[32,8,1024]{2,1,0:T(8,128)(2,1)}), bf16[32,8,1024]{2,1,0:T(8,128)(2,1)S(1)}, u32[]{:S(2)}, u32[]{:S(2)}) async-start(bf16[32,8,1024]{2,1,0:T(8,128)(2,1)} %broadcast_in_dim.36), calls=%async_computation | async-start | bytes 1048576 | tf_op jit(solution)/shard_map/all_to_all | solution.py:20
  11.3 11.6 %all-to-all-done = bf16[32,8,1024]{2,1,0:T(8,128)(2,1)S(1)} async-done(((bf16[32,8,1024]{2,1,0:T(8,128)(2,1)}), bf16[32,8,1024]{2,1,0:T(8,128)(2,1)S(1)}, u32[]{:S(2)}, u32[]{:S(2)}) %all-to-all-start) | async-done | bytes 524320 | tf_op jit(solution)/shard_map/all_to_all | solution.py:20
  23.1 0.8 copy-done.12
  27.2 0.8 copy.151
  29.2 3.7 %all-to-all-start.1 = ((bf16[32,24,256]{2,1,0:T(8,128)(2,1)}), bf16[32,24,256]{2,1,0:T(8,128)(2,1)S(1)}, u32[]{:S(2)}, u32[]{:S(2)}) async-start(bf16[32,24,256]{2,1,0:T(8,128)(2,1)} %pad_maximum_fusion), calls=%async_computation.1 | async-start | bytes 786432 | tf_op jit(solution)/shard_map/all_to_all | solution.py:20
  33.9 9.3 %all-to-all-done.1 = bf16[32,24,256]{2,1,0:T(8,128)(2,1)S(1)} async-done(((bf16[32,24,256]{2,1,0:T(8,128)(2,1)}), bf16[32,24,256]{2,1,0:T(8,128)(2,1)S(1)}, u32[]{:S(2)}, u32[]{:S(2)}) %all-to-all-start.1) | async-done | bytes 393248 | tf_op jit(solution)/shard_map/all_to_all | solution.py:20
  45.4 0.8 broadcast_in_dim.38
  46.2 4.5 %all-to-all-start.2 = ((bf16[32,16,256]{2,1,0:T(8,128)(2,1)}), bf16[32,16,256]{2,1,0:T(8,128)(2,1)}, u32[]{:S(2)}, u32[]{:S(2)}) async-start(bf16[32,16,256]{2,1,0:T(8,128)(2,1)} %broadcast_in_dim.38), calls=%async_computation.2 | async-start | bytes 524288 | tf_op jit(solution)/shard_map/all_to_all | solution.py:20
  50.7 1.5 %fusion.139 = (f32[4,256]{1,0:T(4,128)S(1)}, f32[4,256,256]{2,1,0:T(8,128)}) fusion(bf16[256,4,128]{0,2,1:T(8,128)(2,1)S(1)} %bitcast.236, bf16[256,512]{1,0:T(8,128)(2,1)S(1)} %copy-done.15), kind=kOutput, calls=%fused_computation.213 | convolution fusion | flops 67895552 | bytes 1576960 | tf_op jit(solution)/shard_map/sub | solution.py:127
  52.2 7.3 %all-to-all-done.2 = bf16[32,16,256]{2,1,0:T(8,128)(2,1)} async-done(((bf16[32,16,256]{2,1,0:T(8,128)(2,1)}), bf16[32,16,256]{2,1,0:T(8,128)(2,1)}, u32[]{:S(2)}, u32[]{:S(2)}) %all-to-all-start.2) | async-done | bytes 262176 | tf_op jit(solution)/shard_map/all_to_all | solution.py:20
  59.5 3.7 %fusion.31 = (f32[256]{0:T(256)S(1)}, f32[4,128,256]{2,1,0:T(8,128)}) fusion(bf16[4,128,256]{2,1,0:T(8,128)(2,1)} %bitcast.12, f32[4,256]{1,0:T(4,128)S(1)} %get-tuple-element.49, bf16[256,4,128]{0,2,1:T(8,128)(2,1)S(1)} %bitcast.237, bf16[256,512]{1,0:T(8,128)(2,1)S(1)} %copy-done.15), kind=kOutput, calls=%fused_computation.79 | convolution fusion | flops 135529472 | bytes 1315840 | tf_op jit(solution)/shard_map/htl,hdl->thd/dot_general | solution.py:131
  63.3 1.2 copy.157
  64.5 1.1 fusion.21
  66.3 8.2 %all-to-all-start.3 = ((f32[8,2,256]{2,1,0:T(2,128)}), f32[8,2,256]{2,1,0:T(2,128)S(1)}, u32[]{:S(2)}, u32[]{:S(2)}) async-start(f32[8,2,256]{2,1,0:T(2,128)} %broadcast_in_dim.39), calls=%async_computation.3 | async-start | bytes 32768 | tf_op jit(solution)/shard_map/all_to_all | solution.py:20
  75.6 5.5 %all-to-all-done.3 = f32[8,2,256]{2,1,0:T(2,128)S(1)} async-done(((f32[8,2,256]{2,1,0:T(2,128)}), f32[8,2,256]{2,1,0:T(2,128)S(1)}, u32[]{:S(2)}, u32[]{:S(2)}) %all-to-all-start.3) | async-done | bytes 16416 | tf_op jit(solution)/shard_map/all_to_all | solution.py:20
  81.1 2.0 %fusion.25 = (f32[512]{0:T(512)S(1)}, bf16[256,512]{1,0:T(8,128)(2,1)}, bf16[256,512]{1,0:T(8,128)(2,1)}) fusion(f32[256,512]{1,0:T(8,128)S(1)} %copy.157, bf16[256,512]{1,0:T(8,128)(2,1)} %param.9, f32[256]{0:T(256)S(1)} %bitcast.254, f32[256]{0:T(256)S(1)} %multiply_multiply_fusion, f32[512]{0:T(512)S(1)} %copy-done.18), kind=kLoop, calls=%fused_computation.68 | loop fusion | flops 1572352 | bytes 1316864 | tf_op jit(solution)/shard_map/reduce_sum | solution.py:144
  83.2 1.8 %copy.196 = bf16[256,512]{0,1:T(8,128)(2,1)} copy(bf16[256,512]{1,0:T(8,128)(2,1)} %get-tuple-element.31) | data formatting | bytes 524288 | tf_op jit(solution)/shard_map/reshape | solution.py:145
  85.0 2.9 %convolution_convert_fusion.2 = bf16[4,128,256]{2,1,0:T(8,128)(2,1)S(1)} fusion(bf16[256,4,128]{0,2,1:T(8,128)(2,1)} %bitcast.246, f32[4,256]{1,0:T(4,128)S(1)} %copy-done.20, bf16[256,4,128]{0,2,1:T(8,128)(2,1)S(1)} %bitcast.238, bf16[256,512]{1,0:T(8,128)(2,1)} %param.5), kind=kOutput, calls=%fused_computation.21 | convolution fusion | flops 135398656 | bytes 1052672 | tf_op jit(solution)/shard_map/thd,htl->hdl/dot_general | solution.py:147
  88.0 0.8 pad_maximum_fusion.1
  88.8 5.9 %all-to-all-start.4 = ((bf16[32,24,256]{2,1,0:T(8,128)(2,1)}), bf16[32,24,256]{2,1,0:T(8,128)(2,1)}, u32[]{:S(2)}, u32[]{:S(2)}) async-start(bf16[32,24,256]{2,1,0:T(8,128)(2,1)} %pad_maximum_fusion.1), calls=%async_computation.4 | async-start | bytes 786432 | tf_op jit(solution)/shard_map/all_to_all | solution.py:20
  94.8 1.9 %multiply_reduce_fusion = (f32[4,256]{1,0:T(4,128)S(1)}, f32[4,256,256]{2,1,0:T(8,128)S(1)}) fusion(f32[4,256,256]{2,1,0:T(8,128)} %get-tuple-element.50, f32[4,256]{1,0:T(4,128)S(1)} %copy-done.20, bf16[256,4,128]{0,2,1:T(8,128)(2,1)S(1)} %bitcast.247, bf16[4,128,256]{2,1,0:T(8,128)(2,1)} %bitcast.12), kind=kOutput, calls=%fused_computation.54 | convolution fusion | flops 67894272 | bytes 2629632 | tf_op jit(solution)/shard_map/thd,hdl->htl/dot_general | solution.py:159
  98.4 1.0 copy.174
  99.4 5.8 %all-to-all-done.4 = bf16[32,24,256]{2,1,0:T(8,128)(2,1)} async-done(((bf16[32,24,256]{2,1,0:T(8,128)(2,1)}), bf16[32,24,256]{2,1,0:T(8,128)(2,1)}, u32[]{:S(2)}, u32[]{:S(2)}) %all-to-all-start.4) | async-done | bytes 393248 | tf_op jit(solution)/shard_map/all_to_all | solution.py:20
  105.2 1.1 convert_reduce_fusion.1
  115.6 3.7 %all-to-all-start.5 = ((bf16[32,24,256]{2,1,0:T(8,128)(2,1)}), bf16[32,24,256]{2,1,0:T(8,128)(2,1)S(1)}, u32[]{:S(2)}, u32[]{:S(2)}) async-start(bf16[32,24,256]{2,1,0:T(8,128)(2,1)} %broadcast_in_dim.42), calls=%async_computation.5 | async-start | bytes 786432 | tf_op jit(solution)/shard_map/all_to_all | solution.py:20
  121.5 7.9 %all-to-all-done.5 = bf16[32,24,256]{2,1,0:T(8,128)(2,1)S(1)} async-done(((bf16[32,24,256]{2,1,0:T(8,128)(2,1)}), bf16[32,24,256]{2,1,0:T(8,128)(2,1)S(1)}, u32[]{:S(2)}, u32[]{:S(2)}) %all-to-all-start.5) | async-done | bytes 393248 | tf_op jit(solution)/shard_map/all_to_all | solution.py:20
  131.3 1.0 reshape.304
  132.3 3.7 %all-to-all-start.6 = ((bf16[32,8,1024]{2,1,0:T(8,128)(2,1)}), bf16[32,8,1024]{2,1,0:T(8,128)(2,1)S(1)}, u32[]{:S(2)}, u32[]{:S(2)}) async-start(bf16[32,8,1024]{2,1,0:T(8,128)(2,1)} %reshape.304), calls=%async_computation.6 | async-start | bytes 1048576 | tf_op jit(solution)/shard_map/all_to_all | solution.py:20
  136.3 0.8 copy.176
  138.4 9.1 %all-to-all-done.6 = bf16[32,8,1024]{2,1,0:T(8,128)(2,1)S(1)} async-done(((bf16[32,8,1024]{2,1,0:T(8,128)(2,1)}), bf16[32,8,1024]{2,1,0:T(8,128)(2,1)S(1)}, u32[]{:S(2)}, u32[]{:S(2)}) %all-to-all-start.6) | async-done | bytes 524320 | tf_op jit(solution)/shard_map/all_to_all | solution.py:20
  (149 shorter events, 27.0 us)
Async XLA Ops:
  0.6 27.4 %copy-start = (bf16[256,512]{1,0:T(8,128)(2,1)S(1)}, bf16[256,512]{1,0:T(8,128)(2,1)}, u32[]{:S(2)}) copy-start(bf16[256,512]{1,0:T(8,128)(2,1)} %param.7) | copy-start | bytes 786436
  0.6 1.1 copy-start.14
  2.7 20.2 %all-to-all-start = ((bf16[32,8,1024]{2,1,0:T(8,128)(2,1)}), bf16[32,8,1024]{2,1,0:T(8,128)(2,1)S(1)}, u32[]{:S(2)}, u32[]{:S(2)}) async-start(bf16[32,8,1024]{2,1,0:T(8,128)(2,1)} %broadcast_in_dim.36), calls=%async_computation | async-start | bytes 1048576 | tf_op jit(solution)/shard_map/all_to_all | solution.py:20
  22.9 1.0 copy-start.12
  23.1 1.1 copy-start.1
  24.6 20.5 %copy-start.3 = (f32[256,256]{0,1:T(8,128)}, f32[256,256]{0,1:T(8,128)S(1)}, u32[]{:S(2)}) copy-start(f32[256,256]{0,1:T(8,128)S(1)} %get-tuple-element.48) | copy-start | bytes 786436
  24.7 20.4 %copy-start.21 = (f32[256]{0:T(256)}, f32[256]{0:T(256)S(1)}, u32[]{:S(2)}) copy-start(f32[256]{0:T(256)S(1)} %fusion.44) | copy-start | bytes 3076
  29.2 13.9 %all-to-all-start.1 = ((bf16[32,24,256]{2,1,0:T(8,128)(2,1)}), bf16[32,24,256]{2,1,0:T(8,128)(2,1)S(1)}, u32[]{:S(2)}, u32[]{:S(2)}) async-start(bf16[32,24,256]{2,1,0:T(8,128)(2,1)} %pad_maximum_fusion), calls=%async_computation.1 | async-start | bytes 786432 | tf_op jit(solution)/shard_map/all_to_all | solution.py:20
  46.2 4.5 %copy-start.8 = (bf16[256,512]{0,1:T(8,128)(2,1)S(1)}, bf16[256,512]{0,1:T(8,128)(2,1)}, u32[]{:S(2)}) copy-start(bf16[256,512]{0,1:T(8,128)(2,1)} %copy.151) | copy-start | bytes 786436
  46.2 4.5 %copy-start.15 = (bf16[256,512]{1,0:T(8,128)(2,1)S(1)}, bf16[256,512]{1,0:T(8,128)(2,1)}, u32[]{:S(2)}) copy-start(bf16[256,512]{1,0:T(8,128)(2,1)} %param.5) | copy-start | bytes 786436
  46.2 13.3 %all-to-all-start.2 = ((bf16[32,16,256]{2,1,0:T(8,128)(2,1)}), bf16[32,16,256]{2,1,0:T(8,128)(2,1)}, u32[]{:S(2)}, u32[]{:S(2)}) async-start(bf16[32,16,256]{2,1,0:T(8,128)(2,1)} %broadcast_in_dim.38), calls=%async_computation.2 | async-start | bytes 524288 | tf_op jit(solution)/shard_map/all_to_all | solution.py:20
  52.2 11.0 %copy-start.19 = (f32[4,256]{1,0:T(4,128)}, f32[4,256]{1,0:T(4,128)S(1)}, u32[]{:S(2)}) copy-start(f32[4,256]{1,0:T(4,128)S(1)} %get-tuple-element.49) | copy-start | bytes 12292
  63.3 1.3 copy-start.18
  66.3 14.8 %all-to-all-start.3 = ((f32[8,2,256]{2,1,0:T(2,128)}), f32[8,2,256]{2,1,0:T(2,128)S(1)}, u32[]{:S(2)}, u32[]{:S(2)}) async-start(f32[8,2,256]{2,1,0:T(2,128)} %broadcast_in_dim.39), calls=%async_computation.3 | async-start | bytes 32768 | tf_op jit(solution)/shard_map/all_to_all | solution.py:20
  83.1 1.9 %copy-start.9 = (bf16[256,512]{0,1:T(8,128)(2,1)S(1)}, bf16[256,512]{0,1:T(8,128)(2,1)}, u32[]{:S(2)}) copy-start(bf16[256,512]{0,1:T(8,128)(2,1)} %copy.151) | copy-start | bytes 786436
  83.2 1.8 %copy-start.20 = (f32[4,256]{1,0:T(4,128)S(1)}, f32[4,256]{1,0:T(4,128)}, u32[]{:S(2)}) copy-start(f32[4,256]{1,0:T(4,128)} %copy-done.19) | copy-start | bytes 12292
  88.8 6.0 %copy-start.17 = (bf16[256,512]{0,1:T(8,128)(2,1)S(1)}, bf16[256,512]{0,1:T(8,128)(2,1)}, u32[]{:S(2)}) copy-start(bf16[256,512]{0,1:T(8,128)(2,1)} %copy.196) | copy-start | bytes 786436
  88.8 16.4 %all-to-all-start.4 = ((bf16[32,24,256]{2,1,0:T(8,128)(2,1)}), bf16[32,24,256]{2,1,0:T(8,128)(2,1)}, u32[]{:S(2)}, u32[]{:S(2)}) async-start(bf16[32,24,256]{2,1,0:T(8,128)(2,1)} %pad_maximum_fusion.1), calls=%async_computation.4 | async-start | bytes 786432 | tf_op jit(solution)/shard_map/all_to_all | solution.py:20
  94.8 1.9 %copy-start.11 = (f32[4,256,256]{2,1,0:T(8,128)S(1)}, f32[4,256,256]{2,1,0:T(8,128)}, u32[]{:S(2)}) copy-start(f32[4,256,256]{2,1,0:T(8,128)} %get-tuple-element.50) | copy-start | bytes 3145732
  96.6 1.0 copy-start.10
  97.6 0.8 copy-start.5
  99.4 7.4 %copy-start.4 = (f32[256,256]{0,1:T(8,128)S(1)}, f32[256,256]{0,1:T(8,128)}, u32[]{:S(2)}) copy-start(f32[256,256]{0,1:T(8,128)} %copy-done.3) | copy-start | bytes 786436
  106.3 0.7 copy-start.22
  114.1 0.7 copy-start.24
  115.6 13.8 %all-to-all-start.5 = ((bf16[32,24,256]{2,1,0:T(8,128)(2,1)}), bf16[32,24,256]{2,1,0:T(8,128)(2,1)S(1)}, u32[]{:S(2)}, u32[]{:S(2)}) async-start(bf16[32,24,256]{2,1,0:T(8,128)(2,1)} %broadcast_in_dim.42), calls=%async_computation.5 | async-start | bytes 786432 | tf_op jit(solution)/shard_map/all_to_all | solution.py:20
  120.0 1.0 copy-start.6
  120.0 1.1 copy-start.16
  120.1 1.1 copy-start.25
  129.6 1.0 copy-start.13
  132.3 15.2 %all-to-all-start.6 = ((bf16[32,8,1024]{2,1,0:T(8,128)(2,1)}), bf16[32,8,1024]{2,1,0:T(8,128)(2,1)S(1)}, u32[]{:S(2)}, u32[]{:S(2)}) async-start(bf16[32,8,1024]{2,1,0:T(8,128)(2,1)} %reshape.304), calls=%async_computation.6 | async-start | bytes 1048576 | tf_op jit(solution)/shard_map/all_to_all | solution.py:20
  136.3 1.0 copy-start.2
  137.8 9.8 %copy-start.7 = (f32[256,512]{1,0:T(8,128)S(1)}, f32[256,512]{1,0:T(8,128)}, u32[]{:S(2)}) copy-start(f32[256,512]{1,0:T(8,128)} %copy.174) | copy-start | bytes 1572868
  (1 other events, 0.7 us)

commit v2 on v1

v2 whole, which is shorter than its diff:
```python
import functools

import jax
import jax.numpy as jnp
from jax import lax
from jax.experimental import pallas as pl
from jax.experimental.pallas import tpu as pltpu
from jax.sharding import PartitionSpec as P

DH = 128
M = 256
EPS = 1e-06
F32 = jnp.float32
BF16 = jnp.bfloat16
SCALE = DH ** (-0.5)
VMEM_BYTES = 32 * 1024 * 1024

NN = (((1,), (0,)), ((), ()))
NT = (((1,), (1,)), ((), ()))
TN = (((0,), (0,)), ((), ()))


def dot(a, b, dims=NN):
    return lax.dot_general(a, b, dims, preferred_element_type=F32)


def exact(a, b, dims=NN):
    return lax.dot_general(
        a, b, dims, precision=lax.Precision.HIGHEST, preferred_element_type=F32
    )


def exchange(parts, axis):
    return lax.all_to_all(parts, axis, 0, 0)


def high_low(x):
    high = x.astype(BF16).astype(F32)
    return high, x - high


def rows_of(*rows):
    index = lax.broadcasted_iota(jnp.int32, (8, rows[0].shape[1]), 0)
    out = jnp.zeros((8, rows[0].shape[1]), F32)
    for place, row in enumerate(rows):
        out = jnp.where(index == place, row, out)
    return out


def eye_times(value):
    row = lax.broadcasted_iota(jnp.int32, (M, M), 0)
    col = lax.broadcasted_iota(jnp.int32, (M, M), 1)
    return jnp.where(row == col, value, 0.0).astype(F32)


def head_cols(h):
    return slice(h * DH, (h + 1) * DH)


def call(body, outs, *args, scalars=0, flops=0, name):
    nbytes = sum(a.size * a.dtype.itemsize for a in (*args, *outs))
    in_specs = [pl.BlockSpec(memory_space=pltpu.SMEM)] * scalars + [
        pl.BlockSpec(memory_space=pltpu.VMEM)
    ] * (len(args) - scalars)
    return pl.pallas_call(
        body,
        out_shape=outs,
        in_specs=in_specs,
        out_specs=[pl.BlockSpec(memory_space=pltpu.VMEM)] * len(outs),
        compiler_params=pltpu.CompilerParams(vmem_limit_bytes=VMEM_BYTES),
        cost_estimate=pl.CostEstimate(flops=flops, bytes_accessed=nbytes, transcendentals=0),
        name=name,
    )(*args)


def shape(*dims, dtype=F32):
    return jax.ShapeDtypeStruct(dims, dtype)


def means_body(q_ref, k_ref, out_ref):
    count, land_dev, both = out_ref.shape
    width = both // 2
    seg_len = q_ref.shape[0] // land_dev
    means = [
        jnp.sum(ref[...].astype(F32).reshape(land_dev, seg_len, width), axis=1) / seg_len
        for ref in (q_ref, k_ref)
    ]
    own = jnp.concatenate(means, axis=1).astype(BF16)
    for place in range(count):
        out_ref[place] = own


def context_body(land_ref, k_ref, v_ref, out_ref):
    count, rows, _ = out_ref.shape
    heads = k_ref.shape[1] // DH
    per_head = count // heads
    cols = DH // per_head
    for h in range(heads):
        score = dot(k_ref[:, head_cols(h)], land_ref[:, head_cols(h)], NT) * SCALE
        shift = jnp.max(score, axis=0, keepdims=True).astype(BF16).astype(F32)
        exp_local = jnp.exp(score - shift)
        high, low = high_low(jnp.sum(exp_local, axis=0, keepdims=True))
        weighted = dot(v_ref[:, head_cols(h)], exp_local.astype(BF16), TN)
        stats = rows_of(shift, high, low)
        for j in range(per_head):
            out_ref[h * per_head + j] = jnp.concatenate(
                [weighted[j * cols : (j + 1) * cols], stats], axis=0
            ).astype(BF16)


def inverse_body(head_ref, land_ref, out_ref, factor_ref):
    width = land_ref.shape[1] // 2
    at = pl.multiple_of(head_ref[0] * DH, DH)
    lq = land_ref[:, pl.ds(at, DH)]
    lk = land_ref[:, pl.ds(at + width, DH)]
    score = dot(lq, lk, NT) * SCALE
    top = jnp.exp(score - jnp.max(score, axis=1, keepdims=True))
    ktwo = top / jnp.sum(top, axis=1, keepdims=True)
    factor = 1.0 / jnp.max(jnp.sum(ktwo, axis=0, keepdims=True), axis=1, keepdims=True)
    x = factor * exact(ktwo, ktwo, NT)
    h2 = eye_times(15.0) - exact(x, eye_times(7.0) - x)
    h3 = eye_times(13.0) - exact(x, h2)
    p1 = 0.25 * exact(x, h3)
    b2 = eye_times(15.0) - exact(p1, eye_times(7.0) - p1)
    b3 = eye_times(13.0) - exact(p1, b2)
    out_ref[0] = (factor * 0.0625) * exact(b3, exact(h3, ktwo))
    out_ref[1] = ktwo
    out_ref[2] = x
    out_ref[3] = h2
    out_ref[4] = h3
    out_ref[5] = p1
    out_ref[6] = b2
    out_ref[7] = b3
    factor_ref[...] = jnp.broadcast_to(factor, (8, 128))


def mixing_body(got_ref, inv_ref, out_ref, ctx_ref, stat_ref):
    count, rows, _ = got_ref.shape
    cols = rows - 8
    top = got_ref[0].astype(F32)[cols:]
    for place in range(1, count):
        top = jnp.maximum(top, got_ref[place].astype(F32)[cols:])
    top = top[0:1]
    total = jnp.zeros((1, M), F32)
    weighted = jnp.zeros((cols, M), F32)
    for place in range(count):
        part = got_ref[place].astype(F32)
        fade = jnp.exp(part[cols : cols + 1] - top)
        total = total + fade * (part[cols + 1 : cols + 2] + part[cols + 2 : cols + 3])
        weighted = weighted + fade * part[:cols]
    context = weighted / total
    mixing = exact(context, inv_ref[0]).astype(BF16)
    for place in range(count):
        out_ref[place] = mixing
    ctx_ref[...] = context
    stat_ref[...] = rows_of(total, top)


def kernel_one_body(q_ref, land_ref, out_ref):
    heads = q_ref.shape[1] // DH
    for h in range(heads):
        score = dot(q_ref[:, head_cols(h)], land_ref[:, head_cols(heads + h)], NT) * SCALE
        top = jnp.exp(score - jnp.max(score, axis=1, keepdims=True))
        out_ref[h] = top / jnp.sum(top, axis=1, keepdims=True)


def output_body(kone_ref, mix_ref, og_ref, gain_ref, out_ref, sum_ref):
    heads = kone_ref.shape[0]
    tok = kone_ref.shape[1]
    squares = jnp.zeros((tok, DH), F32)
    slopes = jnp.zeros((tok, DH), F32)
    for h in range(heads):
        out = dot(kone_ref[h].astype(BF16), mix_ref[h], NT)
        out_ref[:, head_cols(h)] = out
        scaled = og_ref[:, head_cols(h)].astype(F32) * gain_ref[:, head_cols(h)]
        squares = squares + out * out
        slopes = slopes + scaled * out
    ones = jnp.ones((8, DH), F32)
    both = rows_of(exact(ones, squares, NT)[0:1], exact(ones, slopes, NT)[0:1])
    for place in range(sum_ref.shape[0]):
        sum_ref[place] = both[:2]


def norm_body(sum_ref, out_ref, og_ref, gain_ref, kone_ref, normed_ref, dout_ref, part_ref):
    heads, tok, _ = kone_ref.shape
    count, rows, _ = part_ref.shape
    per_head = count // heads
    cols = rows - 8
    features = heads * DH * sum_ref.shape[0]
    total = sum_ref[0]
    for place in range(1, sum_ref.shape[0]):
        total = total + sum_ref[place]
    root_inv = lax.rsqrt(total[0:1] / features + EPS)
    slope = total[1:2] * root_inv / features
    columns = jnp.transpose(rows_of(root_inv, root_inv * slope))
    root_inv = columns[:, 0:1]
    bent = columns[:, 1:2]
    for h in range(heads):
        gain = gain_ref[:, head_cols(h)]
        out = out_ref[:, head_cols(h)]
        grad = og_ref[:, head_cols(h)].astype(F32)
        straight = out * root_inv
        normed_ref[:, head_cols(h)] = (straight * gain).astype(BF16)
        d_out = (root_inv * (grad * gain - out * bent)).astype(BF16)
        dout_ref[:, head_cols(h)] = d_out
        g_mixing = dot(d_out, kone_ref[h].astype(BF16), TN)
        high, low = high_low(jnp.sum(grad * straight, axis=0, keepdims=True))
        gain_rows = rows_of(jnp.concatenate([high, low], axis=1))
        for j in range(per_head):
            part_ref[h * per_head + j] = jnp.concatenate(
                [g_mixing[j * cols : (j + 1) * cols], gain_rows], axis=0
            ).astype(BF16)


def query_body(dout_ref, mix_ref, kone_ref, q_ref, land_ref, query_ref, keyland_ref):
    heads = kone_ref.shape[0]
    for h in range(heads):
        g_kernel = dot(dout_ref[:, head_cols(h)], mix_ref[h])
        kone = kone_ref[h]
        inner = jnp.sum(kone * g_kernel, axis=1, keepdims=True)
        g_score = (kone * (g_kernel - inner)).astype(BF16)
        query_ref[:, head_cols(h)] = dot(g_score, land_ref[:, head_cols(heads + h)]) * SCALE
        keyland_ref[:, head_cols(h)] = dot(g_score, q_ref[:, head_cols(h)], TN) * SCALE


def grad_context_body(got_ref, inv_ref, ctx_ref, stat_ref, out_ref, g_ref):
    count, rows, _ = got_ref.shape
    cols = rows - 8
    got = got_ref[0].astype(F32)
    for place in range(1, count):
        got = got + got_ref[place].astype(F32)
    g_mixing = got[:cols]
    gain = got[cols : cols + 1]
    gain_high, gain_low = high_low(gain[:, :DH] + gain[:, DH:])
    total = stat_ref[0:1]
    g_context = exact(g_mixing, inv_ref[0], NT)
    high, low = high_low(-jnp.sum(g_context * ctx_ref[...], axis=0, keepdims=True) / total)
    tail = rows_of(high, low, jnp.concatenate([gain_high, gain_low], axis=1), stat_ref[1:2])
    mine = jnp.concatenate([g_context / total, tail], axis=0).astype(BF16)
    for place in range(count):
        out_ref[place] = mine
    g_ref[...] = g_mixing


def inverse_back_body(head_ref, inv_ref, factor_ref, ctx_ref, g_ref, land_ref, ql_ref, kl_ref):
    width = land_ref.shape[1] // 2
    at = pl.multiple_of(head_ref[0] * DH, DH)
    lq = land_ref[:, pl.ds(at, DH)].astype(F32)
    lk = land_ref[:, pl.ds(at + width, DH)].astype(F32)
    factor = factor_ref[0:1, 0:1]
    ktwo, x, h2, h3, p1, b2, b3 = [inv_ref[place] for place in range(1, 8)]
    context = ctx_ref[...]
    g_mixing = g_ref[...]
    inner = exact(context, b3)
    outer = exact(inner, h3)
    d_outer = (factor * 0.0625) * exact(g_mixing, ktwo, NT)
    d_inner = exact(d_outer, h3)
    d_b3 = exact(context, d_inner, TN)
    d_b2 = -exact(p1, d_b3)
    d_b1 = -exact(p1, d_b2)
    d_p1 = -exact(d_b3, b2) - exact(d_b2, eye_times(7.0) - p1) - d_b1
    d_h3 = exact(inner, d_outer, TN) + 0.25 * exact(x, d_p1)
    d_h2 = -exact(x, d_h3)
    d_h1 = -exact(x, d_h2)
    d_x = 0.25 * exact(d_p1, h3) - exact(d_h3, h2) - exact(d_h2, eye_times(7.0) - x) - d_h1
    d_ktwo = (factor * 0.0625) * exact(outer, g_mixing, TN) + factor * exact(
        d_x + jnp.transpose(d_x), ktwo
    )
    g_score = ktwo * (d_ktwo - jnp.sum(ktwo * d_ktwo, axis=1, keepdims=True))
    ql_ref[...] = exact(g_score, lk) * SCALE
    kl_ref[...] = exact(g_score, lq, TN) * SCALE


def three_back(got_ref, land_ref, k_ref, v_ref, h):
    count, rows, _ = got_ref.shape
    cols = rows - 8
    per_head = DH // cols
    parts = [got_ref[h * per_head + j] for j in range(per_head)]
    g_weighted = jnp.concatenate([part[:cols] for part in parts], axis=0)
    tails = [part.astype(F32)[cols:] for part in parts]
    summed = functools.reduce(jnp.add, tails)
    g_totals = summed[0:1] + summed[1:2]
    top = tails[0][3:4]
    score = dot(k_ref[:, head_cols(h)], land_ref[:, head_cols(h)], NT) * SCALE
    exp_three = jnp.exp(score - top)
    g_exp = dot(v_ref[:, head_cols(h)], g_weighted) + g_totals
    return g_weighted, exp_three, (exp_three * g_exp).astype(BF16)


def queryland_body(
    head_ref, got_ref, land_ref, k_ref, v_ref, keyland_ref, ql_ref, kl_ref, out_ref
):
    heads = k_ref.shape[1] // DH
    for h in range(heads):
        g_score = three_back(got_ref, land_ref, k_ref, v_ref, h)[2]
        queryland = dot(g_score, k_ref[:, head_cols(h)], TN) * SCALE
        mine = (head_ref[0] == h).astype(F32)
        out_ref[:, head_cols(h)] = (queryland + mine * ql_ref[...]).astype(BF16)
        out_ref[:, head_cols(heads + h)] = (
            keyland_ref[:, head_cols(h)] + mine * kl_ref[...]
        ).astype(BF16)


def value_body(got_ref, land_ref, k_ref, v_ref, value_ref, key_ref, gain_ref):
    count, rows, _ = got_ref.shape
    cols = rows - 8
    heads = k_ref.shape[1] // DH
    per_head = count // heads
    for h in range(heads):
        g_weighted, exp_three, g_score = three_back(got_ref, land_ref, k_ref, v_ref, h)
        value_ref[:, head_cols(h)] = dot(exp_three.astype(BF16), g_weighted, NT).astype(BF16)
        key_ref[:, head_cols(h)] = dot(g_score, land_ref[:, head_cols(h)]) * SCALE
        gain = got_ref[h * per_head].astype(F32)[cols + 2 : cols + 3]
        gain_ref[:, head_cols(h)] = gain[:, :DH] + gain[:, DH:]


def finish_body(got_ref, query_ref, key_ref, query_out, key_out):
    count, land_dev, both = got_ref.shape
    tok, width = query_ref.shape
    seg_len = tok // land_dev
    got = got_ref[0].astype(F32)
    for place in range(1, count):
        got = got + got_ref[place].astype(F32)
    got = got / seg_len
    for ref, out, land in (
        (query_ref, query_out, got[:, :width]),
        (key_ref, key_out, got[:, width:]),
    ):
        for row in range(land_dev):
            span = slice(row * seg_len, (row + 1) * seg_len)
            out[span] = (ref[span] + land[row : row + 1]).astype(BF16)


def on_device(queries, keys_in, values, norm_gain, out_grad):
    tok, width = queries.shape
    heads = width // DH
    n_ctx = lax.axis_size("ctx")
    n_head = lax.axis_size("head")
    per_head = n_ctx // heads
    cols = DH // per_head
    land_dev = M // n_ctx
    my_head = (lax.axis_index("ctx") // per_head).astype(jnp.int32).reshape(1)
    gain = norm_gain.reshape(1, width)
    packed = shape(n_ctx, cols + 8, M, dtype=BF16)
    wide = shape(tok, width)
    wide_b = shape(tok, width, dtype=BF16)

    (own,) = call(
        means_body, [shape(n_ctx, land_dev, 2 * width, dtype=BF16)], queries, keys_in,
        flops=10**6, name="landmark_means",
    )
    land = exchange(own, "ctx").reshape(M, 2 * width)

    (parts,) = call(
        context_body, [packed], land, keys_in, values, flops=10**8, name="local_context"
    )
    got = exchange(parts, "ctx")
    inverse, factor = call(
        inverse_body, [shape(8, M, M), shape(8, 128)], my_head, land,
        scalars=1, flops=3 * 10**9, name="inverse",
    )
    (kernel_one,) = call(
        kernel_one_body, [shape(heads, tok, M)], queries, land, flops=10**9, name="kernel_one"
    )
    parts, context, stats = call(
        mixing_body, [shape(n_ctx, cols, M, dtype=BF16), shape(cols, M), shape(8, M)],
        got, inverse, flops=10**8, name="mixing",
    )
    mixing = exchange(parts, "ctx").reshape(heads, DH, M)

    output, sums = call(
        output_body, [wide, shape(n_head, 2, tok)], kernel_one, mixing, out_grad, gain,
        flops=10**8, name="output",
    )
    sums = exchange(sums, "head")
    normed, d_output, parts = call(
        norm_body, [wide_b, wide_b, packed], sums, output, out_grad, gain, kernel_one,
        flops=10**8, name="norm",
    )
    got = exchange(parts, "ctx")
    query_one, keyland = call(
        query_body, [wide, shape(M, width)], d_output, mixing, kernel_one, queries, land,
        flops=2 * 10**9, name="kernel_one_back",
    )
    parts, g_mixing = call(
        grad_context_body, [packed, shape(cols, M)], got, inverse, context, stats,
        flops=10**8, name="context_back",
    )
    got = exchange(parts, "ctx")
    ql_two, kl_two = call(
        inverse_back_body, [shape(M, DH), shape(M, DH)],
        my_head, inverse, factor, context, g_mixing, land,
        scalars=1, flops=5 * 10**9, name="inverse_back",
    )
    (both,) = call(
        queryland_body, [shape(M, 2 * width, dtype=BF16)],
        my_head, got, land, keys_in, values, keyland, ql_two, kl_two,
        scalars=1, flops=10**8, name="landmarks_back",
    )
    landed = exchange(both.reshape(n_ctx, land_dev, 2 * width), "ctx")
    value_grad, key_three, gain_grad = call(
        value_body, [wide_b, wide, shape(1, width)], got, land, keys_in, values,
        flops=2 * 10**9, name="kernel_three_back",
    )
    query_grad, key_grad = call(
        finish_body, [wide_b, wide_b], landed, query_one, key_three, flops=10**6, name="finish"
    )
    return (normed, query_grad, key_grad, value_grad, gain_grad.reshape(width))


def solution(mesh):
    return jax.shard_map(
        on_device,
        mesh=mesh,
        in_specs=(
            P("ctx", "head"),
            P("ctx", "head"),
            P("ctx", "head"),
            P("head"),
            P("ctx", "head"),
        ),
        out_specs=(
            P("ctx", "head"),
            P("ctx", "head"),
            P("ctx", "head"),
            P("ctx", "head"),
            P("head"),
        ),
        check_vma=False,
    )
```

time: 150 us -> 129 us (0.86)
  blocking collectives: 0 us -> 34.6 us
  waiting for transfers between devices: 56.4 us -> 27.2 us
  matrix products: 24.1 us -> 0 us
  Pallas kernels: 0 us -> 21.7 us
  starting transfers between devices: 38.2 us -> 22.5 us
  other arithmetic: 12 us -> 0 us
  local copies, waits for them, and re-layouts: 16.2 us -> 20.7 us
    all_to_all x0 -> x2, blocking collectives: none -> 34.6 us  [exchange(): return lax.all_to_all(parts, axis, 0, 0)]
    all_to_all x7 -> x5, waiting for transfers between devices: 56.4 us -> 27.2 us  [exchange(): return lax.all_to_all(parts, axis, 0, 0)]
    dot_general x42 -> x0, matrix products: 22.6 us -> none  [the longest x30 11.2 us: exact(): lax.dot_general(a, b, dims, precision=HIGHEST, preferred_element_type=F32)]
    pallas_call x0 -> x13, Pallas kernels: none -> 21.7 us  [call(): pl.pallas_call(body, out_shape=outs, in_specs=in_specs, out_specs=[pl.Blo...]
    all_to_all x7 -> x5, starting transfers between devices: 38.2 us -> 22.5 us  [exchange(): return lax.all_to_all(parts, axis, 0, 0)]
    unnamed x54 -> x60, local copies, waits for them, and re-layouts: 5.75 us -> 20.7 us
    reduce_sum x13 -> x0, other arithmetic: 5.95 us -> none  [the longest x1 2.02 us: on_device(): local_gain = jnp.sum(grad_float * output * root_inv, axis=0)]
    reshape x5 -> x0, local copies, waits for them, and re-layouts: 5.3 us -> none  [the longest x1 1.83 us: on_device(): d3 = d_output.reshape(tok, heads, DH)]
  transfers between devices with their start and end apart: 7 -> 5, of which waited for: 7 -> 5; matrix products, arithmetic and copies ran while one was open for 7% -> 0% of each run, Pallas kernels for 0% -> 11%
where the time goes in v2:
time: 129 us; the launch traced here: 128 us
  blocking collectives  34.6 us (27%)
  waiting for transfers between devices  27.2 us (21%)
  starting transfers between devices  22.5 us (17%)
  Pallas kernels  21.7 us (17%)
  local copies, waits for them, and re-layouts  20.7 us (16%)
    all_to_all x2, blocking collectives, exchange(): return lax.all_to_all(parts, axis, 0, 0)  34.6 us
    all_to_all x5, waiting for transfers between devices, exchange(): return lax.all_to_all(parts, axis, 0, 0)  27.2 us
    all_to_all x5, starting transfers between devices, exchange(): return lax.all_to_all(parts, axis, 0, 0)  22.5 us
    pallas_call x13, Pallas kernels, call(): pl.pallas_call(body, out_shape=outs, in_specs=in_specs, out_specs=[pl.Blo...  21.7 us
    unnamed x60, local copies, waits for them, and re-layouts  20.7 us
  transfers between devices with their start and end apart: 5, of which 5 were waited for; matrix products, arithmetic and copies ran while one was open for 0% of the time, Pallas kernels for 11%

profile of v2, /device:TPU:1, one launch (start us, length us, event | category | flops | bytes accessed | tf_op | source)
XLA Modules:
  0.0 127.6 jit_solution(9283828764932254810)
XLA Ops:
  0.6 0.9 copy-done.3
  1.6 0.9 copy-done.14
  2.7 20.0 %all_to_all.35 = bf16[32,8,1024]{2,1,0:T(8,128)(2,1)S(1)} all-to-all(bf16[32,8,1024]{2,1,0:T(8,128)(2,1)S(1)} %landmark_means.1), channel_id=1, replica_groups=mesh['ctx'=32,'head'=8] {'ctx'}, dimensions={0} | all-to-all | bytes 1048576 | tf_op jit(solution)/shard_map/all_to_all | solution.py:34
  22.7 2.1 %local_context.1 = bf16[32,24,256]{2,1,0:T(8,128)(2,1)} custom-call(bf16[256,1024]{1,0:T(8,128)(2,1)S(1)} %bitcast.6, bf16[256,512]{1,0:T(8,128)(2,1)S(1)} %copy-done.3, bf16[256,512]{1,0:T(8,128)(2,1)S(1)} %copy-done.5), custom_call_target="tpu_custom_call" | custom-call | flops 100000000 | bytes 1441792 | tf_op jit(solution)/shard_map/local_context/pallas_call | solution.py:65
  24.8 3.7 %all-to-all-start.1 = ((bf16[32,24,256]{2,1,0:T(8,128)(2,1)}), bf16[32,24,256]{2,1,0:T(8,128)(2,1)S(1)}, u32[]{:S(2)}, u32[]{:S(2)}) async-start(bf16[32,24,256]{2,1,0:T(8,128)(2,1)} %local_context.1), calls=%async_computation.1 | async-start | bytes 786432 | tf_op jit(solution)/shard_map/all_to_all | solution.py:34
  28.5 4.0 %inverse.1 = (f32[8,256,256]{2,1,0:T(8,128)S(1)}, f32[8,128]{1,0:T(8,128)S(1)}) custom-call(s32[1]{0:T(128)} %bitcast.1.head_ref, bf16[256,1024]{1,0:T(8,128)(2,1)S(1)} %bitcast.7), custom_call_target="tpu_custom_call" | custom-call | flops 3000000000 | bytes 2625540 | tf_op jit(solution)/shard_map/inverse/pallas_call | solution.py:65
  33.1 5.6 %all-to-all-done.1.got_ref = bf16[32,24,256]{2,1,0:T(8,128)(2,1)S(1)} async-done(((bf16[32,24,256]{2,1,0:T(8,128)(2,1)}), bf16[32,24,256]{2,1,0:T(8,128)(2,1)S(1)}, u32[]{:S(2)}, u32[]{:S(2)}) %all-to-all-start.1) | async-done | bytes 393248 | tf_op jit(solution)/shard_map/all_to_all | solution.py:34
  40.4 3.8 %all-to-all-start.2 = ((bf16[32,16,256]{2,1,0:T(8,128)(2,1)}), bf16[32,16,256]{2,1,0:T(8,128)(2,1)S(1)}, u32[]{:S(2)}, u32[]{:S(2)}) async-start(bf16[32,16,256]{2,1,0:T(8,128)(2,1)} %copy-done.13), calls=%async_computation.2 | async-start | bytes 524288 | tf_op jit(solution)/shard_map/all_to_all | solution.py:34
  44.3 0.9 copy-done.15
  45.8 1.0 copy-done
  46.8 6.4 %all-to-all-done.2 = bf16[32,16,256]{2,1,0:T(8,128)(2,1)S(1)} async-done(((bf16[32,16,256]{2,1,0:T(8,128)(2,1)}), bf16[32,16,256]{2,1,0:T(8,128)(2,1)S(1)}, u32[]{:S(2)}, u32[]{:S(2)}) %all-to-all-start.2) | async-done | bytes 262176 | tf_op jit(solution)/shard_map/all_to_all | solution.py:34
  53.1 1.2 copy-done.1
  54.9 14.6 %all_to_all.36.sum_ref = f32[8,2,256]{2,1,0:T(2,128)S(1)} all-to-all(f32[8,2,256]{2,1,0:T(2,128)S(1)} %get-tuple-element.28), channel_id=1, replica_groups=mesh['ctx'=32,'head'=8] {'head'}, dimensions={0} | all-to-all | bytes 32768 | tf_op jit(solution)/shard_map/all_to_all | solution.py:34
  69.5 1.2 norm.1
  72.2 5.2 %all-to-all-start.4 = ((bf16[32,24,256]{2,1,0:T(8,128)(2,1)}), bf16[32,24,256]{2,1,0:T(8,128)(2,1)S(1)}, u32[]{:S(2)}, u32[]{:S(2)}) async-start(bf16[32,24,256]{2,1,0:T(8,128)(2,1)} %copy-done.12), calls=%async_computation.4 | async-start | bytes 786432 | tf_op jit(solution)/shard_map/all_to_all | solution.py:34
  77.4 1.2 copy-done.2
  78.6 0.9 copy-done.16
  79.5 0.9 copy-done.25
  80.5 1.3 %kernel_one_back.1 = (f32[256,512]{1,0:T(8,128)S(1)}, f32[256,512]{1,0:T(8,128)S(1)}) custom-call(bf16[256,512]{1,0:T(8,128)(2,1)S(1)} %copy-done.25, bf16[4,128,256]{2,1,0:T(8,128)(2,1)S(1)} %bitcast.14, f32[4,256,256]{2,1,0:T(8,128)S(1)} %copy-done.2, bf16[256,512]{1,0:T(8,128)(2,1)S(1)} %copy-done.16, bf16[256,1024]{1,0:T(8,128)(2,1)S(1)} %bitcast.9), custom_call_target="tpu_custom_call" | custom-call | flops 2000000000 | bytes 3407872 | tf_op jit(solution)/shard_map/kernel_one_back/pallas_call | solution.py:65
  82.6 0.8 copy-done.9
  83.4 4.4 %all-to-all-done.4.got_ref = bf16[32,24,256]{2,1,0:T(8,128)(2,1)S(1)} async-done(((bf16[32,24,256]{2,1,0:T(8,128)(2,1)}), bf16[32,24,256]{2,1,0:T(8,128)(2,1)S(1)}, u32[]{:S(2)}, u32[]{:S(2)}) %all-to-all-start.4) | async-done | bytes 393248 | tf_op jit(solution)/shard_map/all_to_all | solution.py:34
  90.2 3.9 %all-to-all-start.5 = ((bf16[32,24,256]{2,1,0:T(8,128)(2,1)}), bf16[32,24,256]{2,1,0:T(8,128)(2,1)S(1)}, u32[]{:S(2)}, u32[]{:S(2)}) async-start(bf16[32,24,256]{2,1,0:T(8,128)(2,1)} %copy-done.11), calls=%async_computation.5 | async-start | bytes 786432 | tf_op jit(solution)/shard_map/all_to_all | solution.py:34
  95.5 6.2 %inverse_back.1 = (f32[256,128]{1,0:T(8,128)S(1)}, f32[256,128]{1,0:T(8,128)S(1)}) custom-call(s32[1]{0:T(128)} %bitcast.1.head_ref, f32[8,256,256]{2,1,0:T(8,128)S(1)} %get-tuple-element.26.inv_ref, f32[8,128]{1,0:T(8,128)S(1)} %copy-done.29, f32[16,256]{1,0:T(8,128)S(1)} %get-tuple-element.32.ctx_ref, f32[16,256]{1,0:T(8,128)S(1)} %copy-done.27, ...), custom_call_target="tpu_custom_call" | custom-call | flops 5000000000 | bytes 2920452 | tf_op jit(solution)/shard_map/inverse_back/pallas_call | solution.py:65
  103.0 1.0 all-to-all-done.5.got_ref
  104.0 1.0 copy-done.10
  105.1 0.9 copy-done.18
  106.0 0.9 copy-done.20
  106.9 2.2 %landmarks_back.1 = bf16[256,1024]{1,0:T(8,128)(2,1)} custom-call(s32[1]{0:T(128)} %bitcast.1.head_ref, bf16[32,24,256]{2,1,0:T(8,128)(2,1)S(1)} %all-to-all-done.5.got_ref, bf16[256,1024]{1,0:T(8,128)(2,1)S(1)} %bitcast.11, bf16[256,512]{1,0:T(8,128)(2,1)S(1)} %copy-done.4, bf16[256,512]{1,0:T(8,128)(2,1)S(1)} %copy-done.5, f32[256,512]{1,0:T(8,128)S(1)} %copy-done.10, ...), custom_call_target="tpu_custom_call" | custom-call | flops 100000000 | bytes 2752516 | tf_op jit(solution)/shard_map/landmarks_back/pallas_call | solution.py:65
  109.1 6.0 %all-to-all-start.6 = ((bf16[32,8,1024]{2,1,0:T(8,128)(2,1)}), bf16[32,8,1024]{2,1,0:T(8,128)(2,1)S(1)}, u32[]{:S(2)}, u32[]{:S(2)}) async-start(bf16[32,8,1024]{2,1,0:T(8,128)(2,1)} %bitcast.4), calls=%async_computation.6 | async-start | bytes 1048576 | tf_op jit(solution)/shard_map/all_to_all | solution.py:34
  115.1 1.7 %kernel_three_back.1 = (bf16[256,512]{1,0:T(8,128)(2,1)}, f32[256,512]{1,0:T(8,128)S(1)}, f32[1,512]{1,0:T(1,128)}) custom-call(bf16[32,24,256]{2,1,0:T(8,128)(2,1)S(1)} %all-to-all-done.5.got_ref, bf16[256,1024]{1,0:T(8,128)(2,1)S(1)} %bitcast.12, bf16[256,512]{1,0:T(8,128)(2,1)S(1)} %copy-done.4, bf16[256,512]{1,0:T(8,128)(2,1)S(1)} %copy-done.5), custom_call_target="tpu_custom_call" | custom-call | flops 2000000000 | bytes 2230272 | tf_op jit(solution)/shard_map/kernel_three_back/pallas_call | solution.py:65
  116.9 9.9 %all-to-all-done.6.got_ref = bf16[32,8,1024]{2,1,0:T(8,128)(2,1)S(1)} async-done(((bf16[32,8,1024]{2,1,0:T(8,128)(2,1)}), bf16[32,8,1024]{2,1,0:T(8,128)(2,1)S(1)}, u32[]{:S(2)}, u32[]{:S(2)}) %all-to-all-start.6) | async-done | bytes 524320 | tf_op jit(solution)/shard_map/all_to_all | solution.py:34
  126.8 0.9 finish.1
  (53 shorter events, 11.0 us)
Async XLA Ops:
  0.6 1.0 copy-start.3
  1.6 0.9 copy-start.14
  2.5 20.2 %copy-start.5 = (bf16[256,512]{1,0:T(8,128)(2,1)S(1)}, bf16[256,512]{1,0:T(8,128)(2,1)}, u32[]{:S(2)}) copy-start(bf16[256,512]{1,0:T(8,128)(2,1)} %v_ref.5) | copy-start | bytes 786436
  24.8 13.9 %all-to-all-start.1 = ((bf16[32,24,256]{2,1,0:T(8,128)(2,1)}), bf16[32,24,256]{2,1,0:T(8,128)(2,1)S(1)}, u32[]{:S(2)}, u32[]{:S(2)}) async-start(bf16[32,24,256]{2,1,0:T(8,128)(2,1)} %local_context.1), calls=%async_computation.1 | async-start | bytes 786432 | tf_op jit(solution)/shard_map/all_to_all | solution.py:34
  39.1 0.7 copy-start.13
  40.4 12.7 %copy-start.6 = (bf16[256,512]{1,0:T(8,128)(2,1)S(1)}, bf16[256,512]{1,0:T(8,128)(2,1)}, u32[]{:S(2)}) copy-start(bf16[256,512]{1,0:T(8,128)(2,1)} %og_ref.3) | copy-start | bytes 786436
  40.4 12.7 %copy-start.23 = (f32[512]{0:T(512)S(1)}, f32[512]{0:T(512)}, u32[]{:S(2)}) copy-start(f32[512]{0:T(512)} %param.8) | copy-start | bytes 6148
  40.4 12.7 %all-to-all-start.2 = ((bf16[32,16,256]{2,1,0:T(8,128)(2,1)}), bf16[32,16,256]{2,1,0:T(8,128)(2,1)S(1)}, u32[]{:S(2)}, u32[]{:S(2)}) async-start(bf16[32,16,256]{2,1,0:T(8,128)(2,1)} %copy-done.13), calls=%async_computation.2 | async-start | bytes 524288 | tf_op jit(solution)/shard_map/all_to_all | solution.py:34
  44.2 1.0 copy-start.15
  45.8 1.0 copy-start
  53.1 1.2 copy-start.1
  70.7 0.8 copy-start.12
  71.5 0.7 copy-start.24
  72.2 15.6 %all-to-all-start.4 = ((bf16[32,24,256]{2,1,0:T(8,128)(2,1)}), bf16[32,24,256]{2,1,0:T(8,128)(2,1)S(1)}, u32[]{:S(2)}, u32[]{:S(2)}) async-start(bf16[32,24,256]{2,1,0:T(8,128)(2,1)} %copy-done.12), calls=%async_computation.4 | async-start | bytes 786432 | tf_op jit(solution)/shard_map/all_to_all | solution.py:34
  77.4 1.2 copy-start.2
  78.6 0.9 copy-start.16
  79.5 0.9 copy-start.25
  81.8 0.8 copy-start.7
  82.6 0.8 copy-start.9
  87.8 0.7 copy-start.22
  88.8 0.8 copy-start.11
  90.2 13.8 %all-to-all-start.5 = ((bf16[32,24,256]{2,1,0:T(8,128)(2,1)}), bf16[32,24,256]{2,1,0:T(8,128)(2,1)S(1)}, u32[]{:S(2)}, u32[]{:S(2)}) async-start(bf16[32,24,256]{2,1,0:T(8,128)(2,1)} %copy-done.11), calls=%async_computation.5 | async-start | bytes 786432 | tf_op jit(solution)/shard_map/all_to_all | solution.py:34
  94.1 0.7 copy-start.27
  94.8 0.7 copy-start.29
  95.5 8.6 %copy-start.4 = (bf16[256,512]{1,0:T(8,128)(2,1)S(1)}, bf16[256,512]{1,0:T(8,128)(2,1)}, u32[]{:S(2)}) copy-start(bf16[256,512]{1,0:T(8,128)(2,1)} %k_ref.7) | copy-start | bytes 786436
  101.7 0.7 copy-start.17
  102.3 0.7 copy-start.19
  104.0 1.0 copy-start.10
  105.1 0.9 copy-start.18
  106.0 0.9 copy-start.20
  109.1 17.7 %all-to-all-start.6 = ((bf16[32,8,1024]{2,1,0:T(8,128)(2,1)}), bf16[32,8,1024]{2,1,0:T(8,128)(2,1)S(1)}, u32[]{:S(2)}, u32[]{:S(2)}) async-start(bf16[32,8,1024]{2,1,0:T(8,128)(2,1)} %bitcast.4), calls=%async_computation.6 | async-start | bytes 1048576 | tf_op jit(solution)/shard_map/all_to_all | solution.py:34
  115.1 11.6 %copy-start.8 = (f32[256,512]{1,0:T(8,128)S(1)}, f32[256,512]{1,0:T(8,128)}, u32[]{:S(2)}) copy-start(f32[256,512]{1,0:T(8,128)} %copy-done.7) | copy-start | bytes 1572868
  (3 other events, 1.8 us)

commit v3 on v2

v3 whole, which is shorter than its diff:
```python
import functools

import jax
import jax.numpy as jnp
from jax import lax
from jax.experimental import pallas as pl
from jax.experimental.pallas import tpu as pltpu
from jax.sharding import PartitionSpec as P

DH = 128
M = 256
EPS = 1e-06
F32 = jnp.float32
BF16 = jnp.bfloat16
SCALE = DH ** (-0.5)
VMEM_BYTES = 32 * 1024 * 1024
MOST_VMEM = 60 * 1024 * 1024
HALVES = (slice(0, DH), slice(DH, 2 * DH))

NN = (((1,), (0,)), ((), ()))
NT = (((1,), (1,)), ((), ()))
TN = (((0,), (0,)), ((), ()))


def dot(a, b, dims=NN):
    return lax.dot_general(a, b, dims, preferred_element_type=F32)


def split_up(x):
    high = x.astype(BF16)
    return high, (x - high.astype(F32)).astype(BF16)


def exact(a, b, dims=NN):
    a_high, a_low = a if isinstance(a, tuple) else split_up(a)
    b_high, b_low = b if isinstance(b, tuple) else split_up(b)
    return dot(a_high, b_high, dims) + (dot(a_high, b_low, dims) + dot(a_low, b_high, dims))


def exchange(parts, axis, groups=None):
    return lax.all_to_all(parts, axis, 0, 0, axis_index_groups=groups)


def high_low(x):
    high = x.astype(BF16).astype(F32)
    return high, x - high


def rows_of(*rows):
    index = lax.broadcasted_iota(jnp.int32, (8, rows[0].shape[1]), 0)
    out = jnp.zeros((8, rows[0].shape[1]), F32)
    for place, row in enumerate(rows):
        out = jnp.where(index == place, row, out)
    return out


def eye_times(value):
    row = lax.broadcasted_iota(jnp.int32, (M, M), 0)
    col = lax.broadcasted_iota(jnp.int32, (M, M), 1)
    return jnp.where(row == col, value, 0.0).astype(F32)


def head_cols(h):
    return slice(h * DH, (h + 1) * DH)


def halves(x):
    return jnp.concatenate([x[:, :DH], x[:, DH:]], axis=0)


def joined(x):
    n = x.shape[0] // 2
    return jnp.concatenate([x[:n], x[n:]], axis=1)


def own_head(ids_ref, h):
    return pl.ds(pl.multiple_of((ids_ref[0] * 2 + h) * DH, DH), DH)


def stacked(ids_ref, refs, h):
    return jnp.concatenate([ref[:, own_head(ids_ref, h)] for ref in refs], axis=0)


def rows_of(*rows):
    index = lax.broadcasted_iota(jnp.int32, (8, rows[0].shape[1]), 0)
    out = jnp.zeros((8, rows[0].shape[1]), F32)
    for place, row in enumerate(rows):
        out = jnp.where(index == place, row, out)
    return out


def eye_times(value):
    row = lax.broadcasted_iota(jnp.int32, (M, M), 0)
    col = lax.broadcasted_iota(jnp.int32, (M, M), 1)
    return jnp.where(row == col, value, 0.0).astype(F32)


def head_cols(h):
    return slice(h * DH, (h + 1) * DH)


def halves(x):
    return jnp.concatenate([x[:, :DH], x[:, DH:]], axis=0)


def joined(x):
    n = x.shape[0] // 2
    return jnp.concatenate([x[:n], x[n:]], axis=1)


def both_blocks(mine_ref, other_ref, which, h):
    return jnp.concatenate(
        [ref[which, :, head_cols(h)] for ref in (mine_ref, other_ref)], axis=0
    )


def call(
    body, outs, *args, scalars=0, far_in=(), far_out=(), after=(), flops=0,
    vmem=VMEM_BYTES, name
):
    nbytes = sum(a.size * a.dtype.itemsize for a in (*args, *outs))
    n_in, n_after, n_out = len(args), len(after), len(outs)
    n_far = len(far_in) + len(far_out)

    def whole(*refs):
        ins = list(refs[:n_in])
        results = list(refs[n_in + n_after : n_in + n_after + n_out])
        buffers = refs[n_in + n_after + n_out :]
        loads, stores = [], []
        for k, i in enumerate(far_in):
            loads.append(pltpu.make_async_copy(ins[i], buffers[k], buffers[n_far].at[k]))
            ins[i] = buffers[k]
        for k, i in enumerate(far_out, len(far_in)):
            stores.append(
                pltpu.make_async_copy(buffers[k], results[i], buffers[n_far].at[k])
            )
            results[i] = buffers[k]
        for copy in loads:
            copy.start()
        for copy in loads:
            copy.wait()
        body(*ins, *results)
        for copy in stores:
            copy.start()
        for copy in stores:
            copy.wait()

    def space(place, far):
        return pl.BlockSpec(memory_space=pltpu.HBM if place in far else pltpu.VMEM)

    in_specs = [
        pl.BlockSpec(memory_space=pltpu.SMEM) if i < scalars else space(i, far_in)
        for i in range(n_in)
    ] + [pl.BlockSpec(memory_space=pl.ANY)] * n_after
    scratch = [pltpu.VMEM(args[i].shape, args[i].dtype) for i in far_in]
    scratch += [pltpu.VMEM(outs[i].shape, outs[i].dtype) for i in far_out]
    if n_far:
        scratch.append(pltpu.SemaphoreType.DMA((n_far,)))
    return pl.pallas_call(
        whole,
        out_shape=outs,
        in_specs=in_specs,
        out_specs=[space(i, far_out) for i in range(n_out)],
        scratch_shapes=scratch,
        compiler_params=pltpu.CompilerParams(vmem_limit_bytes=vmem),
        cost_estimate=pl.CostEstimate(flops=flops, bytes_accessed=nbytes, transcendentals=0),
        name=name,
    )(*args, *after)


def shape(*dims, dtype=F32):
    return jax.ShapeDtypeStruct(dims, dtype)


def means_body(q_ref, k_ref, out_ref):
    count, land_dev, both = out_ref.shape
    half = both // 2
    seg_len = q_ref.shape[0] // land_dev
    q_mean, k_mean = [
        jnp.sum(ref[...].astype(F32).reshape(land_dev, seg_len, 2 * half), axis=1) / seg_len
        for ref in (q_ref, k_ref)
    ]
    for core in range(2):
        cols = slice(core * half, (core + 1) * half)
        own = jnp.concatenate([q_mean[:, cols], k_mean[:, cols]], axis=1).astype(BF16)
        for chip in range(count // 2):
            out_ref[2 * chip + core] = own


def stack_body(ids_ref, *refs):
    count = len(refs) // 3
    for mine, there, out in zip(refs[:count], refs[count : 2 * count], refs[2 * count :]):
        for h in range(out.shape[1] // DH):
            out[:, head_cols(h)] = stacked(ids_ref, (mine, there), h)


def context_body(land_ref, k_ref, v_ref, out_ref):
    count = out_ref.shape[0]
    heads = land_ref.shape[1] // (2 * DH)
    per_head = count // heads
    cols = DH // per_head
    for h in range(heads):
        keys = k_ref[:, head_cols(h)]
        vals = v_ref[:, head_cols(h)]
        score = dot(keys, land_ref[:, head_cols(h)], NT) * SCALE
        shift = jnp.max(score, axis=0, keepdims=True).astype(BF16).astype(F32)
        exp_local = jnp.exp(score - shift)
        high, low = high_low(jnp.sum(exp_local, axis=0, keepdims=True))
        weighted = dot(vals, exp_local.astype(BF16), TN)
        stats = rows_of(*[row[:, part] for row in (shift, high, low) for part in HALVES])
        for j in range(per_head):
            out_ref[h * per_head + j] = jnp.concatenate(
                [halves(weighted[j * cols : (j + 1) * cols]), stats], axis=0
            ).astype(BF16)


def inverse_body(ids_ref, land_ref, first_ref, again_ref, out_ref):
    half = land_ref.shape[1] // 2
    at = pl.multiple_of(ids_ref[1] * DH, DH)
    lq = land_ref[:, pl.ds(at, DH)]
    lk = land_ref[:, pl.ds(at + half, DH)]
    score = dot(lq, lk, NT) * SCALE
    top = jnp.exp(score - jnp.max(score, axis=1, keepdims=True))
    ktwo = top / jnp.sum(top, axis=1, keepdims=True)
    factor = column_factor(ktwo)
    ktwo_s = split_up(ktwo)
    x = factor * exact(ktwo_s, ktwo_s, NT)
    x_s = split_up(x)
    h2 = eye_times(15.0) - exact(x_s, eye_times(7.0) - x)
    h3 = eye_times(13.0) - exact(x_s, h2)
    h3_s = split_up(h3)
    p1 = 0.25 * exact(x_s, h3_s)
    p1_s = split_up(p1)
    b2 = eye_times(15.0) - exact(p1_s, eye_times(7.0) - p1)
    b3 = eye_times(13.0) - exact(p1_s, b2)
    inverse = (factor * 0.0625) * exact(b3, exact(h3_s, ktwo_s))
    first_ref[...] = inverse
    again_ref[...] = inverse
    for place, part in enumerate((ktwo, x, h2, h3, p1, b2, b3)):
        out_ref[place] = part


def column_factor(ktwo):
    return 1.0 / jnp.max(jnp.sum(ktwo, axis=0, keepdims=True), axis=1, keepdims=True)


def mixing_body(got_ref, inv_ref, out_ref, kept_ref):
    count, rows, _ = got_ref.shape
    cols = (rows - 8) // 2
    tops = got_ref[0].astype(F32)[rows - 8 :]
    for place in range(1, count):
        tops = jnp.maximum(tops, got_ref[place].astype(F32)[rows - 8 :])
    tops = tops[0:2]
    total = jnp.zeros((2, DH), F32)
    left = jnp.zeros((cols, DH), F32)
    right = jnp.zeros((cols, DH), F32)
    for place in range(count):
        part = got_ref[place].astype(F32)
        stats = part[rows - 8 :]
        fade = jnp.exp(stats[0:2] - tops)
        total = total + fade * (stats[2:4] + stats[4:6])
        left = left + fade[0:1] * part[:cols]
        right = right + fade[1:2] * part[cols : 2 * cols]
    total = joined(total)
    context = jnp.concatenate([left, right], axis=1) / total
    mixing = exact(context, inv_ref[...]).astype(BF16)
    for place in range(count):
        out_ref[place] = mixing
    kept_ref[...] = jnp.concatenate([context, rows_of(total, joined(tops))], axis=0)


def softmax_rows(score):
    top = jnp.exp(score - jnp.max(score, axis=1, keepdims=True))
    return top / jnp.sum(top, axis=1, keepdims=True)


def kernel_one(q_ref, land_ref, h):
    heads = land_ref.shape[1] // (2 * DH)
    score = dot(q_ref[:, head_cols(h)], land_ref[:, head_cols(heads + h)], NT) * SCALE
    return softmax_rows(score)


def ahead_body(
    q_ref, k_ref, land_ref, first_ref, again_ref, exp_ref
):
    heads, tok, _ = first_ref.shape
    for h in range(heads):
        kone = kernel_one(q_ref, land_ref, h).astype(BF16)
        first_ref[h] = kone
        again_ref[h] = kone
        keys = k_ref[:, head_cols(h)]
        score = dot(keys, land_ref[:, head_cols(h)], NT) * SCALE
        shift = jnp.max(score, axis=0, keepdims=True)
        exp_ref[h, :tok] = jnp.exp(score - shift)
        exp_ref[h, tok:] = rows_of(shift)


def output_body(ids_ref, kone_ref, mix_ref, g_ref, gain_ref, out_ref, sum_ref):
    heads, tok, _ = kone_ref.shape
    squares = jnp.zeros((tok, DH), F32)
    slopes = jnp.zeros((tok, DH), F32)
    for h in range(heads):
        out = dot(kone_ref[h], mix_ref[h], NT)
        out_ref[:, head_cols(h)] = out
        grad = g_ref[:, head_cols(h)].astype(F32)
        squares = squares + out * out
        slopes = slopes + grad * gain_ref[:, own_head(ids_ref, h)] * out
    high, low = split_up(jnp.concatenate([squares, slopes], axis=0))
    ones = jnp.ones((8, DH), BF16)
    row = (dot(ones, high, NT) + dot(ones, low, NT))[0:1]
    both = rows_of(
        swap_blocks(ids_ref, row[:, :tok], 1), swap_blocks(ids_ref, row[:, tok:], 1)
    )
    for place in range(sum_ref.shape[0]):
        sum_ref[place] = both[:2]


def swap_blocks(ids_ref, x, axis):
    size = x.shape[axis] // 2
    left = lax.slice_in_dim(x, 0, size, axis=axis)
    right = lax.slice_in_dim(x, size, 2 * size, axis=axis)
    swapped = jnp.concatenate([right, left], axis=axis)
    return jnp.where(ids_ref[0] == 0, x, swapped)


def token_factors(ids_ref, sum_ref, features):
    total = sum_ref[0]
    for place in range(1, sum_ref.shape[0]):
        total = total + sum_ref[place]
    root_inv = lax.rsqrt(total[0:1] / features + EPS)
    slope = total[1:2] * root_inv / features
    columns = jnp.transpose(
        rows_of(
            swap_blocks(ids_ref, root_inv, 1), swap_blocks(ids_ref, root_inv * slope, 1)
        )
    )
    return columns[:, 0:1], columns[:, 1:2]


def output_grad(factors, out, grad, gain):
    root_inv, bent = factors
    return (root_inv * (grad * gain - out * bent)).astype(BF16)


def norm_body(ids_ref, sum_ref, out_ref, g_ref, gain_ref, kone_ref, part_ref):
    heads = kone_ref.shape[0]
    per_head = part_ref.shape[0] // heads
    cols = DH // per_head
    factors = token_factors(ids_ref, sum_ref, heads * DH * sum_ref.shape[0])
    for h in range(heads):
        out = out_ref[:, head_cols(h)]
        grad = g_ref[:, head_cols(h)].astype(F32)
        gain = gain_ref[:, own_head(ids_ref, h)]
        g_mixing = dot(output_grad(factors, out, grad, gain), kone_ref[h], TN)
        gain_sum = jnp.sum(grad * (out * factors[0]), axis=0, keepdims=True)
        tail = rows_of(*high_low(gain_sum))
        for j in range(per_head):
            part_ref[h * per_head + j] = jnp.concatenate(
                [halves(g_mixing[j * cols : (j + 1) * cols]), tail], axis=0
            ).astype(BF16)


def query_body(
    ids_ref, sum_ref, out_ref, g_ref, gain_ref, mix_ref, q_ref, land_ref,
    norm_mine, norm_other, query_mine, query_other, keyland_ref,
):
    heads = mix_ref.shape[0]
    tok = norm_mine.shape[0]
    factors = token_factors(ids_ref, sum_ref, heads * DH * sum_ref.shape[0])
    for h in range(heads):
        out = out_ref[:, head_cols(h)]
        grad = g_ref[:, head_cols(h)].astype(F32)
        gain = gain_ref[:, own_head(ids_ref, h)]
        normed = (out * factors[0] * gain).astype(BF16)
        norm_mine[:, head_cols(h)] = normed[:tok]
        norm_other[:, head_cols(h)] = normed[tok:]
        kone = kernel_one(q_ref, land_ref, h)
        g_kernel = dot(output_grad(factors, out, grad, gain), mix_ref[h])
        inner = jnp.sum(kone * g_kernel, axis=1, keepdims=True)
        g_score = (kone * (g_kernel - inner)).astype(BF16)
        query = dot(g_score, land_ref[:, head_cols(heads + h)]) * SCALE
        query_mine[:, head_cols(h)] = query[:tok]
        query_other[:, head_cols(h)] = query[tok:]
        queries = q_ref[:, head_cols(h)]
        keyland_ref[:, head_cols(h)] = dot(g_score, queries, TN) * SCALE


def grad_context_body(got_ref, inv_ref, kept_ref, out_ref, g_ref):
    count, rows, _ = got_ref.shape
    cols = (rows - 8) // 2
    got = got_ref[0].astype(F32)
    for place in range(1, count):
        got = got + got_ref[place].astype(F32)
    g_mixing = joined(got[: 2 * cols])
    gain = high_low(got[2 * cols : 2 * cols + 1] + got[2 * cols + 1 : 2 * cols + 2])
    context = kept_ref[:cols]
    total = kept_ref[cols : cols + 1]
    top = kept_ref[cols + 1 : cols + 2]
    g_context = exact(g_mixing, inv_ref[...], NT)
    high, low = high_low(-jnp.sum(g_context * context, axis=0, keepdims=True) / total)
    tail = rows_of(
        *[row[:, part] for row in (high, low) for part in HALVES],
        *gain,
        *[top[:, part] for part in HALVES],
    )
    mine = jnp.concatenate([halves(g_context / total), tail], axis=0).astype(BF16)
    for place in range(count):
        out_ref[place] = mine
    g_ref[...] = g_mixing


def inverse_back_body(ids_ref, inv_ref, kept_ref, g_ref, land_ref, keyland_ref, out_ref):
    half = land_ref.shape[1] // 2
    at = pl.multiple_of(ids_ref[1] * DH, DH)
    lq = land_ref[:, pl.ds(at, DH)]
    lk = land_ref[:, pl.ds(at + half, DH)]
    ktwo, x, h2, h3, p1, b2, b3 = [inv_ref[place] for place in range(7)]
    factor = column_factor(ktwo)
    ktwo_s, x_s, h3_s, p1_s, b3_s = [split_up(part) for part in (ktwo, x, h3, p1, b3)]
    g_mixing = split_up(g_ref[...])
    context = split_up(kept_ref[: g_ref.shape[0]])
    inner = split_up(exact(context, b3_s))
    outer = exact(inner, h3_s)
    d_outer = split_up((factor * 0.0625) * exact(g_mixing, ktwo_s, NT))
    d_inner = exact(d_outer, h3_s)
    d_b3 = split_up(exact(context, d_inner, TN))
    d_b2 = split_up(-exact(p1_s, d_b3))
    d_b1 = -exact(p1_s, d_b2)
    d_p1 = -exact(d_b3, b2) - exact(d_b2, eye_times(7.0) - p1) - d_b1
    d_p1 = split_up(d_p1)
    d_h3 = split_up(exact(inner, d_outer, TN) + 0.25 * exact(x_s, d_p1))
    d_h2 = split_up(-exact(x_s, d_h3))
    d_h1 = -exact(x_s, d_h2)
    d_x = 0.25 * exact(d_p1, h3_s) - exact(d_h3, h2) - exact(d_h2, eye_times(7.0) - x) - d_h1
    d_ktwo = (factor * 0.0625) * exact(outer, g_mixing, TN) + factor * exact(
        d_x + jnp.transpose(d_x), ktwo_s
    )
    g_score = ktwo * (d_ktwo - jnp.sum(ktwo * d_ktwo, axis=1, keepdims=True))
    out_ref[:, :half] = jnp.zeros((M, half), F32)
    out_ref[:, half:] = keyland_ref[...]
    high, low = split_up(g_score)
    out_ref[:, pl.ds(at, DH)] = (dot(high, lk) + dot(low, lk)) * SCALE
    out_ref[:, pl.ds(at + half, DH)] = keyland_ref[:, pl.ds(at, DH)] + (
        (dot(high, lq, TN) + dot(low, lq, TN)) * SCALE
    )


def unpacked(got_ref, h, heads):
    count, rows, _ = got_ref.shape
    per_head = count // heads
    cols = (rows - 8) // 2
    parts = [got_ref[h * per_head + j] for j in range(per_head)]
    g_weighted = jnp.concatenate(
        [
            jnp.concatenate([part[:cols], part[cols : 2 * cols]], axis=1)
            for part in parts
        ],
        axis=0,
    )
    tails = [part.astype(F32)[2 * cols :] for part in parts]
    summed = functools.reduce(jnp.add, tails)
    g_totals = joined(summed[0:2] + summed[2:4])
    top = joined(tails[0][6:8])
    gain = tails[0][4:5] + tails[0][5:6]
    return g_weighted, g_totals, top, gain


def queryland_body(got_ref, exp_ref, k_ref, v_ref, extra_ref, out_ref, again_ref):
    heads = exp_ref.shape[0]
    half = heads * DH
    for h in range(heads):
        g_weighted, g_totals, top, _ = unpacked(got_ref, h, heads)
        keys = k_ref[:, head_cols(h)]
        vals = v_ref[:, head_cols(h)]
        tok = keys.shape[0]
        exp_three = exp_ref[h, :tok] * jnp.exp(exp_ref[h, tok : tok + 1] - top)
        g_score = (exp_three * (dot(vals, g_weighted) + g_totals)).astype(BF16)
        queryland = dot(g_score, keys, TN) * SCALE
        out_ref[:, head_cols(h)] = (queryland + extra_ref[:, head_cols(h)]).astype(BF16)
    out_ref[:, half:] = extra_ref[:, half:].astype(BF16)
    again_ref[...] = got_ref[...]


def value_body(
    ids_ref, k_ref, v_ref, land_ref, land_there, got_ref, got_there,
    value_out, key_out, gain_out,
):
    heads = land_ref.shape[1] // (2 * DH)

    def place_halves(core, own, away):
        for place, land, got in ((own, land_ref, got_ref), (away, land_there, got_there)):
            for h in range(heads):
                cols = slice(place.start + h * DH, place.start + (h + 1) * DH)
                g_weighted, g_totals, top, gain = unpacked(got, h, heads)
                lq = land[:, head_cols(h)]
                exp_three = jnp.exp(dot(k_ref[:, cols], lq, NT) * SCALE - top)
                g_exp = dot(v_ref[:, cols], g_weighted) + g_totals
                value_out[:, cols] = dot(exp_three.astype(BF16), g_weighted, NT).astype(BF16)
                key_out[:, cols] = dot((exp_three * g_exp).astype(BF16), lq) * SCALE
                gain_out[:, cols] = gain

    by_core(ids_ref, place_halves)


def by_core(ids_ref, place_halves):
    half = 2 * DH
    left, right = slice(0, half), slice(half, 2 * half)

    @pl.when(ids_ref[0] == 0)
    def _():
        place_halves(0, left, right)

    @pl.when(ids_ref[0] != 0)
    def _():
        place_halves(1, right, left)


def gather_body(ids_ref, norm_mine, norm_there, norm_out):
    def place_halves(core, own, away):
        norm_out[:, own] = norm_mine[...]
        norm_out[:, away] = norm_there[...]

    by_core(ids_ref, place_halves)


def finish_body(
    ids_ref, got_ref, query_mine, query_there, key_ref, query_out, key_out
):
    count, land_dev, both = got_ref.shape
    tok, half = query_mine.shape
    seg_len = tok // land_dev
    lands = []
    for core in range(2):
        got = got_ref[core].astype(F32)
        for chip in range(1, count // 2):
            got = got + got_ref[2 * chip + core].astype(F32)
        lands.append(got / seg_len)
    spans = [(row, slice(row * seg_len, (row + 1) * seg_len)) for row in range(land_dev)]

    def place_halves(core, own, away):
        for place, land, ref in (
            (own, lands[core], query_mine), (away, lands[1 - core], query_there)
        ):
            for row, span in spans:
                query_out[span, place] = (ref[span] + land[row : row + 1, :half]).astype(BF16)

    by_core(ids_ref, place_halves)
    for core in range(2):
        place = slice(core * half, (core + 1) * half)
        for row, span in spans:
            key_out[span, place] = (
                key_ref[span, place] + lands[core][row : row + 1, half:]
            ).astype(BF16)


def on_device(queries, keys_in, values, norm_gain, out_grad):
    tok, width = queries.shape
    half = width // 2
    heads = half // DH
    n_ctx = lax.axis_size("ctx")
    n_head = lax.axis_size("head")
    chips = n_ctx // 2
    per_head = chips // heads
    cols = DH // per_head
    land_dev = M // n_ctx
    here = lax.axis_index("ctx").astype(jnp.int32)
    ids = jnp.stack([lax.rem(here, 2), lax.div(here, 2 * per_head)])
    gain = norm_gain.reshape(1, width)
    same_core = [list(range(core, n_ctx, 2)) for core in range(2)]
    same_chip = [
        [(2 * chip + core) * n_head + z for core in range(2) for z in range(n_head)]
        for chip in range(chips)
    ]
    swap = [(i, i ^ 1) for i in range(n_ctx)]
    packed = shape(chips, 2 * cols + 8, DH, dtype=BF16)
    block = shape(tok, half)
    block_b = shape(tok, half, dtype=BF16)
    wide_b = shape(tok, width, dtype=BF16)
    units = shape(heads, 2 * tok, M, dtype=BF16)

    both_b = shape(2 * tok, half, dtype=BF16)
    k_there, v_there, q_there, g_there = [
        lax.ppermute(x, "ctx", swap) for x in (keys_in, values, queries, out_grad)
    ]
    (own,) = call(
        means_body, [shape(n_ctx, land_dev, 2 * half, dtype=BF16)], queries, keys_in,
        far_in=(0, 1), far_out=(0,), vmem=MOST_VMEM, flops=10**6, name="landmark_means",
    )
    land = exchange(own, "ctx").reshape(M, 2 * half)
    keys, vals = call(
        stack_body, [both_b, both_b], ids, keys_in, values, k_there, v_there,
        scalars=1, after=(own,), flops=10**6, name="stack_kv",
    )

    (parts,) = call(context_body, [packed], land, keys, vals, flops=10**8, name="local_context")
    got = exchange(parts, "ctx", same_core)
    inverse, inverse_again, chain = call(
        inverse_body, [shape(M, M), shape(M, M), shape(7, M, M)], ids, land,
        scalars=1, after=(parts,), flops=3 * 10**9, name="inverse",
    )
    parts, kept = call(
        mixing_body, [shape(chips, cols, M, dtype=BF16), shape(cols + 8, M)],
        got, inverse, flops=10**8, name="mixing",
    )
    land_there = lax.ppermute(land, "ctx", swap)
    qs, grads = call(
        stack_body, [both_b, both_b], ids, queries, out_grad, q_there, g_there,
        scalars=1, after=(parts,), flops=10**6, name="stack_qg",
    )
    kone, kone_again, exp_local = call(
        ahead_body, [units, units, shape(heads, 2 * tok + 8, M)], qs, keys, land,
        far_out=(2,), after=(parts,), flops=2 * 10**9, name="ahead",
    )
    mixing = exchange(parts, "ctx", same_core).reshape(heads, DH, M)

    output, sums = call(
        output_body, [shape(2 * tok, half), shape(2 * n_head, 2, 2 * tok)],
        ids, kone, mixing, grads, gain, scalars=1, flops=10**8, name="output",
    )
    sums = exchange(sums, ("ctx", "head"), same_chip)
    (parts,) = call(
        norm_body, [packed], ids, sums, output, grads, gain, kone_again,
        scalars=1, flops=10**8, name="norm",
    )
    got = exchange(parts, "ctx", same_core)
    norm_mine, norm_other, query_mine, query_other, keyland = call(
        query_body, [block_b, block_b, block, block, shape(M, half)],
        ids, sums, output, grads, gain, mixing, qs, land,
        scalars=1, after=(parts,), flops=2 * 10**9, name="kernel_one_back",
    )
    parts, g_mixing = call(
        grad_context_body, [packed, shape(cols, M)], got, inverse_again, kept,
        after=(keyland,), flops=10**8, name="context_back",
    )
    got = exchange(parts, "ctx", same_core)
    (extra,) = call(
        inverse_back_body, [shape(M, 2 * half)], ids, chain, kept, g_mixing, land, keyland,
        scalars=1, after=(parts,), flops=5 * 10**9, name="inverse_back",
    )
    both, got = call(
        queryland_body, [shape(M, 2 * half, dtype=BF16), packed],
        got, exp_local, keys, vals, extra, far_in=(1,), flops=10**8, name="landmarks_back",
    )
    landed = exchange(both.reshape(n_ctx, land_dev, 2 * half), "ctx")
    norm_there = lax.ppermute(norm_other, "ctx", swap)
    query_there = lax.ppermute(query_other, "ctx", swap)
    got_there = lax.ppermute(got, "ctx", swap)
    (normed,) = call(
        gather_body, [wide_b], ids, norm_mine, norm_there,
        scalars=1, after=(both,), flops=10**6, name="gather",
    )
    value_grad, key_three, gain_grad = call(
        value_body, [wide_b, shape(tok, width), shape(1, width)],
        ids, keys_in, values, land, land_there, got, got_there,
        scalars=1, after=(both,), flops=2 * 10**9, name="kernel_three_back",
    )
    query_grad, key_grad = call(
        finish_body, [wide_b, wide_b], ids, landed, query_mine, query_there, key_three,
        scalars=1, after=(normed,), flops=10**6, name="finish",
    )
    return (normed, query_grad, key_grad, value_grad, gain_grad.reshape(width))


def solution(mesh):
    return jax.shard_map(
        on_device,
        mesh=mesh,
        in_specs=(
            P("ctx", "head"),
            P("ctx", "head"),
            P("ctx", "head"),
            P("head"),
            P("ctx", "head"),
        ),
        out_specs=(
            P("ctx", "head"),
            P("ctx", "head"),
            P("ctx", "head"),
            P("ctx", "head"),
            P("head"),
        ),
        check_vma=False,
    )
```

time: 129 us -> 113 us (0.88)
  blocking collectives: 34.6 us -> 0 us
  starting transfers between devices: 22.5 us -> 46.9 us
  local copies, waits for them, and re-layouts: 20.7 us -> 11.5 us
  Pallas kernels: 21.7 us -> 28.5 us
  waiting for transfers between devices: 27.2 us -> 24.4 us
    all_to_all x2 -> x0, blocking collectives: 34.6 us -> none  [exchange(): return lax.all_to_all(parts, axis, 0, 0)]
    all_to_all x5 -> x7, starting transfers between devices: 22.5 us -> 39.3 us  [exchange(): return lax.all_to_all(parts, axis, 0, 0, axis_index_groups=groups)]
    unnamed x60 -> x50, local copies, waits for them, and re-layouts: 20.7 us -> 11.5 us
    ppermute x0 -> x8, starting transfers between devices: none -> 7.55 us  [the longest x4 4.03 us: on_device(): lax.ppermute(x, 'ctx', swap)]
    pallas_call x13 -> x16, Pallas kernels: 21.7 us -> 28.5 us  [call(): pl.pallas_call(whole, out_shape=outs, in_specs=in_specs, out_specs=[space...]
    all_to_all x5 -> x7, waiting for transfers between devices: 27.2 us -> 24.4 us  [exchange(): return lax.all_to_all(parts, axis, 0, 0, axis_index_groups=groups)]
  transfers between devices with their start and end apart: 5 -> 15, of which waited for: 5 -> 6; matrix products, arithmetic and copies ran while one was open for 0% -> 0% of each run, Pallas kernels for 11% -> 23%
where the time goes in v3:
time: 113 us; the launch traced here: 112 us
  starting transfers between devices  46.9 us (42%)
  Pallas kernels  28.5 us (25%)
  waiting for transfers between devices  24.4 us (22%)
  local copies, waits for them, and re-layouts  11.5 us (10%)
    all_to_all x7, starting transfers between devices, exchange(): return lax.all_to_all(parts, axis, 0, 0, axis_index_groups=groups)  39.3 us
    pallas_call x16, Pallas kernels, call(): pl.pallas_call(whole, out_shape=outs, in_specs=in_specs, out_specs=[space...  28.5 us
    all_to_all x7, waiting for transfers between devices, exchange(): return lax.all_to_all(parts, axis, 0, 0, axis_index_groups=groups)  24.4 us
    unnamed x50, local copies, waits for them, and re-layouts  11.5 us
    ppermute x4, starting transfers between devices, on_device(): lax.ppermute(x, 'ctx', swap)  4.03 us
    ppermute x1, starting transfers between devices, on_device(): got_there = lax.ppermute(got, 'ctx', swap)  2.83 us
  transfers between devices with their start and end apart: 15, of which 6 were waited for; matrix products, arithmetic and copies ran while one was open for 0% of the time, Pallas kernels for 23%

profile of v3, /device:TPU:1, one launch (start us, length us, event | category | flops | bytes accessed | tf_op | source)
XLA Modules:
  0.0 112.3 jit_solution(12653204609578212747)
XLA Ops:
  0.6 3.3 %collective-permute-start.2 = (bf16[256,512]{1,0:T(8,128)(2,1)}, bf16[256,512]{1,0:T(8,128)(2,1)S(1)}, u32[]{:S(2)}, u32[]{:S(2)}) collective-permute-start(bf16[256,512]{1,0:T(8,128)(2,1)} %refs_1_.7), channel_id=1, source_target_pairs={{0,8},{8,0},{16,24},{24,16},{32,40},{40,32},{48,56},{56,48},{64,72... | collective-permute-start | bytes 786440 | tf_op jit(solution)/shard_map/ppermute | solution.py:583
  4.1 1.9 %landmark_means.1.refs_5_ = bf16[32,8,512]{2,1,0:T(8,128)(2,1)} custom-call(bf16[256,512]{1,0:T(8,128)(2,1)} %refs_1_.6, bf16[256,512]{1,0:T(8,128)(2,1)} %refs_1_.7), custom_call_target="tpu_custom_call" | custom-call | flops 1000000 | bytes 786432 | tf_op jit(solution)/shard_map/landmark_means/pallas_call | solution.py:159
  6.0 5.8 %all-to-all-start = ((bf16[32,8,512]{2,1,0:T(8,128)(2,1)}), bf16[32,8,512]{2,1,0:T(8,128)(2,1)S(1)}, u32[]{:S(2)}, u32[]{:S(2)}) async-start(bf16[32,8,512]{2,1,0:T(8,128)(2,1)} %landmark_means.1.refs_5_), calls=%async_computation | async-start | bytes 524288 | tf_op jit(solution)/shard_map/all_to_all | solution.py:41
  12.4 0.9 copy-done
  13.4 0.9 copy-done.1
  14.3 0.9 copy-done.7
  15.9 4.8 %all-to-all-done = bf16[32,8,512]{2,1,0:T(8,128)(2,1)S(1)} async-done(((bf16[32,8,512]{2,1,0:T(8,128)(2,1)}), bf16[32,8,512]{2,1,0:T(8,128)(2,1)S(1)}, u32[]{:S(2)}, u32[]{:S(2)}) %all-to-all-start) | async-done | bytes 262176 | tf_op jit(solution)/shard_map/all_to_all | solution.py:41
  20.7 1.6 %local_context.1.refs_2_ = bf16[16,40,128]{2,1,0:T(8,128)(2,1)} custom-call(bf16[256,512]{1,0:T(8,128)(2,1)S(1)} %bitcast.7, bf16[512,256]{1,0:T(8,128)(2,1)S(1)} %get-tuple-element.33.refs_1_.refs_2_, bf16[512,256]{1,0:T(8,128)(2,1)S(1)} %get-tuple-element.34.refs_2_.refs_3_), custom_call_target="tpu_custom_call" | custom-call | flops 100000000 | bytes 950272 | tf_op jit(solution)/shard_map/local_context/pallas_call | solution.py:159
  22.4 3.5 %all-to-all-start.1 = ((bf16[16,40,128]{2,1,0:T(8,128)(2,1)}), bf16[16,40,128]{2,1,0:T(8,128)(2,1)S(1)}, u32[]{:S(2)}, u32[]{:S(2)}) async-start(bf16[16,40,128]{2,1,0:T(8,128)(2,1)} %local_context.1.refs_2_), calls=%async_computation.1 | async-start | bytes 327680 | tf_op jit(solution)/shard_map/all_to_all | solution.py:41
  25.9 3.1 %inverse.1 = (f32[256,256]{1,0:T(8,128)S(1)}, f32[256,256]{1,0:T(8,128)S(1)}, f32[7,256,256]{2,1,0:T(8,128)S(1)}) custom-call(s32[2]{0:T(128)S(1)} %pad_add_fusion.refs_0_, bf16[256,512]{1,0:T(8,128)(2,1)S(1)} %bitcast.8, bf16[16,40,128]{2,1,0:T(8,128)(2,1)} %local_context.1.refs_2_), custom_call_target="tpu_custom_call" | custom-call | flops 3000000000 | bytes 2621448 | tf_op jit(solution)/shard_map/inverse/pallas_call | solution.py:159
  29.1 1.3 %copy-done.23 = f32[7,256,256]{2,1,0:T(8,128)} copy-done((f32[7,256,256]{2,1,0:T(8,128)}, f32[7,256,256]{2,1,0:T(8,128)S(1)}, u32[]{:S(2)}) %copy-start.23) | copy-done | bytes 1835032
  30.3 2.5 %all-to-all-done.1.refs_0_ = bf16[16,40,128]{2,1,0:T(8,128)(2,1)S(1)} async-done(((bf16[16,40,128]{2,1,0:T(8,128)(2,1)}), bf16[16,40,128]{2,1,0:T(8,128)(2,1)S(1)}, u32[]{:S(2)}, u32[]{:S(2)}) %all-to-all-start.1) | async-done | bytes 163872 | tf_op jit(solution)/shard_map/all_to_all | solution.py:41
  33.7 4.1 %all-to-all-start.2 = ((bf16[16,16,256]{2,1,0:T(8,128)(2,1)}), bf16[16,16,256]{2,1,0:T(8,128)(2,1)S(1)}, u32[]{:S(2)}, u32[]{:S(2)}) async-start(bf16[16,16,256]{2,1,0:T(8,128)(2,1)} %get-tuple-element.36.refs_5_.refs_3_), calls=%async_computation.2 | async-start | bytes 262144 | tf_op jit(solution)/shard_map/all_to_all | solution.py:41
  40.3 4.4 %all-to-all-done.2 = bf16[16,16,256]{2,1,0:T(8,128)(2,1)S(1)} async-done(((bf16[16,16,256]{2,1,0:T(8,128)(2,1)}), bf16[16,16,256]{2,1,0:T(8,128)(2,1)S(1)}, u32[]{:S(2)}, u32[]{:S(2)}) %all-to-all-start.2) | async-done | bytes 131104 | tf_op jit(solution)/shard_map/all_to_all | solution.py:41
  44.7 1.7 %output.1 = (f32[512,256]{1,0:T(8,128)S(1)}, f32[16,2,512]{2,1,0:T(2,128)}) custom-call(s32[2]{0:T(128)S(1)} %pad_add_fusion.refs_0_, bf16[2,512,256]{2,1,0:T(8,128)(2,1)S(1)} %get-tuple-element.38.refs_1_, bf16[2,128,256]{2,1,0:T(8,128)(2,1)S(1)} %bitcast.14, bf16[512,256]{1,0:T(8,128)(2,1)S(1)} %get-tuple-element.39.refs_3_, f32[1,512]{1,0:T(1,128)S(1)} %bitcast.16), custom_call_target="tpu_custom_call" | custom-call | flops 100000000 | bytes 1509384 | tf_op jit(solution)/shard_map/output/pallas_call | solution.py:159
  46.4 10.4 %all-to-all-start.3 = ((f32[16,2,512]{2,1,0:T(2,128)}), f32[16,2,512]{2,1,0:T(2,128)S(1)}, u32[]{:S(2)}, u32[]{:S(2)}) async-start(f32[16,2,512]{2,1,0:T(2,128)} %get-tuple-element.40), calls=%async_computation.3 | async-start | bytes 131072 | tf_op jit(solution)/shard_map/all_to_all | solution.py:41
  57.0 7.0 %all-to-all-done.3.refs_1_ = f32[16,2,512]{2,1,0:T(2,128)S(1)} async-done(((f32[16,2,512]{2,1,0:T(2,128)}), f32[16,2,512]{2,1,0:T(2,128)S(1)}, u32[]{:S(2)}, u32[]{:S(2)}) %all-to-all-start.3) | async-done | bytes 65568 | tf_op jit(solution)/shard_map/all_to_all | solution.py:41
  64.0 1.0 copy-done.6
  65.0 1.9 %norm.1.refs_8_ = bf16[16,40,128]{2,1,0:T(8,128)(2,1)} custom-call(s32[2]{0:T(128)S(1)} %pad_add_fusion.refs_0_, f32[16,2,512]{2,1,0:T(2,128)S(1)} %all-to-all-done.3.refs_1_, f32[512,256]{1,0:T(8,128)S(1)} %get-tuple-element.41.refs_2_, bf16[512,256]{1,0:T(8,128)(2,1)S(1)} %get-tuple-element.39.refs_3_, f32[1,512]{1,0:T(1,128)S(1)} %bitcast.17, ...), custom_call_target="tpu_custom_call" | custom-call | flops 100000000 | bytes 1542152 | tf_op jit(solution)/shard_map/norm/pallas_call | solution.py:159
  66.9 3.5 %all-to-all-start.4 = ((bf16[16,40,128]{2,1,0:T(8,128)(2,1)}), bf16[16,40,128]{2,1,0:T(8,128)(2,1)S(1)}, u32[]{:S(2)}, u32[]{:S(2)}) async-start(bf16[16,40,128]{2,1,0:T(8,128)(2,1)} %norm.1.refs_8_), calls=%async_computation.4 | async-start | bytes 327680 | tf_op jit(solution)/shard_map/all_to_all | solution.py:41
  71.4 3.0 %kernel_one_back.1 = (bf16[256,256]{1,0:T(8,128)(2,1)S(1)}, bf16[256,256]{1,0:T(8,128)(2,1)}, f32[256,256]{1,0:T(8,128)S(1)}, f32[256,256]{1,0:T(8,128)S(1)}, f32[256,256]{1,0:T(8,128)S(1)}) custom-call(s32[2]{0:T(128)S(1)} %pad_add_fusion.refs_0_, f32[16,2,512]{2,1,0:T(2,128)S(1)} %all-to-all-done.3.refs_1_, f32[512,256]{1,0:T(8,128)S(1)} %get-tuple-element.41.refs_2_, ...), custom_call_target="tpu_custom_call" | custom-call | flops 2000000000 | bytes 2557960 | tf_op jit(solution)/shard_map/kernel_one_back/pallas_call | solution.py:159
  77.3 0.9 context_back.1
  78.3 5.8 %all-to-all-start.5 = ((bf16[16,40,128]{2,1,0:T(8,128)(2,1)}), bf16[16,40,128]{2,1,0:T(8,128)(2,1)S(1)}, u32[]{:S(2)}, u32[]{:S(2)}) async-start(bf16[16,40,128]{2,1,0:T(8,128)(2,1)} %get-tuple-element.48.refs_6_), calls=%async_computation.5 | async-start | bytes 327680 | tf_op jit(solution)/shard_map/all_to_all | solution.py:41
  85.0 1.5 %copy-done.24 = f32[7,256,256]{2,1,0:T(8,128)S(1)} copy-done((f32[7,256,256]{2,1,0:T(8,128)S(1)}, f32[7,256,256]{2,1,0:T(8,128)}, u32[]{:S(2)}) %copy-start.24) | copy-done | bytes 1835032
  86.5 4.2 %inverse_back.1.refs_4_ = f32[256,512]{1,0:T(8,128)S(1)} custom-call(s32[2]{0:T(128)S(1)} %pad_add_fusion.refs_0_, f32[7,256,256]{2,1,0:T(8,128)S(1)} %copy-done.24, f32[24,256]{1,0:T(8,128)S(1)} %get-tuple-element.46.refs_2_, f32[16,256]{1,0:T(8,128)S(1)} %get-tuple-element.51.refs_3_, bf16[256,512]{1,0:T(8,128)(2,1)S(1)} %bitcast.12, ...), custom_call_target="tpu_custom_call" | custom-call | flops 5000000000 | bytes 2924552 | tf_op jit(solution)/shard_map/inverse_back/pallas_call | solution.py:159
  90.8 1.4 %landmarks_back.1 = (bf16[256,512]{1,0:T(8,128)(2,1)}, bf16[16,40,128]{2,1,0:T(8,128)(2,1)}) custom-call(bf16[16,40,128]{2,1,0:T(8,128)(2,1)S(1)} %all-to-all-done.5.refs_0_, f32[2,520,256]{2,1,0:T(8,128)S(1)} %get-tuple-element.49.refs_1_, bf16[512,256]{1,0:T(8,128)(2,1)S(1)} %get-tuple-element.33.refs_1_.refs_2_, ...), custom_call_target="tpu_custom_call" | custom-call | flops 100000000 | bytes 2703360 | tf_op jit(solution)/shard_map/landmarks_back/pallas_call | solution.py:159
  92.3 2.8 %collective-permute-start.7 = (bf16[16,40,128]{2,1,0:T(8,128)(2,1)}, bf16[16,40,128]{2,1,0:T(8,128)(2,1)S(1)}, u32[]{:S(2)}, u32[]{:S(2)}) collective-permute-start(bf16[16,40,128]{2,1,0:T(8,128)(2,1)} %get-tuple-element.55.refs_5_), channel_id=1, source_target_pairs={{0,8},{8,0},{16,24},{24,16},{32,40},{40,32},{48,56},{56,48},{64,72... | collective-permute-start | bytes 491528 | tf_op jit(solution)/shard_map/ppermute | solution.py:647
  95.6 6.2 %all-to-all-start.6 = ((bf16[32,8,512]{2,1,0:T(8,128)(2,1)}), bf16[32,8,512]{2,1,0:T(8,128)(2,1)S(1)}, u32[]{:S(2)}, u32[]{:S(2)}) async-start(bf16[32,8,512]{2,1,0:T(8,128)(2,1)} %bitcast.5), calls=%async_computation.6 | async-start | bytes 524288 | tf_op jit(solution)/shard_map/all_to_all | solution.py:41
  101.9 1.3 %gather.1.refs_5_ = bf16[256,512]{1,0:T(8,128)(2,1)} custom-call(s32[2]{0:T(128)S(1)} %pad_add_fusion.refs_0_, bf16[256,256]{1,0:T(8,128)(2,1)S(1)} %copy-done.17, bf16[256,256]{1,0:T(8,128)(2,1)S(1)} %collective-permute-done.4.refs_2_, bf16[256,512]{1,0:T(8,128)(2,1)} %get-tuple-element.52.refs_3_.refs_7_), custom_call_target="tpu_custom_call" | custom-call | flops 1000000 | bytes 524296 | tf_op jit(solution)/shard_map/gather/pallas_call | solution.py:159
  103.2 2.8 %kernel_three_back.1 = (bf16[256,512]{1,0:T(8,128)(2,1)}, f32[256,512]{1,0:T(8,128)S(1)}, f32[1,512]{1,0:T(1,128)}) custom-call(s32[2]{0:T(128)S(1)} %pad_add_fusion.refs_0_, bf16[256,512]{1,0:T(8,128)(2,1)S(1)} %copy-done.2, bf16[256,512]{1,0:T(8,128)(2,1)S(1)} %copy-done.8, bf16[256,512]{1,0:T(8,128)(2,1)S(1)} %bitcast.13, ...), custom_call_target="tpu_custom_call" | custom-call | flops 2000000000 | bytes 2164744 | tf_op jit(solution)/shard_map/kernel_three_back/pallas_call | solution.py:159
  106.0 4.8 %all-to-all-done.6.refs_1_ = bf16[32,8,512]{2,1,0:T(8,128)(2,1)S(1)} async-done(((bf16[32,8,512]{2,1,0:T(8,128)(2,1)}), bf16[32,8,512]{2,1,0:T(8,128)(2,1)S(1)}, u32[]{:S(2)}, u32[]{:S(2)}) %all-to-all-start.6) | async-done | bytes 262176 | tf_op jit(solution)/shard_map/all_to_all | solution.py:41
  110.9 1.4 %finish.1 = (bf16[256,512]{1,0:T(8,128)(2,1)}, bf16[256,512]{1,0:T(8,128)(2,1)}) custom-call(s32[2]{0:T(128)S(1)} %pad_add_fusion.refs_0_, bf16[32,8,512]{2,1,0:T(8,128)(2,1)S(1)} %all-to-all-done.6.refs_1_, f32[256,256]{1,0:T(8,128)S(1)} %copy-done.11, f32[256,256]{1,0:T(8,128)S(1)} %collective-permute-done.5.refs_3_, ...), custom_call_target="tpu_custom_call" | custom-call | flops 1000000 | bytes 1835016 | tf_op jit(solution)/shard_map/finish/pallas_call | solution.py:159
  (65 shorter events, 10.3 us)
Async XLA Ops:
  0.6 11.8 %collective-permute-start.2 = (bf16[256,512]{1,0:T(8,128)(2,1)}, bf16[256,512]{1,0:T(8,128)(2,1)S(1)}, u32[]{:S(2)}, u32[]{:S(2)}) collective-permute-start(bf16[256,512]{1,0:T(8,128)(2,1)} %refs_1_.7), channel_id=1, source_target_pairs={{0,8},{8,0},{16,24},{24,16},{32,40},{40,32},{48,56},{56,48},{64,72... | collective-permute-start | bytes 786440 | tf_op jit(solution)/shard_map/ppermute | solution.py:583
  4.0 8.5 %collective-permute-start.3 = (bf16[256,512]{1,0:T(8,128)(2,1)}, bf16[256,512]{1,0:T(8,128)(2,1)S(1)}, u32[]{:S(2)}, u32[]{:S(2)}) collective-permute-start(bf16[256,512]{1,0:T(8,128)(2,1)} %refs_2_.5), channel_id=1, source_target_pairs={{0,8},{8,0},{16,24},{24,16},{32,40},{40,32},{48,56},{56,48},{64,72... | collective-permute-start | bytes 786440 | tf_op jit(solution)/shard_map/ppermute | solution.py:583
  6.0 14.8 %all-to-all-start = ((bf16[32,8,512]{2,1,0:T(8,128)(2,1)}), bf16[32,8,512]{2,1,0:T(8,128)(2,1)S(1)}, u32[]{:S(2)}, u32[]{:S(2)}) async-start(bf16[32,8,512]{2,1,0:T(8,128)(2,1)} %landmark_means.1.refs_5_), calls=%async_computation | async-start | bytes 524288 | tf_op jit(solution)/shard_map/all_to_all | solution.py:41
  11.7 26.1 %collective-permute-start = (bf16[256,512]{1,0:T(8,128)(2,1)}, bf16[256,512]{1,0:T(8,128)(2,1)S(1)}, u32[]{:S(2)}, u32[]{:S(2)}) collective-permute-start(bf16[256,512]{1,0:T(8,128)(2,1)} %refs_1_.6), channel_id=1, source_target_pairs={{0,8},{8,0},{16,24},{24,16},{32,40},{40,32},{48,56},{56,48},{64,72... | collective-permute-start | bytes 786440 | tf_op jit(solution)/shard_map/ppermute | solution.py:583
  12.1 25.8 %collective-permute-start.1 = (bf16[256,512]{1,0:T(8,128)(2,1)}, bf16[256,512]{1,0:T(8,128)(2,1)S(1)}, u32[]{:S(2)}, u32[]{:S(2)}) collective-permute-start(bf16[256,512]{1,0:T(8,128)(2,1)} %refs_2_.4), channel_id=1, source_target_pairs={{0,8},{8,0},{16,24},{24,16},{32,40},{40,32},{48,56},{56,48},{64,72... | collective-permute-start | bytes 786440 | tf_op jit(solution)/shard_map/ppermute | solution.py:583
  22.4 10.4 %all-to-all-start.1 = ((bf16[16,40,128]{2,1,0:T(8,128)(2,1)}), bf16[16,40,128]{2,1,0:T(8,128)(2,1)S(1)}, u32[]{:S(2)}, u32[]{:S(2)}) async-start(bf16[16,40,128]{2,1,0:T(8,128)(2,1)} %local_context.1.refs_2_), calls=%async_computation.1 | async-start | bytes 327680 | tf_op jit(solution)/shard_map/all_to_all | solution.py:41
  25.9 12.0 %copy-start.3 = (bf16[256,512]{1,0:T(8,128)(2,1)S(1)}, bf16[256,512]{1,0:T(8,128)(2,1)}, u32[]{:S(2)}) copy-start(bf16[256,512]{1,0:T(8,128)(2,1)} %refs_1_.6) | copy-start | bytes 786436
  25.9 12.0 %copy-start.9 = (bf16[256,512]{1,0:T(8,128)(2,1)S(1)}, bf16[256,512]{1,0:T(8,128)(2,1)}, u32[]{:S(2)}) copy-start(bf16[256,512]{1,0:T(8,128)(2,1)} %refs_2_.4) | copy-start | bytes 786436
  29.1 1.3 %copy-start.23 = (f32[7,256,256]{2,1,0:T(8,128)}, f32[7,256,256]{2,1,0:T(8,128)S(1)}, u32[]{:S(2)}) copy-start(f32[7,256,256]{2,1,0:T(8,128)S(1)} %get-tuple-element.50.refs_1_) | copy-start | bytes 5505028
  30.3 3.4 %copy-start.12 = (f32[256,256]{1,0:T(8,128)}, f32[256,256]{1,0:T(8,128)S(1)}, u32[]{:S(2)}) copy-start(f32[256,256]{1,0:T(8,128)S(1)} %get-tuple-element.45.refs_1_) | copy-start | bytes 786436
  33.7 11.0 %all-to-all-start.2 = ((bf16[16,16,256]{2,1,0:T(8,128)(2,1)}), bf16[16,16,256]{2,1,0:T(8,128)(2,1)S(1)}, u32[]{:S(2)}, u32[]{:S(2)}) async-start(bf16[16,16,256]{2,1,0:T(8,128)(2,1)} %get-tuple-element.36.refs_5_.refs_3_), calls=%async_computation.2 | async-start | bytes 262144 | tf_op jit(solution)/shard_map/all_to_all | solution.py:41
  38.5 1.0 copy-start.21
  38.6 6.2 %copy-start.18 = (f32[512]{0:T(512)S(1)}, f32[512]{0:T(512)}, u32[]{:S(2)}) copy-start(f32[512]{0:T(512)} %param.8) | copy-start | bytes 6148
  46.4 17.6 %all-to-all-start.3 = ((f32[16,2,512]{2,1,0:T(2,128)}), f32[16,2,512]{2,1,0:T(2,128)S(1)}, u32[]{:S(2)}, u32[]{:S(2)}) async-start(f32[16,2,512]{2,1,0:T(2,128)} %get-tuple-element.40), calls=%async_computation.3 | async-start | bytes 131072 | tf_op jit(solution)/shard_map/all_to_all | solution.py:41
  56.8 46.3 %collective-permute-start.6 = (bf16[256,512]{1,0:T(8,128)(2,1)S(1)}, bf16[256,512]{1,0:T(8,128)(2,1)}, u32[]{:S(2)}, u32[]{:S(2)}) collective-permute-start(bf16[256,512]{1,0:T(8,128)(2,1)S(1)} %bitcast.10), channel_id=1, source_target_pairs={{0,8},{8,0},{16,24},{24,16},{32,40},{40,32},{48,56},{56,48},{64,72... | collective-permute-start | bytes 786440 | tf_op jit(solution)/shard_map/ppermute | solution.py:605
  64.0 1.0 copy-start.6
  66.9 10.4 %all-to-all-start.4 = ((bf16[16,40,128]{2,1,0:T(8,128)(2,1)}), bf16[16,40,128]{2,1,0:T(8,128)(2,1)S(1)}, u32[]{:S(2)}, u32[]{:S(2)}) async-start(bf16[16,40,128]{2,1,0:T(8,128)(2,1)} %norm.1.refs_8_), calls=%async_computation.4 | async-start | bytes 327680 | tf_op jit(solution)/shard_map/all_to_all | solution.py:41
  70.4 1.0 copy-start.22
  71.4 5.9 %copy-start.13 = (f32[256,256]{1,0:T(8,128)S(1)}, f32[256,256]{1,0:T(8,128)}, u32[]{:S(2)}) copy-start(f32[256,256]{1,0:T(8,128)} %copy-done.12) | copy-start | bytes 786436
  76.5 7.6 %copy-start.14 = (f32[256,256]{1,0:T(8,128)}, f32[256,256]{1,0:T(8,128)S(1)}, u32[]{:S(2)}) copy-start(f32[256,256]{1,0:T(8,128)S(1)} %get-tuple-element.47.refs_3_.refs_5_) | copy-start | bytes 786436
  78.3 12.6 %all-to-all-start.5 = ((bf16[16,40,128]{2,1,0:T(8,128)(2,1)}), bf16[16,40,128]{2,1,0:T(8,128)(2,1)S(1)}, u32[]{:S(2)}, u32[]{:S(2)}) async-start(bf16[16,40,128]{2,1,0:T(8,128)(2,1)} %get-tuple-element.48.refs_6_), calls=%async_computation.5 | async-start | bytes 327680 | tf_op jit(solution)/shard_map/all_to_all | solution.py:41
  85.0 1.5 %copy-start.24 = (f32[7,256,256]{2,1,0:T(8,128)S(1)}, f32[7,256,256]{2,1,0:T(8,128)}, u32[]{:S(2)}) copy-start(f32[7,256,256]{2,1,0:T(8,128)} %copy-done.23) | copy-start | bytes 5505028
  90.8 4.5 %copy-start.20 = (f32[256,256]{1,0:T(8,128)S(1)}, f32[256,256]{1,0:T(8,128)}, u32[]{:S(2)}) copy-start(f32[256,256]{1,0:T(8,128)} %copy-done.19) | copy-start | bytes 786436
  90.8 11.1 %copy-start.17 = (bf16[256,256]{1,0:T(8,128)(2,1)S(1)}, bf16[256,256]{1,0:T(8,128)(2,1)}, u32[]{:S(2)}) copy-start(bf16[256,256]{1,0:T(8,128)(2,1)} %copy-done.16) | copy-start | bytes 393220
  90.8 12.4 %copy-start.2 = (bf16[256,512]{1,0:T(8,128)(2,1)S(1)}, bf16[256,512]{1,0:T(8,128)(2,1)}, u32[]{:S(2)}) copy-start(bf16[256,512]{1,0:T(8,128)(2,1)} %refs_1_.7) | copy-start | bytes 786436
  90.8 12.4 %copy-start.8 = (bf16[256,512]{1,0:T(8,128)(2,1)S(1)}, bf16[256,512]{1,0:T(8,128)(2,1)}, u32[]{:S(2)}) copy-start(bf16[256,512]{1,0:T(8,128)(2,1)} %refs_2_.5) | copy-start | bytes 786436
  92.3 10.9 %collective-permute-start.7 = (bf16[16,40,128]{2,1,0:T(8,128)(2,1)}, bf16[16,40,128]{2,1,0:T(8,128)(2,1)S(1)}, u32[]{:S(2)}, u32[]{:S(2)}) collective-permute-start(bf16[16,40,128]{2,1,0:T(8,128)(2,1)} %get-tuple-element.55.refs_5_), channel_id=1, source_target_pairs={{0,8},{8,0},{16,24},{24,16},{32,40},{40,32},{48,56},{56,48},{64,72... | collective-permute-start | bytes 491528 | tf_op jit(solution)/shard_map/ppermute | solution.py:647
  95.1 6.8 %collective-permute-start.4 = (bf16[256,256]{1,0:T(8,128)(2,1)}, bf16[256,256]{1,0:T(8,128)(2,1)S(1)}, u32[]{:S(2)}, u32[]{:S(2)}) collective-permute-start(bf16[256,256]{1,0:T(8,128)(2,1)} %get-tuple-element.44), channel_id=1, source_target_pairs={{0,8},{8,0},{16,24},{24,16},{32,40},{40,32},{48,56},{56,48},{64,72... | collective-permute-start | bytes 393224 | tf_op jit(solution)/shard_map/ppermute | solution.py:645
  95.2 10.8 %collective-permute-start.5 = (f32[256,256]{1,0:T(8,128)S(1)}, f32[256,256]{1,0:T(8,128)S(1)}, u32[]{:S(2)}, u32[]{:S(2)}) collective-permute-start(f32[256,256]{1,0:T(8,128)S(1)} %copy-done.20), channel_id=1, source_target_pairs={{0,8},{8,0},{16,24},{24,16},{32,40},{40,32},{48,56},{56,48},{64,72... | collective-permute-start | bytes 786440 | tf_op jit(solution)/shard_map/ppermute | solution.py:646
  95.6 15.2 %all-to-all-start.6 = ((bf16[32,8,512]{2,1,0:T(8,128)(2,1)}), bf16[32,8,512]{2,1,0:T(8,128)(2,1)S(1)}, u32[]{:S(2)}, u32[]{:S(2)}) async-start(bf16[32,8,512]{2,1,0:T(8,128)(2,1)} %bitcast.5), calls=%async_computation.6 | async-start | bytes 524288 | tf_op jit(solution)/shard_map/all_to_all | solution.py:41
  103.2 7.7 %copy-start.4 = (bf16[256,512]{1,0:T(8,128)(2,1)S(1)}, bf16[256,512]{1,0:T(8,128)(2,1)}, u32[]{:S(2)}) copy-start(bf16[256,512]{1,0:T(8,128)(2,1)} %gather.1.refs_5_) | copy-start | bytes 786436
  103.2 7.7 %copy-start.11 = (f32[256,256]{1,0:T(8,128)S(1)}, f32[256,256]{1,0:T(8,128)}, u32[]{:S(2)}) copy-start(f32[256,256]{1,0:T(8,128)} %copy-done.10) | copy-start | bytes 786436
  (8 other events, 6.7 us)

commit v4 on v3

--- a/solution.py
+++ b/solution.py
@@ -281,18 +281,17 @@
 
 
 def ahead_body(
-    q_ref, k_ref, land_ref, first_ref, again_ref, exp_ref
+    q_ref, k_ref, land_ref, kone_ref, exp_ref
 ):
-    heads, tok, _ = first_ref.shape
+    heads, tok, _ = kone_ref.shape
     for h in range(heads):
         kone = kernel_one(q_ref, land_ref, h).astype(BF16)
-        first_ref[h] = kone
-        again_ref[h] = kone
+        kone_ref[h] = kone
         keys = k_ref[:, head_cols(h)]
         score = dot(keys, land_ref[:, head_cols(h)], NT) * SCALE
-        shift = jnp.max(score, axis=0, keepdims=True)
-        exp_ref[h, :tok] = jnp.exp(score - shift)
-        exp_ref[h, tok:] = rows_of(shift)
+        shift = jnp.max(score, axis=0, keepdims=True).astype(BF16).astype(F32)
+        exp_ref[h, :tok] = jnp.exp(score - shift).astype(BF16)
+        exp_ref[h, tok:] = jnp.broadcast_to(shift, (16, M)).astype(BF16)
 
 
 def output_body(ids_ref, kone_ref, mix_ref, g_ref, gain_ref, out_ref, sum_ref):
@@ -362,25 +361,25 @@
 
 def query_body(
     ids_ref, sum_ref, out_ref, g_ref, gain_ref, mix_ref, q_ref, land_ref,
-    norm_mine, norm_other, query_mine, query_other, keyland_ref,
+    mine_ref, other_ref, keyland_ref,
 ):
     heads = mix_ref.shape[0]
-    tok = norm_mine.shape[0]
+    tok = mine_ref.shape[1]
     factors = token_factors(ids_ref, sum_ref, heads * DH * sum_ref.shape[0])
     for h in range(heads):
         out = out_ref[:, head_cols(h)]
         grad = g_ref[:, head_cols(h)].astype(F32)
         gain = gain_ref[:, own_head(ids_ref, h)]
         normed = (out * factors[0] * gain).astype(BF16)
-        norm_mine[:, head_cols(h)] = normed[:tok]
-        norm_other[:, head_cols(h)] = normed[tok:]
+        mine_ref[0, :, head_cols(h)] = normed[:tok]
+        other_ref[0, :, head_cols(h)] = normed[tok:]
         kone = kernel_one(q_ref, land_ref, h)
         g_kernel = dot(output_grad(factors, out, grad, gain), mix_ref[h])
         inner = jnp.sum(kone * g_kernel, axis=1, keepdims=True)
         g_score = (kone * (g_kernel - inner)).astype(BF16)
         query = dot(g_score, land_ref[:, head_cols(heads + h)]) * SCALE
-        query_mine[:, head_cols(h)] = query[:tok]
-        query_other[:, head_cols(h)] = query[tok:]
+        mine_ref[1, :, head_cols(h)] = query[:tok].astype(BF16)
+        other_ref[1, :, head_cols(h)] = query[tok:].astype(BF16)
         queries = q_ref[:, head_cols(h)]
         keyland_ref[:, head_cols(h)] = dot(g_score, queries, TN) * SCALE
 
@@ -445,11 +444,11 @@
     )
 
 
-def unpacked(got_ref, h, heads):
-    count, rows, _ = got_ref.shape
+def unpacked(got, h, heads):
+    count, rows, _ = got.shape
     per_head = count // heads
     cols = (rows - 8) // 2
-    parts = [got_ref[h * per_head + j] for j in range(per_head)]
+    parts = [got[h * per_head + j] for j in range(per_head)]
     g_weighted = jnp.concatenate(
         [
             jnp.concatenate([part[:cols], part[cols : 2 * cols]], axis=1)
@@ -465,7 +464,9 @@
     return g_weighted, g_totals, top, gain
 
 
-def queryland_body(got_ref, exp_ref, k_ref, v_ref, extra_ref, out_ref, again_ref):
+def queryland_body(
+    got_ref, exp_ref, k_ref, v_ref, extra_ref, land_ref, out_ref, pass_ref
+):
     heads = exp_ref.shape[0]
     half = heads * DH
     for h in range(heads):
@@ -473,26 +474,43 @@
         keys = k_ref[:, head_cols(h)]
         vals = v_ref[:, head_cols(h)]
         tok = keys.shape[0]
-        exp_three = exp_ref[h, :tok] * jnp.exp(exp_ref[h, tok : tok + 1] - top)
+        shift = exp_ref[h, tok:].astype(F32)[0:1]
+        exp_three = exp_ref[h, :tok].astype(F32) * jnp.exp(shift - top)
         g_score = (exp_three * (dot(vals, g_weighted) + g_totals)).astype(BF16)
         queryland = dot(g_score, keys, TN) * SCALE
         out_ref[:, head_cols(h)] = (queryland + extra_ref[:, head_cols(h)]).astype(BF16)
     out_ref[:, half:] = extra_ref[:, half:].astype(BF16)
-    again_ref[...] = got_ref[...]
+    count, rows, _ = got_ref.shape
+    for place in range(count):
+        pass_ref[place * rows : (place + 1) * rows] = got_ref[place]
+    for h in range(heads):
+        at = count * rows + h * M
+        pass_ref[at : at + M] = land_ref[:, head_cols(h)]
+
+
+class Parts:
+    def __init__(self, ref, count, rows):
+        self.ref, self.shape = ref, (count, rows, ref.shape[1])
+
+    def __getitem__(self, place):
+        rows = self.shape[1]
+        return self.ref[place * rows : (place + 1) * rows]
 
 
 def value_body(
-    ids_ref, k_ref, v_ref, land_ref, land_there, got_ref, got_there,
-    value_out, key_out, gain_out,
+    count, ids_ref, k_ref, v_ref, pass_ref, pass_there, value_out, key_out, gain_out
 ):
-    heads = land_ref.shape[1] // (2 * DH)
+    heads = k_ref.shape[1] // (2 * DH)
+    total = pass_ref.shape[0] - heads * M
 
     def place_halves(core, own, away):
-        for place, land, got in ((own, land_ref, got_ref), (away, land_there, got_there)):
+        for place, ref in ((own, pass_ref), (away, pass_there)):
             for h in range(heads):
                 cols = slice(place.start + h * DH, place.start + (h + 1) * DH)
-                g_weighted, g_totals, top, gain = unpacked(got, h, heads)
-                lq = land[:, head_cols(h)]
+                g_weighted, g_totals, top, gain = unpacked(
+                    Parts(ref, count, total // count), h, heads
+                )
+                lq = ref[total + h * M : total + (h + 1) * M]
                 exp_three = jnp.exp(dot(k_ref[:, cols], lq, NT) * SCALE - top)
                 g_exp = dot(v_ref[:, cols], g_weighted) + g_totals
                 value_out[:, cols] = dot(exp_three.astype(BF16), g_weighted, NT).astype(BF16)
@@ -515,19 +533,19 @@
         place_halves(1, right, left)
 
 
-def gather_body(ids_ref, norm_mine, norm_there, norm_out):
+def gather_body(ids_ref, mine_ref, there_ref, norm_out):
     def place_halves(core, own, away):
-        norm_out[:, own] = norm_mine[...]
-        norm_out[:, away] = norm_there[...]
+        norm_out[:, own] = mine_ref[0]
+        norm_out[:, away] = there_ref[0]
 
     by_core(ids_ref, place_halves)
 
 
 def finish_body(
-    ids_ref, got_ref, query_mine, query_there, key_ref, query_out, key_out
+    ids_ref, got_ref, mine_ref, there_ref, key_ref, query_out, key_out
 ):
     count, land_dev, both = got_ref.shape
-    tok, half = query_mine.shape
+    _, tok, half = mine_ref.shape
     seg_len = tok // land_dev
     lands = []
     for core in range(2):
@@ -539,10 +557,12 @@
 
     def place_halves(core, own, away):
         for place, land, ref in (
-            (own, lands[core], query_mine), (away, lands[1 - core], query_there)
+            (own, lands[core], mine_ref), (away, lands[1 - core], there_ref)
         ):
             for row, span in spans:
-                query_out[span, place] = (ref[span] + land[row : row + 1, :half]).astype(BF16)
+                query_out[span, place] = (
+                    ref[1, span].astype(F32) + land[row : row + 1, :half]
+                ).astype(BF16)
 
     by_core(ids_ref, place_halves)
     for core in range(2):
@@ -573,19 +593,17 @@
     ]
     swap = [(i, i ^ 1) for i in range(n_ctx)]
     packed = shape(chips, 2 * cols + 8, DH, dtype=BF16)
-    block = shape(tok, half)
-    block_b = shape(tok, half, dtype=BF16)
+    pair = shape(2, tok, half, dtype=BF16)
     wide_b = shape(tok, width, dtype=BF16)
     units = shape(heads, 2 * tok, M, dtype=BF16)
 
     both_b = shape(2 * tok, half, dtype=BF16)
-    k_there, v_there, q_there, g_there = [
-        lax.ppermute(x, "ctx", swap) for x in (keys_in, values, queries, out_grad)
-    ]
     (own,) = call(
         means_body, [shape(n_ctx, land_dev, 2 * half, dtype=BF16)], queries, keys_in,
         far_in=(0, 1), far_out=(0,), vmem=MOST_VMEM, flops=10**6, name="landmark_means",
     )
+    held = lax.optimization_barrier((own, keys_in, values, queries, out_grad))
+    k_there, v_there, q_there, g_there = [lax.ppermute(x, "ctx", swap) for x in held[1:]]
     land = exchange(own, "ctx").reshape(M, 2 * half)
     keys, vals = call(
         stack_body, [both_b, both_b], ids, keys_in, values, k_there, v_there,
@@ -602,14 +620,13 @@
         mixing_body, [shape(chips, cols, M, dtype=BF16), shape(cols + 8, M)],
         got, inverse, flops=10**8, name="mixing",
     )
-    land_there = lax.ppermute(land, "ctx", swap)
     qs, grads = call(
         stack_body, [both_b, both_b], ids, queries, out_grad, q_there, g_there,
         scalars=1, after=(parts,), flops=10**6, name="stack_qg",
     )
-    kone, kone_again, exp_local = call(
-        ahead_body, [units, units, shape(heads, 2 * tok + 8, M)], qs, keys, land,
-        far_out=(2,), after=(parts,), flops=2 * 10**9, name="ahead",
+    kone, exp_local = call(
+        ahead_body, [units, shape(heads, 2 * tok + 16, M, dtype=BF16)], qs, keys, land,
+        after=(parts,), flops=2 * 10**9, name="ahead",
     )
     mixing = exchange(parts, "ctx", same_core).reshape(heads, DH, M)
 
@@ -619,43 +636,43 @@
     )
     sums = exchange(sums, ("ctx", "head"), same_chip)
     (parts,) = call(
-        norm_body, [packed], ids, sums, output, grads, gain, kone_again,
+        norm_body, [packed], ids, sums, output, grads, gain, kone,
         scalars=1, flops=10**8, name="norm",
     )
     got = exchange(parts, "ctx", same_core)
-    norm_mine, norm_other, query_mine, query_other, keyland = call(
-        query_body, [block_b, block_b, block, block, shape(M, half)],
+    mine, other, keyland = call(
+        query_body, [pair, pair, shape(M, half)],
         ids, sums, output, grads, gain, mixing, qs, land,
         scalars=1, after=(parts,), flops=2 * 10**9, name="kernel_one_back",
     )
     parts, g_mixing = call(
         grad_context_body, [packed, shape(cols, M)], got, inverse_again, kept,
-        after=(keyland,), flops=10**8, name="context_back",
+        after=(other,), flops=10**8, name="context_back",
     )
     got = exchange(parts, "ctx", same_core)
     (extra,) = call(
         inverse_back_body, [shape(M, 2 * half)], ids, chain, kept, g_mixing, land, keyland,
         scalars=1, after=(parts,), flops=5 * 10**9, name="inverse_back",
     )
-    both, got = call(
-        queryland_body, [shape(M, 2 * half, dtype=BF16), packed],
-        got, exp_local, keys, vals, extra, far_in=(1,), flops=10**8, name="landmarks_back",
+    both, passed = call(
+        queryland_body,
+        [shape(M, 2 * half, dtype=BF16), shape(chips * (2 * cols + 8) + heads * M, DH, dtype=BF16)],
+        got, exp_local, keys, vals, extra, land, flops=10**8, name="landmarks_back",
     )
     landed = exchange(both.reshape(n_ctx, land_dev, 2 * half), "ctx")
-    norm_there = lax.ppermute(norm_other, "ctx", swap)
-    query_there = lax.ppermute(query_other, "ctx", swap)
-    got_there = lax.ppermute(got, "ctx", swap)
+    there = lax.ppermute(other, "ctx", swap)
+    passed_there = lax.ppermute(passed, "ctx", swap)
     (normed,) = call(
-        gather_body, [wide_b], ids, norm_mine, norm_there,
+        gather_body, [wide_b], ids, mine, there,
         scalars=1, after=(both,), flops=10**6, name="gather",
     )
     value_grad, key_three, gain_grad = call(
-        value_body, [wide_b, shape(tok, width), shape(1, width)],
-        ids, keys_in, values, land, land_there, got, got_there,
+        functools.partial(value_body, chips), [wide_b, shape(tok, width), shape(1, width)],
+        ids, keys_in, values, passed, passed_there,
         scalars=1, after=(both,), flops=2 * 10**9, name="kernel_three_back",
     )
     query_grad, key_grad = call(
-        finish_body, [wide_b, wide_b], ids, landed, query_mine, query_there, key_three,
+        finish_body, [wide_b, wide_b], ids, landed, mine, there, key_three,
         scalars=1, after=(normed,), flops=10**6, name="finish",
     )
     return (normed, query_grad, key_grad, value_grad, gain_grad.reshape(width))

time: 113 us -> 109 us (0.965)
  blocking collectives: 0 us -> 17.4 us
  starting transfers between devices: 46.9 us -> 34.3 us
  waiting for transfers between devices: 24.4 us -> 20.4 us
  local copies, waits for them, and re-layouts: 11.5 us -> 8.22 us
  Pallas kernels: 28.5 us -> 27.2 us
    all_to_all x0 -> x1, blocking collectives: none -> 17.4 us  [exchange(): return lax.all_to_all(parts, axis, 0, 0, axis_index_groups=groups)]
    all_to_all x7 -> x6, starting transfers between devices: 39.3 us -> 27.3 us  [exchange(): return lax.all_to_all(parts, axis, 0, 0, axis_index_groups=groups)]
    all_to_all x7 -> x6, waiting for transfers between devices: 24.4 us -> 20.4 us  [exchange(): return lax.all_to_all(parts, axis, 0, 0, axis_index_groups=groups)]
    unnamed x50 -> x30, local copies, waits for them, and re-layouts: 11.5 us -> 8.22 us
    pallas_call x16, Pallas kernels: 28.5 us -> 27.2 us  [call(): pl.pallas_call(whole, out_shape=outs, in_specs=in_specs, out_specs=[space...]
    ppermute x4 -> x2, starting transfers between devices: 3.53 us -> 2.93 us  [the longest x1 2.93 us: on_device(): passed_there = lax.ppermute(passed, 'ctx', swap)]
  transfers between devices with their start and end apart: 15 -> 12, of which waited for: 6 -> 6; matrix products, arithmetic and copies ran while one was open for 0% -> 0% of each run, Pallas kernels for 23% -> 17%
where the time goes in v4:
time: 109 us; the launch traced here: 108 us
  starting transfers between devices  34.3 us (31%)
  Pallas kernels  27.2 us (25%)
  waiting for transfers between devices  20.4 us (19%)
  blocking collectives  17.4 us (16%)
  local copies, waits for them, and re-layouts  8.22 us (8%)
    all_to_all x6, starting transfers between devices, exchange(): return lax.all_to_all(parts, axis, 0, 0, axis_index_groups=groups)  27.3 us
    pallas_call x16, Pallas kernels, call(): pl.pallas_call(whole, out_shape=outs, in_specs=in_specs, out_specs=[space...  27.2 us
    all_to_all x6, waiting for transfers between devices, exchange(): return lax.all_to_all(parts, axis, 0, 0, axis_index_groups=groups)  20.4 us
    all_to_all x1, blocking collectives, exchange(): return lax.all_to_all(parts, axis, 0, 0, axis_index_groups=groups)  17.4 us
    unnamed x30, local copies, waits for them, and re-layouts  8.22 us
    ppermute x4, starting transfers between devices, on_device(): lax.ppermute(x, 'ctx', swap)  4.03 us
    ppermute x1, starting transfers between devices, on_device(): passed_there = lax.ppermute(passed, 'ctx', swap)  2.93 us
  transfers between devices with their start and end apart: 12, of which 6 were waited for; matrix products, arithmetic and copies ran while one was open for 0% of the time, Pallas kernels for 17%

profile of v4, /device:TPU:1, one launch (start us, length us, event | category | flops | bytes accessed | tf_op | source)
XLA Modules:
  0.0 108.5 jit_solution(17320260410323550794)
XLA Ops:
  0.6 1.9 %landmark_means.1.refs_5_ = bf16[32,8,512]{2,1,0:T(8,128)(2,1)} custom-call(bf16[256,512]{1,0:T(8,128)(2,1)} %refs_1_.6, bf16[256,512]{1,0:T(8,128)(2,1)} %refs_1_.7), custom_call_target="tpu_custom_call" | custom-call | flops 1000000 | bytes 786432 | tf_op jit(solution)/shard_map/landmark_means/pallas_call | solution.py:159
  2.5 3.3 %collective-permute-start.2 = (bf16[256,512]{1,0:T(8,128)(2,1)}, bf16[256,512]{1,0:T(8,128)(2,1)S(1)}, u32[]{:S(2)}, u32[]{:S(2)}) collective-permute-start(bf16[256,512]{1,0:T(8,128)(2,1)} %refs_1_.7), channel_id=1, source_target_pairs={{0,8},{8,0},{16,24},{24,16},{32,40},{40,32},{48,56},{56,48},{64,72... | collective-permute-start | bytes 786440 | tf_op jit(solution)/shard_map/ppermute | solution.py:606
  6.0 5.8 %all-to-all-start = ((bf16[32,8,512]{2,1,0:T(8,128)(2,1)}), bf16[32,8,512]{2,1,0:T(8,128)(2,1)S(1)}, u32[]{:S(2)}, u32[]{:S(2)}) async-start(bf16[32,8,512]{2,1,0:T(8,128)(2,1)} %landmark_means.1.refs_5_), calls=%async_computation | async-start | bytes 524288 | tf_op jit(solution)/shard_map/all_to_all | solution.py:41
  12.4 0.9 copy-done
  13.4 0.9 copy-done.1
  14.3 0.9 copy-done.5
  15.9 4.8 %all-to-all-done = bf16[32,8,512]{2,1,0:T(8,128)(2,1)S(1)} async-done(((bf16[32,8,512]{2,1,0:T(8,128)(2,1)}), bf16[32,8,512]{2,1,0:T(8,128)(2,1)S(1)}, u32[]{:S(2)}, u32[]{:S(2)}) %all-to-all-start) | async-done | bytes 262176 | tf_op jit(solution)/shard_map/all_to_all | solution.py:41
  20.7 1.6 %local_context.1.refs_2_ = bf16[16,40,128]{2,1,0:T(8,128)(2,1)} custom-call(bf16[256,512]{1,0:T(8,128)(2,1)S(1)} %bitcast.7, bf16[512,256]{1,0:T(8,128)(2,1)S(1)} %get-tuple-element.38.refs_1_.refs_2_, bf16[512,256]{1,0:T(8,128)(2,1)S(1)} %get-tuple-element.39.refs_2_.refs_3_), custom_call_target="tpu_custom_call" | custom-call | flops 100000000 | bytes 950272 | tf_op jit(solution)/shard_map/local_context/pallas_call | solution.py:159
  22.4 3.5 %all-to-all-start.1 = ((bf16[16,40,128]{2,1,0:T(8,128)(2,1)}), bf16[16,40,128]{2,1,0:T(8,128)(2,1)S(1)}, u32[]{:S(2)}, u32[]{:S(2)}) async-start(bf16[16,40,128]{2,1,0:T(8,128)(2,1)} %local_context.1.refs_2_), calls=%async_computation.1 | async-start | bytes 327680 | tf_op jit(solution)/shard_map/all_to_all | solution.py:41
  25.9 3.1 %inverse.1 = (f32[256,256]{1,0:T(8,128)S(1)}, f32[256,256]{1,0:T(8,128)S(1)}, f32[7,256,256]{2,1,0:T(8,128)S(1)}) custom-call(s32[2]{0:T(128)S(1)} %pad_add_fusion.refs_0_, bf16[256,512]{1,0:T(8,128)(2,1)S(1)} %bitcast.8, bf16[16,40,128]{2,1,0:T(8,128)(2,1)} %local_context.1.refs_2_), custom_call_target="tpu_custom_call" | custom-call | flops 3000000000 | bytes 2621448 | tf_op jit(solution)/shard_map/inverse/pallas_call | solution.py:159
  29.1 1.2 %copy-done.11 = f32[7,256,256]{2,1,0:T(8,128)} copy-done((f32[7,256,256]{2,1,0:T(8,128)}, f32[7,256,256]{2,1,0:T(8,128)S(1)}, u32[]{:S(2)}) %copy-start.11) | copy-done | bytes 1835032
  30.3 2.5 %all-to-all-done.1.refs_0_ = bf16[16,40,128]{2,1,0:T(8,128)(2,1)S(1)} async-done(((bf16[16,40,128]{2,1,0:T(8,128)(2,1)}), bf16[16,40,128]{2,1,0:T(8,128)(2,1)S(1)}, u32[]{:S(2)}, u32[]{:S(2)}) %all-to-all-start.1) | async-done | bytes 163872 | tf_op jit(solution)/shard_map/all_to_all | solution.py:41
  33.7 4.1 %all-to-all-start.2 = ((bf16[16,16,256]{2,1,0:T(8,128)(2,1)}), bf16[16,16,256]{2,1,0:T(8,128)(2,1)S(1)}, u32[]{:S(2)}, u32[]{:S(2)}) async-start(bf16[16,16,256]{2,1,0:T(8,128)(2,1)} %get-tuple-element.41.refs_5_.refs_3_), calls=%async_computation.2 | async-start | bytes 262144 | tf_op jit(solution)/shard_map/all_to_all | solution.py:41
  39.4 5.2 %all-to-all-done.2 = bf16[16,16,256]{2,1,0:T(8,128)(2,1)S(1)} async-done(((bf16[16,16,256]{2,1,0:T(8,128)(2,1)}), bf16[16,16,256]{2,1,0:T(8,128)(2,1)S(1)}, u32[]{:S(2)}, u32[]{:S(2)}) %all-to-all-start.2) | async-done | bytes 131104 | tf_op jit(solution)/shard_map/all_to_all | solution.py:41
  44.7 1.0 output.1
  45.7 17.4 %all_to_all.35.refs_1_ = f32[16,2,512]{2,1,0:T(2,128)S(1)} all-to-all(f32[16,2,512]{2,1,0:T(2,128)S(1)} %get-tuple-element.45), channel_id=1, replica_groups={{0,1,2,3,4,5,6,7,8,9,10,11,12,13,14,15},{16,17,18,19,20,21,22,23,24,25,..., dimensions={0} | all-to-all | bytes 131072 | tf_op jit(solution)/shard_map/all_to_all | solution.py:41
  63.2 1.9 %norm.1.refs_8_ = bf16[16,40,128]{2,1,0:T(8,128)(2,1)} custom-call(s32[2]{0:T(128)S(1)} %pad_add_fusion.refs_0_, f32[16,2,512]{2,1,0:T(2,128)S(1)} %all_to_all.35.refs_1_, f32[512,256]{1,0:T(8,128)S(1)} %get-tuple-element.46.refs_2_, bf16[512,256]{1,0:T(8,128)(2,1)S(1)} %get-tuple-element.44.refs_3_, f32[1,512]{1,0:T(1,128)S(1)} %bitcast.16, ...), custom_call_target="tpu_custom_call" | custom-call | flops 100000000 | bytes 1542152 | tf_op jit(solution)/shard_map/norm/pallas_call | solution.py:159
  65.0 3.5 %all-to-all-start.4 = ((bf16[16,40,128]{2,1,0:T(8,128)(2,1)}), bf16[16,40,128]{2,1,0:T(8,128)(2,1)S(1)}, u32[]{:S(2)}, u32[]{:S(2)}) async-start(bf16[16,40,128]{2,1,0:T(8,128)(2,1)} %norm.1.refs_8_), calls=%async_computation.4 | async-start | bytes 327680 | tf_op jit(solution)/shard_map/all_to_all | solution.py:41
  69.5 2.4 %kernel_one_back.1 = (bf16[2,256,256]{2,1,0:T(8,128)(2,1)S(1)}, bf16[2,256,256]{2,1,0:T(8,128)(2,1)S(1)}, f32[256,256]{1,0:T(8,128)S(1)}) custom-call(s32[2]{0:T(128)S(1)} %pad_add_fusion.refs_0_, f32[16,2,512]{2,1,0:T(2,128)S(1)} %all_to_all.35.refs_1_, f32[512,256]{1,0:T(8,128)S(1)} %get-tuple-element.46.refs_2_, ...), custom_call_target="tpu_custom_call" | custom-call | flops 2000000000 | bytes 2295816 | tf_op jit(solution)/shard_map/kernel_one_back/pallas_call | solution.py:159
  72.7 2.8 %all-to-all-done.4.refs_0_ = bf16[16,40,128]{2,1,0:T(8,128)(2,1)S(1)} async-done(((bf16[16,40,128]{2,1,0:T(8,128)(2,1)}), bf16[16,40,128]{2,1,0:T(8,128)(2,1)S(1)}, u32[]{:S(2)}, u32[]{:S(2)}) %all-to-all-start.4) | async-done | bytes 163872 | tf_op jit(solution)/shard_map/all_to_all | solution.py:41
  75.4 0.9 context_back.1
  76.4 3.8 %all-to-all-start.5 = ((bf16[16,40,128]{2,1,0:T(8,128)(2,1)}), bf16[16,40,128]{2,1,0:T(8,128)(2,1)S(1)}, u32[]{:S(2)}, u32[]{:S(2)}) async-start(bf16[16,40,128]{2,1,0:T(8,128)(2,1)} %get-tuple-element.51.refs_6_), calls=%async_computation.5 | async-start | bytes 327680 | tf_op jit(solution)/shard_map/all_to_all | solution.py:41
  80.2 1.5 %copy-done.12 = f32[7,256,256]{2,1,0:T(8,128)S(1)} copy-done((f32[7,256,256]{2,1,0:T(8,128)S(1)}, f32[7,256,256]{2,1,0:T(8,128)}, u32[]{:S(2)}) %copy-start.12) | copy-done | bytes 1835032
  81.7 0.9 copy-done.14
  82.7 4.2 %inverse_back.1.refs_4_ = f32[256,512]{1,0:T(8,128)S(1)} custom-call(s32[2]{0:T(128)S(1)} %pad_add_fusion.refs_0_, f32[7,256,256]{2,1,0:T(8,128)S(1)} %copy-done.12, f32[24,256]{1,0:T(8,128)S(1)} %get-tuple-element.50.refs_2_, f32[16,256]{1,0:T(8,128)S(1)} %get-tuple-element.54.refs_3_, bf16[256,512]{1,0:T(8,128)(2,1)S(1)} %bitcast.11, ...), custom_call_target="tpu_custom_call" | custom-call | flops 5000000000 | bytes 2924552 | tf_op jit(solution)/shard_map/inverse_back/pallas_call | solution.py:159
  87.1 1.4 %landmarks_back.1 = (bf16[256,512]{1,0:T(8,128)(2,1)}, bf16[1152,128]{1,0:T(8,128)(2,1)}) custom-call(bf16[16,40,128]{2,1,0:T(8,128)(2,1)S(1)} %all-to-all-done.5.refs_0_, bf16[2,528,256]{2,1,0:T(8,128)(2,1)S(1)} %get-tuple-element.52.refs_1_, bf16[512,256]{1,0:T(8,128)(2,1)S(1)} %get-tuple-element.38.refs_1_.refs_2_, ...), custom_call_target="tpu_custom_call" | custom-call | flops 100000000 | bytes 2572288 | tf_op jit(solution)/shard_map/landmarks_back/pallas_call | solution.py:159
  88.5 2.9 %collective-permute-start.5 = (bf16[1152,128]{1,0:T(8,128)(2,1)}, bf16[1152,128]{1,0:T(8,128)(2,1)S(1)}, u32[]{:S(2)}, u32[]{:S(2)}) collective-permute-start(bf16[1152,128]{1,0:T(8,128)(2,1)} %get-tuple-element.57.refs_3_), channel_id=1, source_target_pairs={{0,8},{8,0},{16,24},{24,16},{32,40},{40,32},{48,56},{56,48},{64,72... | collective-permute-start | bytes 884744 | tf_op jit(solution)/shard_map/ppermute | solution.py:664
  91.5 6.6 %all-to-all-start.6 = ((bf16[32,8,512]{2,1,0:T(8,128)(2,1)}), bf16[32,8,512]{2,1,0:T(8,128)(2,1)S(1)}, u32[]{:S(2)}, u32[]{:S(2)}) async-start(bf16[32,8,512]{2,1,0:T(8,128)(2,1)} %bitcast.5), calls=%async_computation.6 | async-start | bytes 524288 | tf_op jit(solution)/shard_map/all_to_all | solution.py:41
  98.0 1.3 %gather.1.refs_5_ = bf16[256,512]{1,0:T(8,128)(2,1)} custom-call(s32[2]{0:T(128)S(1)} %pad_add_fusion.refs_0_, bf16[2,256,256]{2,1,0:T(8,128)(2,1)S(1)} %get-tuple-element.47.refs_1_.refs_2_, bf16[2,256,256]{2,1,0:T(8,128)(2,1)S(1)} %collective-permute-done.4.refs_2_.refs_3_, bf16[256,512]{1,0:T(8,128)(2,1)} %get-tuple-element.56.refs_3_.refs_5_), custom_call_target="tpu_custom_call" | custom-call | flops 1000000 | bytes 786440 | tf_op jit(solution)/shard_map/gather/pallas_call | solution.py:159
  99.3 2.8 %kernel_three_back.1 = (bf16[256,512]{1,0:T(8,128)(2,1)}, f32[256,512]{1,0:T(8,128)S(1)}, f32[1,512]{1,0:T(1,128)}) custom-call(s32[2]{0:T(128)S(1)} %pad_add_fusion.refs_0_, bf16[256,512]{1,0:T(8,128)(2,1)S(1)} %copy-done.2, bf16[256,512]{1,0:T(8,128)(2,1)S(1)} %copy-done.6, bf16[1152,128]{1,0:T(8,128)(2,1)} %get-tuple-element.57.refs_3_, ...), custom_call_target="tpu_custom_call" | custom-call | flops 2000000000 | bytes 1902600 | tf_op jit(solution)/shard_map/kernel_three_back/pallas_call | solution.py:159
  102.1 4.9 %all-to-all-done.6.refs_1_ = bf16[32,8,512]{2,1,0:T(8,128)(2,1)S(1)} async-done(((bf16[32,8,512]{2,1,0:T(8,128)(2,1)}), bf16[32,8,512]{2,1,0:T(8,128)(2,1)S(1)}, u32[]{:S(2)}, u32[]{:S(2)}) %all-to-all-start.6) | async-done | bytes 262176 | tf_op jit(solution)/shard_map/all_to_all | solution.py:41
  107.0 1.4 %finish.1 = (bf16[256,512]{1,0:T(8,128)(2,1)}, bf16[256,512]{1,0:T(8,128)(2,1)}) custom-call(s32[2]{0:T(128)S(1)} %pad_add_fusion.refs_0_, bf16[32,8,512]{2,1,0:T(8,128)(2,1)S(1)} %all-to-all-done.6.refs_1_, bf16[2,256,256]{2,1,0:T(8,128)(2,1)S(1)} %get-tuple-element.47.refs_1_.refs_2_, bf16[2,256,256]{2,1,0:T(8,128)(2,1)S(1)} %collective-permute-done.4.refs_2_.refs_3_, ...), custom_call_target="tpu_custom_call" | custom-call | flops 1000000 | bytes 1835016 | tf_op jit(solution)/shard_map/finish/pallas_call | solution.py:159
  (40 shorter events, 5.7 us)
Async XLA Ops:
  2.5 9.9 %collective-permute-start.2 = (bf16[256,512]{1,0:T(8,128)(2,1)}, bf16[256,512]{1,0:T(8,128)(2,1)S(1)}, u32[]{:S(2)}, u32[]{:S(2)}) collective-permute-start(bf16[256,512]{1,0:T(8,128)(2,1)} %refs_1_.7), channel_id=1, source_target_pairs={{0,8},{8,0},{16,24},{24,16},{32,40},{40,32},{48,56},{56,48},{64,72... | collective-permute-start | bytes 786440 | tf_op jit(solution)/shard_map/ppermute | solution.py:606
  5.9 6.5 %collective-permute-start.3 = (bf16[256,512]{1,0:T(8,128)(2,1)}, bf16[256,512]{1,0:T(8,128)(2,1)S(1)}, u32[]{:S(2)}, u32[]{:S(2)}) collective-permute-start(bf16[256,512]{1,0:T(8,128)(2,1)} %refs_2_.5), channel_id=1, source_target_pairs={{0,8},{8,0},{16,24},{24,16},{32,40},{40,32},{48,56},{56,48},{64,72... | collective-permute-start | bytes 786440 | tf_op jit(solution)/shard_map/ppermute | solution.py:606
  6.0 14.8 %all-to-all-start = ((bf16[32,8,512]{2,1,0:T(8,128)(2,1)}), bf16[32,8,512]{2,1,0:T(8,128)(2,1)S(1)}, u32[]{:S(2)}, u32[]{:S(2)}) async-start(bf16[32,8,512]{2,1,0:T(8,128)(2,1)} %landmark_means.1.refs_5_), calls=%async_computation | async-start | bytes 524288 | tf_op jit(solution)/shard_map/all_to_all | solution.py:41
  11.7 26.1 %collective-permute-start = (bf16[256,512]{1,0:T(8,128)(2,1)}, bf16[256,512]{1,0:T(8,128)(2,1)S(1)}, u32[]{:S(2)}, u32[]{:S(2)}) collective-permute-start(bf16[256,512]{1,0:T(8,128)(2,1)} %refs_1_.6), channel_id=1, source_target_pairs={{0,8},{8,0},{16,24},{24,16},{32,40},{40,32},{48,56},{56,48},{64,72... | collective-permute-start | bytes 786440 | tf_op jit(solution)/shard_map/ppermute | solution.py:606
  12.1 25.8 %collective-permute-start.1 = (bf16[256,512]{1,0:T(8,128)(2,1)}, bf16[256,512]{1,0:T(8,128)(2,1)S(1)}, u32[]{:S(2)}, u32[]{:S(2)}) collective-permute-start(bf16[256,512]{1,0:T(8,128)(2,1)} %refs_2_.4), channel_id=1, source_target_pairs={{0,8},{8,0},{16,24},{24,16},{32,40},{40,32},{48,56},{56,48},{64,72... | collective-permute-start | bytes 786440 | tf_op jit(solution)/shard_map/ppermute | solution.py:606
  12.4 1.0 copy-start
  13.4 0.9 copy-start.1
  14.3 0.9 copy-start.5
  22.4 10.4 %all-to-all-start.1 = ((bf16[16,40,128]{2,1,0:T(8,128)(2,1)}), bf16[16,40,128]{2,1,0:T(8,128)(2,1)S(1)}, u32[]{:S(2)}, u32[]{:S(2)}) async-start(bf16[16,40,128]{2,1,0:T(8,128)(2,1)} %local_context.1.refs_2_), calls=%async_computation.1 | async-start | bytes 327680 | tf_op jit(solution)/shard_map/all_to_all | solution.py:41
  25.9 12.0 %copy-start.3 = (bf16[256,512]{1,0:T(8,128)(2,1)S(1)}, bf16[256,512]{1,0:T(8,128)(2,1)}, u32[]{:S(2)}) copy-start(bf16[256,512]{1,0:T(8,128)(2,1)} %refs_1_.6) | copy-start | bytes 786436
  25.9 12.0 %copy-start.7 = (bf16[256,512]{1,0:T(8,128)(2,1)S(1)}, bf16[256,512]{1,0:T(8,128)(2,1)}, u32[]{:S(2)}) copy-start(bf16[256,512]{1,0:T(8,128)(2,1)} %refs_2_.4) | copy-start | bytes 786436
  29.1 1.3 %copy-start.11 = (f32[7,256,256]{2,1,0:T(8,128)}, f32[7,256,256]{2,1,0:T(8,128)S(1)}, u32[]{:S(2)}) copy-start(f32[7,256,256]{2,1,0:T(8,128)S(1)} %get-tuple-element.53.refs_1_) | copy-start | bytes 5505028
  33.7 11.0 %all-to-all-start.2 = ((bf16[16,16,256]{2,1,0:T(8,128)(2,1)}), bf16[16,16,256]{2,1,0:T(8,128)(2,1)S(1)}, u32[]{:S(2)}, u32[]{:S(2)}) async-start(bf16[16,16,256]{2,1,0:T(8,128)(2,1)} %get-tuple-element.41.refs_5_.refs_3_), calls=%async_computation.2 | async-start | bytes 262144 | tf_op jit(solution)/shard_map/all_to_all | solution.py:41
  38.5 0.9 copy-start.9
  38.5 6.1 %copy-start.8 = (f32[512]{0:T(512)S(1)}, f32[512]{0:T(512)}, u32[]{:S(2)}) copy-start(f32[512]{0:T(512)} %param.8) | copy-start | bytes 6148
  65.0 10.4 %all-to-all-start.4 = ((bf16[16,40,128]{2,1,0:T(8,128)(2,1)}), bf16[16,40,128]{2,1,0:T(8,128)(2,1)S(1)}, u32[]{:S(2)}, u32[]{:S(2)}) async-start(bf16[16,40,128]{2,1,0:T(8,128)(2,1)} %norm.1.refs_8_), calls=%async_computation.4 | async-start | bytes 327680 | tf_op jit(solution)/shard_map/all_to_all | solution.py:41
  68.5 1.0 copy-start.10
  71.9 0.7 copy-start.13
  76.4 10.7 %all-to-all-start.5 = ((bf16[16,40,128]{2,1,0:T(8,128)(2,1)}), bf16[16,40,128]{2,1,0:T(8,128)(2,1)S(1)}, u32[]{:S(2)}, u32[]{:S(2)}) async-start(bf16[16,40,128]{2,1,0:T(8,128)(2,1)} %get-tuple-element.51.refs_6_), calls=%async_computation.5 | async-start | bytes 327680 | tf_op jit(solution)/shard_map/all_to_all | solution.py:41
  80.2 1.5 %copy-start.12 = (f32[7,256,256]{2,1,0:T(8,128)S(1)}, f32[7,256,256]{2,1,0:T(8,128)}, u32[]{:S(2)}) copy-start(f32[7,256,256]{2,1,0:T(8,128)} %copy-done.11) | copy-start | bytes 5505028
  81.7 0.9 copy-start.14
  86.9 12.4 %copy-start.2 = (bf16[256,512]{1,0:T(8,128)(2,1)S(1)}, bf16[256,512]{1,0:T(8,128)(2,1)}, u32[]{:S(2)}) copy-start(bf16[256,512]{1,0:T(8,128)(2,1)} %refs_1_.7) | copy-start | bytes 786436
  86.9 12.4 %copy-start.6 = (bf16[256,512]{1,0:T(8,128)(2,1)S(1)}, bf16[256,512]{1,0:T(8,128)(2,1)}, u32[]{:S(2)}) copy-start(bf16[256,512]{1,0:T(8,128)(2,1)} %refs_2_.5) | copy-start | bytes 786436
  88.5 10.8 %collective-permute-start.5 = (bf16[1152,128]{1,0:T(8,128)(2,1)}, bf16[1152,128]{1,0:T(8,128)(2,1)S(1)}, u32[]{:S(2)}, u32[]{:S(2)}) collective-permute-start(bf16[1152,128]{1,0:T(8,128)(2,1)} %get-tuple-element.57.refs_3_), channel_id=1, source_target_pairs={{0,8},{8,0},{16,24},{24,16},{32,40},{40,32},{48,56},{56,48},{64,72... | collective-permute-start | bytes 884744 | tf_op jit(solution)/shard_map/ppermute | solution.py:664
  91.5 6.6 %collective-permute-start.4 = (bf16[2,256,256]{2,1,0:T(8,128)(2,1)S(1)}, bf16[2,256,256]{2,1,0:T(8,128)(2,1)S(1)}, u32[]{:S(2)}, u32[]{:S(2)}) collective-permute-start(bf16[2,256,256]{2,1,0:T(8,128)(2,1)S(1)} %get-tuple-element.48.refs_3_), channel_id=1, source_target_pairs={{0,8},{8,0},{16,24},{24,16},{32,40},{40,32},{48,56},{56,48},{64,72... | collective-permute-start | bytes 786440 | tf_op jit(solution)/shard_map/ppermute | solution.py:663
  91.5 15.6 %all-to-all-start.6 = ((bf16[32,8,512]{2,1,0:T(8,128)(2,1)}), bf16[32,8,512]{2,1,0:T(8,128)(2,1)S(1)}, u32[]{:S(2)}, u32[]{:S(2)}) async-start(bf16[32,8,512]{2,1,0:T(8,128)(2,1)} %bitcast.5), calls=%async_computation.6 | async-start | bytes 524288 | tf_op jit(solution)/shard_map/all_to_all | solution.py:41
  99.3 7.7 %copy-start.4 = (bf16[256,512]{1,0:T(8,128)(2,1)S(1)}, bf16[256,512]{1,0:T(8,128)(2,1)}, u32[]{:S(2)}) copy-start(bf16[256,512]{1,0:T(8,128)(2,1)} %gather.1.refs_5_) | copy-start | bytes 786436

commit v5 on v4

--- a/solution.py
+++ b/solution.py
@@ -415,22 +415,25 @@
     lk = land_ref[:, pl.ds(at + half, DH)]
     ktwo, x, h2, h3, p1, b2, b3 = [inv_ref[place] for place in range(7)]
     factor = column_factor(ktwo)
-    ktwo_s, x_s, h3_s, p1_s, b3_s = [split_up(part) for part in (ktwo, x, h3, p1, b3)]
+    ktwo_s, x_s, h3_s, p1_s = [split_up(part) for part in (ktwo, x, h3, p1)]
     g_mixing = split_up(g_ref[...])
-    context = split_up(kept_ref[: g_ref.shape[0]])
-    inner = split_up(exact(context, b3_s))
+    n = g_ref.shape[0]
+    context = kept_ref[:n]
+    once = exact(context, p1_s)
+    inner = exact(context, b3)
+    u = jnp.concatenate([-context, once, -exact(once, p1_s)], axis=0)
+    r0 = jnp.concatenate([inner, 0.25 * exact(u, x_s)], axis=0)
+    r1 = exact(r0, x_s)
+    left = jnp.concatenate([u, r0, r1, exact(r1, x_s)], axis=0)
+    d_outer = (factor * 0.0625) * exact(g_mixing, ktwo_s, NT)
+    d = exact(d_outer, h3_s)
+    v = jnp.concatenate([exact(d, b2), 7.0 * d - exact(d, p1_s), d], axis=0)
+    s0 = jnp.concatenate([d_outer, v], axis=0)
+    right = jnp.concatenate(
+        [0.25 * exact(v, h3_s), -exact(s0, h2), 7.0 * s0 - exact(s0, x_s), -s0], axis=0
+    )
+    d_x = exact(left, right, TN)
     outer = exact(inner, h3_s)
-    d_outer = split_up((factor * 0.0625) * exact(g_mixing, ktwo_s, NT))
-    d_inner = exact(d_outer, h3_s)
-    d_b3 = split_up(exact(context, d_inner, TN))
-    d_b2 = split_up(-exact(p1_s, d_b3))
-    d_b1 = -exact(p1_s, d_b2)
-    d_p1 = -exact(d_b3, b2) - exact(d_b2, eye_times(7.0) - p1) - d_b1
-    d_p1 = split_up(d_p1)
-    d_h3 = split_up(exact(inner, d_outer, TN) + 0.25 * exact(x_s, d_p1))
-    d_h2 = split_up(-exact(x_s, d_h3))
-    d_h1 = -exact(x_s, d_h2)
-    d_x = 0.25 * exact(d_p1, h3_s) - exact(d_h3, h2) - exact(d_h2, eye_times(7.0) - x) - d_h1
     d_ktwo = (factor * 0.0625) * exact(outer, g_mixing, TN) + factor * exact(
         d_x + jnp.transpose(d_x), ktwo_s
     )

time: 109 us -> 108 us (level)
  transfers between devices with their start and end apart: 12 -> 12, of which waited for: 6 -> 6; matrix products, arithmetic and copies ran while one was open for 0% -> 0% of each run, Pallas kernels for 17% -> 16%
where the time goes in v5:
time: 108 us; the launch traced here: 107 us
  starting transfers between devices  33.3 us (31%)
  Pallas kernels  26.2 us (24%)
  waiting for transfers between devices  21.4 us (20%)
  blocking collectives  17.4 us (16%)
  local copies, waits for them, and re-layouts  8.22 us (8%)
    all_to_all x6, starting transfers between devices, exchange(): return lax.all_to_all(parts, axis, 0, 0, axis_index_groups=groups)  26.3 us
    pallas_call x16, Pallas kernels, call(): pl.pallas_call(whole, out_shape=outs, in_specs=in_specs, out_specs=[space...  26.2 us
    all_to_all x6, waiting for transfers between devices, exchange(): return lax.all_to_all(parts, axis, 0, 0, axis_index_groups=groups)  21.4 us
    all_to_all x1, blocking collectives, exchange(): return lax.all_to_all(parts, axis, 0, 0, axis_index_groups=groups)  17.4 us
    unnamed x30, local copies, waits for them, and re-layouts  8.22 us
    ppermute x4, starting transfers between devices, on_device(): lax.ppermute(x, 'ctx', swap)  4.03 us
    ppermute x1, starting transfers between devices, on_device(): passed_there = lax.ppermute(passed, 'ctx', swap)  2.93 us
  transfers between devices with their start and end apart: 12, of which 6 were waited for; matrix products, arithmetic and copies ran while one was open for 0% of the time, Pallas kernels for 16%

profile of v5, /device:TPU:1, one launch (start us, length us, event | category | flops | bytes accessed | tf_op | source)
XLA Modules:
  0.0 107.5 jit_solution(289177284537597490)
XLA Ops:
  0.6 1.9 %landmark_means.1.refs_5_ = bf16[32,8,512]{2,1,0:T(8,128)(2,1)} custom-call(bf16[256,512]{1,0:T(8,128)(2,1)} %refs_1_.6, bf16[256,512]{1,0:T(8,128)(2,1)} %refs_1_.7), custom_call_target="tpu_custom_call" | custom-call | flops 1000000 | bytes 786432 | tf_op jit(solution)/shard_map/landmark_means/pallas_call | solution.py:159
  2.5 3.3 %collective-permute-start.2 = (bf16[256,512]{1,0:T(8,128)(2,1)}, bf16[256,512]{1,0:T(8,128)(2,1)S(1)}, u32[]{:S(2)}, u32[]{:S(2)}) collective-permute-start(bf16[256,512]{1,0:T(8,128)(2,1)} %refs_1_.7), channel_id=1, source_target_pairs={{0,8},{8,0},{16,24},{24,16},{32,40},{40,32},{48,56},{56,48},{64,72... | collective-permute-start | bytes 786440 | tf_op jit(solution)/shard_map/ppermute | solution.py:609
  6.0 5.8 %all-to-all-start = ((bf16[32,8,512]{2,1,0:T(8,128)(2,1)}), bf16[32,8,512]{2,1,0:T(8,128)(2,1)S(1)}, u32[]{:S(2)}, u32[]{:S(2)}) async-start(bf16[32,8,512]{2,1,0:T(8,128)(2,1)} %landmark_means.1.refs_5_), calls=%async_computation | async-start | bytes 524288 | tf_op jit(solution)/shard_map/all_to_all | solution.py:41
  12.4 0.9 copy-done
  13.4 0.9 copy-done.1
  14.3 0.9 copy-done.5
  15.9 4.8 %all-to-all-done = bf16[32,8,512]{2,1,0:T(8,128)(2,1)S(1)} async-done(((bf16[32,8,512]{2,1,0:T(8,128)(2,1)}), bf16[32,8,512]{2,1,0:T(8,128)(2,1)S(1)}, u32[]{:S(2)}, u32[]{:S(2)}) %all-to-all-start) | async-done | bytes 262176 | tf_op jit(solution)/shard_map/all_to_all | solution.py:41
  20.7 1.6 %local_context.1.refs_2_ = bf16[16,40,128]{2,1,0:T(8,128)(2,1)} custom-call(bf16[256,512]{1,0:T(8,128)(2,1)S(1)} %bitcast.7, bf16[512,256]{1,0:T(8,128)(2,1)S(1)} %get-tuple-element.38.refs_1_.refs_2_, bf16[512,256]{1,0:T(8,128)(2,1)S(1)} %get-tuple-element.39.refs_2_.refs_3_), custom_call_target="tpu_custom_call" | custom-call | flops 100000000 | bytes 950272 | tf_op jit(solution)/shard_map/local_context/pallas_call | solution.py:159
  22.4 3.5 %all-to-all-start.1 = ((bf16[16,40,128]{2,1,0:T(8,128)(2,1)}), bf16[16,40,128]{2,1,0:T(8,128)(2,1)S(1)}, u32[]{:S(2)}, u32[]{:S(2)}) async-start(bf16[16,40,128]{2,1,0:T(8,128)(2,1)} %local_context.1.refs_2_), calls=%async_computation.1 | async-start | bytes 327680 | tf_op jit(solution)/shard_map/all_to_all | solution.py:41
  25.9 3.1 %inverse.1 = (f32[256,256]{1,0:T(8,128)S(1)}, f32[256,256]{1,0:T(8,128)S(1)}, f32[7,256,256]{2,1,0:T(8,128)S(1)}) custom-call(s32[2]{0:T(128)S(1)} %pad_add_fusion.refs_0_, bf16[256,512]{1,0:T(8,128)(2,1)S(1)} %bitcast.8, bf16[16,40,128]{2,1,0:T(8,128)(2,1)} %local_context.1.refs_2_), custom_call_target="tpu_custom_call" | custom-call | flops 3000000000 | bytes 2621448 | tf_op jit(solution)/shard_map/inverse/pallas_call | solution.py:159
  29.1 1.2 %copy-done.11 = f32[7,256,256]{2,1,0:T(8,128)} copy-done((f32[7,256,256]{2,1,0:T(8,128)}, f32[7,256,256]{2,1,0:T(8,128)S(1)}, u32[]{:S(2)}) %copy-start.11) | copy-done | bytes 1835032
  30.3 2.5 %all-to-all-done.1.refs_0_ = bf16[16,40,128]{2,1,0:T(8,128)(2,1)S(1)} async-done(((bf16[16,40,128]{2,1,0:T(8,128)(2,1)}), bf16[16,40,128]{2,1,0:T(8,128)(2,1)S(1)}, u32[]{:S(2)}, u32[]{:S(2)}) %all-to-all-start.1) | async-done | bytes 163872 | tf_op jit(solution)/shard_map/all_to_all | solution.py:41
  33.7 4.1 %all-to-all-start.2 = ((bf16[16,16,256]{2,1,0:T(8,128)(2,1)}), bf16[16,16,256]{2,1,0:T(8,128)(2,1)S(1)}, u32[]{:S(2)}, u32[]{:S(2)}) async-start(bf16[16,16,256]{2,1,0:T(8,128)(2,1)} %get-tuple-element.41.refs_5_.refs_3_), calls=%async_computation.2 | async-start | bytes 262144 | tf_op jit(solution)/shard_map/all_to_all | solution.py:41
  39.4 5.2 %all-to-all-done.2 = bf16[16,16,256]{2,1,0:T(8,128)(2,1)S(1)} async-done(((bf16[16,16,256]{2,1,0:T(8,128)(2,1)}), bf16[16,16,256]{2,1,0:T(8,128)(2,1)S(1)}, u32[]{:S(2)}, u32[]{:S(2)}) %all-to-all-start.2) | async-done | bytes 131104 | tf_op jit(solution)/shard_map/all_to_all | solution.py:41
  44.7 1.0 output.1
  45.7 17.4 %all_to_all.35.refs_1_ = f32[16,2,512]{2,1,0:T(2,128)S(1)} all-to-all(f32[16,2,512]{2,1,0:T(2,128)S(1)} %get-tuple-element.45), channel_id=1, replica_groups={{0,1,2,3,4,5,6,7,8,9,10,11,12,13,14,15},{16,17,18,19,20,21,22,23,24,25,..., dimensions={0} | all-to-all | bytes 131072 | tf_op jit(solution)/shard_map/all_to_all | solution.py:41
  63.2 1.9 %norm.1.refs_8_ = bf16[16,40,128]{2,1,0:T(8,128)(2,1)} custom-call(s32[2]{0:T(128)S(1)} %pad_add_fusion.refs_0_, f32[16,2,512]{2,1,0:T(2,128)S(1)} %all_to_all.35.refs_1_, f32[512,256]{1,0:T(8,128)S(1)} %get-tuple-element.46.refs_2_, bf16[512,256]{1,0:T(8,128)(2,1)S(1)} %get-tuple-element.44.refs_3_, f32[1,512]{1,0:T(1,128)S(1)} %bitcast.16, ...), custom_call_target="tpu_custom_call" | custom-call | flops 100000000 | bytes 1542152 | tf_op jit(solution)/shard_map/norm/pallas_call | solution.py:159
  65.0 3.5 %all-to-all-start.4 = ((bf16[16,40,128]{2,1,0:T(8,128)(2,1)}), bf16[16,40,128]{2,1,0:T(8,128)(2,1)S(1)}, u32[]{:S(2)}, u32[]{:S(2)}) async-start(bf16[16,40,128]{2,1,0:T(8,128)(2,1)} %norm.1.refs_8_), calls=%async_computation.4 | async-start | bytes 327680 | tf_op jit(solution)/shard_map/all_to_all | solution.py:41
  69.5 2.4 %kernel_one_back.1 = (bf16[2,256,256]{2,1,0:T(8,128)(2,1)S(1)}, bf16[2,256,256]{2,1,0:T(8,128)(2,1)S(1)}, f32[256,256]{1,0:T(8,128)S(1)}) custom-call(s32[2]{0:T(128)S(1)} %pad_add_fusion.refs_0_, f32[16,2,512]{2,1,0:T(2,128)S(1)} %all_to_all.35.refs_1_, f32[512,256]{1,0:T(8,128)S(1)} %get-tuple-element.46.refs_2_, ...), custom_call_target="tpu_custom_call" | custom-call | flops 2000000000 | bytes 2295816 | tf_op jit(solution)/shard_map/kernel_one_back/pallas_call | solution.py:159
  72.7 2.8 %all-to-all-done.4.refs_0_ = bf16[16,40,128]{2,1,0:T(8,128)(2,1)S(1)} async-done(((bf16[16,40,128]{2,1,0:T(8,128)(2,1)}), bf16[16,40,128]{2,1,0:T(8,128)(2,1)S(1)}, u32[]{:S(2)}, u32[]{:S(2)}) %all-to-all-start.4) | async-done | bytes 163872 | tf_op jit(solution)/shard_map/all_to_all | solution.py:41
  76.4 3.8 %all-to-all-start.5 = ((bf16[16,40,128]{2,1,0:T(8,128)(2,1)}), bf16[16,40,128]{2,1,0:T(8,128)(2,1)S(1)}, u32[]{:S(2)}, u32[]{:S(2)}) async-start(bf16[16,40,128]{2,1,0:T(8,128)(2,1)} %get-tuple-element.51.refs_6_), calls=%async_computation.5 | async-start | bytes 327680 | tf_op jit(solution)/shard_map/all_to_all | solution.py:41
  80.2 1.5 %copy-done.12 = f32[7,256,256]{2,1,0:T(8,128)S(1)} copy-done((f32[7,256,256]{2,1,0:T(8,128)S(1)}, f32[7,256,256]{2,1,0:T(8,128)}, u32[]{:S(2)}) %copy-start.12) | copy-done | bytes 1835032
  81.7 0.9 copy-done.14
  82.7 3.3 %inverse_back.1.refs_4_ = f32[256,512]{1,0:T(8,128)S(1)} custom-call(s32[2]{0:T(128)S(1)} %pad_add_fusion.refs_0_, f32[7,256,256]{2,1,0:T(8,128)S(1)} %copy-done.12, f32[24,256]{1,0:T(8,128)S(1)} %get-tuple-element.50.refs_2_, f32[16,256]{1,0:T(8,128)S(1)} %get-tuple-element.54.refs_3_, bf16[256,512]{1,0:T(8,128)(2,1)S(1)} %bitcast.11, ...), custom_call_target="tpu_custom_call" | custom-call | flops 5000000000 | bytes 2924552 | tf_op jit(solution)/shard_map/inverse_back/pallas_call | solution.py:159
  86.0 1.2 %all-to-all-done.5.refs_0_ = bf16[16,40,128]{2,1,0:T(8,128)(2,1)S(1)} async-done(((bf16[16,40,128]{2,1,0:T(8,128)(2,1)}), bf16[16,40,128]{2,1,0:T(8,128)(2,1)S(1)}, u32[]{:S(2)}, u32[]{:S(2)}) %all-to-all-start.5) | async-done | bytes 163872 | tf_op jit(solution)/shard_map/all_to_all | solution.py:41
  87.1 1.4 %landmarks_back.1 = (bf16[256,512]{1,0:T(8,128)(2,1)}, bf16[1152,128]{1,0:T(8,128)(2,1)}) custom-call(bf16[16,40,128]{2,1,0:T(8,128)(2,1)S(1)} %all-to-all-done.5.refs_0_, bf16[2,528,256]{2,1,0:T(8,128)(2,1)S(1)} %get-tuple-element.52.refs_1_, bf16[512,256]{1,0:T(8,128)(2,1)S(1)} %get-tuple-element.38.refs_1_.refs_2_, ...), custom_call_target="tpu_custom_call" | custom-call | flops 100000000 | bytes 2572288 | tf_op jit(solution)/shard_map/landmarks_back/pallas_call | solution.py:159
  88.5 2.9 %collective-permute-start.5 = (bf16[1152,128]{1,0:T(8,128)(2,1)}, bf16[1152,128]{1,0:T(8,128)(2,1)S(1)}, u32[]{:S(2)}, u32[]{:S(2)}) collective-permute-start(bf16[1152,128]{1,0:T(8,128)(2,1)} %get-tuple-element.57.refs_3_), channel_id=1, source_target_pairs={{0,8},{8,0},{16,24},{24,16},{32,40},{40,32},{48,56},{56,48},{64,72... | collective-permute-start | bytes 884744 | tf_op jit(solution)/shard_map/ppermute | solution.py:667
  91.5 5.6 %all-to-all-start.6 = ((bf16[32,8,512]{2,1,0:T(8,128)(2,1)}), bf16[32,8,512]{2,1,0:T(8,128)(2,1)S(1)}, u32[]{:S(2)}, u32[]{:S(2)}) async-start(bf16[32,8,512]{2,1,0:T(8,128)(2,1)} %bitcast.5), calls=%async_computation.6 | async-start | bytes 524288 | tf_op jit(solution)/shard_map/all_to_all | solution.py:41
  97.1 1.3 %gather.1.refs_5_ = bf16[256,512]{1,0:T(8,128)(2,1)} custom-call(s32[2]{0:T(128)S(1)} %pad_add_fusion.refs_0_, bf16[2,256,256]{2,1,0:T(8,128)(2,1)S(1)} %get-tuple-element.47.refs_1_.refs_2_, bf16[2,256,256]{2,1,0:T(8,128)(2,1)S(1)} %collective-permute-done.4.refs_2_.refs_3_, bf16[256,512]{1,0:T(8,128)(2,1)} %get-tuple-element.56.refs_3_.refs_5_), custom_call_target="tpu_custom_call" | custom-call | flops 1000000 | bytes 786440 | tf_op jit(solution)/shard_map/gather/pallas_call | solution.py:159
  98.3 2.8 %kernel_three_back.1 = (bf16[256,512]{1,0:T(8,128)(2,1)}, f32[256,512]{1,0:T(8,128)S(1)}, f32[1,512]{1,0:T(1,128)}) custom-call(s32[2]{0:T(128)S(1)} %pad_add_fusion.refs_0_, bf16[256,512]{1,0:T(8,128)(2,1)S(1)} %copy-done.2, bf16[256,512]{1,0:T(8,128)(2,1)S(1)} %copy-done.6, bf16[1152,128]{1,0:T(8,128)(2,1)} %get-tuple-element.57.refs_3_, ...), custom_call_target="tpu_custom_call" | custom-call | flops 2000000000 | bytes 1902600 | tf_op jit(solution)/shard_map/kernel_three_back/pallas_call | solution.py:159
  101.1 4.9 %all-to-all-done.6.refs_1_ = bf16[32,8,512]{2,1,0:T(8,128)(2,1)S(1)} async-done(((bf16[32,8,512]{2,1,0:T(8,128)(2,1)}), bf16[32,8,512]{2,1,0:T(8,128)(2,1)S(1)}, u32[]{:S(2)}, u32[]{:S(2)}) %all-to-all-start.6) | async-done | bytes 262176 | tf_op jit(solution)/shard_map/all_to_all | solution.py:41
  106.0 1.4 %finish.1 = (bf16[256,512]{1,0:T(8,128)(2,1)}, bf16[256,512]{1,0:T(8,128)(2,1)}) custom-call(s32[2]{0:T(128)S(1)} %pad_add_fusion.refs_0_, bf16[32,8,512]{2,1,0:T(8,128)(2,1)S(1)} %all-to-all-done.6.refs_1_, bf16[2,256,256]{2,1,0:T(8,128)(2,1)S(1)} %get-tuple-element.47.refs_1_.refs_2_, bf16[2,256,256]{2,1,0:T(8,128)(2,1)S(1)} %collective-permute-done.4.refs_2_.refs_3_, ...), custom_call_target="tpu_custom_call" | custom-call | flops 1000000 | bytes 1835016 | tf_op jit(solution)/shard_map/finish/pallas_call | solution.py:159
  (40 shorter events, 6.5 us)
Async XLA Ops:
  2.5 9.9 %collective-permute-start.2 = (bf16[256,512]{1,0:T(8,128)(2,1)}, bf16[256,512]{1,0:T(8,128)(2,1)S(1)}, u32[]{:S(2)}, u32[]{:S(2)}) collective-permute-start(bf16[256,512]{1,0:T(8,128)(2,1)} %refs_1_.7), channel_id=1, source_target_pairs={{0,8},{8,0},{16,24},{24,16},{32,40},{40,32},{48,56},{56,48},{64,72... | collective-permute-start | bytes 786440 | tf_op jit(solution)/shard_map/ppermute | solution.py:609
  5.9 6.5 %collective-permute-start.3 = (bf16[256,512]{1,0:T(8,128)(2,1)}, bf16[256,512]{1,0:T(8,128)(2,1)S(1)}, u32[]{:S(2)}, u32[]{:S(2)}) collective-permute-start(bf16[256,512]{1,0:T(8,128)(2,1)} %refs_2_.5), channel_id=1, source_target_pairs={{0,8},{8,0},{16,24},{24,16},{32,40},{40,32},{48,56},{56,48},{64,72... | collective-permute-start | bytes 786440 | tf_op jit(solution)/shard_map/ppermute | solution.py:609
  6.0 14.8 %all-to-all-start = ((bf16[32,8,512]{2,1,0:T(8,128)(2,1)}), bf16[32,8,512]{2,1,0:T(8,128)(2,1)S(1)}, u32[]{:S(2)}, u32[]{:S(2)}) async-start(bf16[32,8,512]{2,1,0:T(8,128)(2,1)} %landmark_means.1.refs_5_), calls=%async_computation | async-start | bytes 524288 | tf_op jit(solution)/shard_map/all_to_all | solution.py:41
  11.7 26.1 %collective-permute-start = (bf16[256,512]{1,0:T(8,128)(2,1)}, bf16[256,512]{1,0:T(8,128)(2,1)S(1)}, u32[]{:S(2)}, u32[]{:S(2)}) collective-permute-start(bf16[256,512]{1,0:T(8,128)(2,1)} %refs_1_.6), channel_id=1, source_target_pairs={{0,8},{8,0},{16,24},{24,16},{32,40},{40,32},{48,56},{56,48},{64,72... | collective-permute-start | bytes 786440 | tf_op jit(solution)/shard_map/ppermute | solution.py:609
  12.1 25.8 %collective-permute-start.1 = (bf16[256,512]{1,0:T(8,128)(2,1)}, bf16[256,512]{1,0:T(8,128)(2,1)S(1)}, u32[]{:S(2)}, u32[]{:S(2)}) collective-permute-start(bf16[256,512]{1,0:T(8,128)(2,1)} %refs_2_.4), channel_id=1, source_target_pairs={{0,8},{8,0},{16,24},{24,16},{32,40},{40,32},{48,56},{56,48},{64,72... | collective-permute-start | bytes 786440 | tf_op jit(solution)/shard_map/ppermute | solution.py:609
  12.4 1.0 copy-start
  13.4 0.9 copy-start.1
  14.3 0.9 copy-start.5
  22.4 10.4 %all-to-all-start.1 = ((bf16[16,40,128]{2,1,0:T(8,128)(2,1)}), bf16[16,40,128]{2,1,0:T(8,128)(2,1)S(1)}, u32[]{:S(2)}, u32[]{:S(2)}) async-start(bf16[16,40,128]{2,1,0:T(8,128)(2,1)} %local_context.1.refs_2_), calls=%async_computation.1 | async-start | bytes 327680 | tf_op jit(solution)/shard_map/all_to_all | solution.py:41
  25.9 12.0 %copy-start.3 = (bf16[256,512]{1,0:T(8,128)(2,1)S(1)}, bf16[256,512]{1,0:T(8,128)(2,1)}, u32[]{:S(2)}) copy-start(bf16[256,512]{1,0:T(8,128)(2,1)} %refs_1_.6) | copy-start | bytes 786436
  25.9 12.0 %copy-start.7 = (bf16[256,512]{1,0:T(8,128)(2,1)S(1)}, bf16[256,512]{1,0:T(8,128)(2,1)}, u32[]{:S(2)}) copy-start(bf16[256,512]{1,0:T(8,128)(2,1)} %refs_2_.4) | copy-start | bytes 786436
  29.1 1.3 %copy-start.11 = (f32[7,256,256]{2,1,0:T(8,128)}, f32[7,256,256]{2,1,0:T(8,128)S(1)}, u32[]{:S(2)}) copy-start(f32[7,256,256]{2,1,0:T(8,128)S(1)} %get-tuple-element.53.refs_1_) | copy-start | bytes 5505028
  33.7 11.0 %all-to-all-start.2 = ((bf16[16,16,256]{2,1,0:T(8,128)(2,1)}), bf16[16,16,256]{2,1,0:T(8,128)(2,1)S(1)}, u32[]{:S(2)}, u32[]{:S(2)}) async-start(bf16[16,16,256]{2,1,0:T(8,128)(2,1)} %get-tuple-element.41.refs_5_.refs_3_), calls=%async_computation.2 | async-start | bytes 262144 | tf_op jit(solution)/shard_map/all_to_all | solution.py:41
  38.5 0.9 copy-start.9
  38.5 6.1 %copy-start.8 = (f32[512]{0:T(512)S(1)}, f32[512]{0:T(512)}, u32[]{:S(2)}) copy-start(f32[512]{0:T(512)} %param.8) | copy-start | bytes 6148
  65.0 10.4 %all-to-all-start.4 = ((bf16[16,40,128]{2,1,0:T(8,128)(2,1)}), bf16[16,40,128]{2,1,0:T(8,128)(2,1)S(1)}, u32[]{:S(2)}, u32[]{:S(2)}) async-start(bf16[16,40,128]{2,1,0:T(8,128)(2,1)} %norm.1.refs_8_), calls=%async_computation.4 | async-start | bytes 327680 | tf_op jit(solution)/shard_map/all_to_all | solution.py:41
  68.5 1.0 copy-start.10
  71.9 0.7 copy-start.13
  76.4 10.7 %all-to-all-start.5 = ((bf16[16,40,128]{2,1,0:T(8,128)(2,1)}), bf16[16,40,128]{2,1,0:T(8,128)(2,1)S(1)}, u32[]{:S(2)}, u32[]{:S(2)}) async-start(bf16[16,40,128]{2,1,0:T(8,128)(2,1)} %get-tuple-element.51.refs_6_), calls=%async_computation.5 | async-start | bytes 327680 | tf_op jit(solution)/shard_map/all_to_all | solution.py:41
  80.2 1.5 %copy-start.12 = (f32[7,256,256]{2,1,0:T(8,128)S(1)}, f32[7,256,256]{2,1,0:T(8,128)}, u32[]{:S(2)}) copy-start(f32[7,256,256]{2,1,0:T(8,128)} %copy-done.11) | copy-start | bytes 5505028
  81.7 0.9 copy-start.14
  85.9 12.4 %copy-start.2 = (bf16[256,512]{1,0:T(8,128)(2,1)S(1)}, bf16[256,512]{1,0:T(8,128)(2,1)}, u32[]{:S(2)}) copy-start(bf16[256,512]{1,0:T(8,128)(2,1)} %refs_1_.7) | copy-start | bytes 786436
  85.9 12.4 %copy-start.6 = (bf16[256,512]{1,0:T(8,128)(2,1)S(1)}, bf16[256,512]{1,0:T(8,128)(2,1)}, u32[]{:S(2)}) copy-start(bf16[256,512]{1,0:T(8,128)(2,1)} %refs_2_.5) | copy-start | bytes 786436
  88.5 9.8 %collective-permute-start.5 = (bf16[1152,128]{1,0:T(8,128)(2,1)}, bf16[1152,128]{1,0:T(8,128)(2,1)S(1)}, u32[]{:S(2)}, u32[]{:S(2)}) collective-permute-start(bf16[1152,128]{1,0:T(8,128)(2,1)} %get-tuple-element.57.refs_3_), channel_id=1, source_target_pairs={{0,8},{8,0},{16,24},{24,16},{32,40},{40,32},{48,56},{56,48},{64,72... | collective-permute-start | bytes 884744 | tf_op jit(solution)/shard_map/ppermute | solution.py:667
  91.5 5.6 %collective-permute-start.4 = (bf16[2,256,256]{2,1,0:T(8,128)(2,1)S(1)}, bf16[2,256,256]{2,1,0:T(8,128)(2,1)S(1)}, u32[]{:S(2)}, u32[]{:S(2)}) collective-permute-start(bf16[2,256,256]{2,1,0:T(8,128)(2,1)S(1)} %get-tuple-element.48.refs_3_), channel_id=1, source_target_pairs={{0,8},{8,0},{16,24},{24,16},{32,40},{40,32},{48,56},{56,48},{64,72... | collective-permute-start | bytes 786440 | tf_op jit(solution)/shard_map/ppermute | solution.py:666
  91.5 14.6 %all-to-all-start.6 = ((bf16[32,8,512]{2,1,0:T(8,128)(2,1)}), bf16[32,8,512]{2,1,0:T(8,128)(2,1)S(1)}, u32[]{:S(2)}, u32[]{:S(2)}) async-start(bf16[32,8,512]{2,1,0:T(8,128)(2,1)} %bitcast.5), calls=%async_computation.6 | async-start | bytes 524288 | tf_op jit(solution)/shard_map/all_to_all | solution.py:41
  98.3 7.7 %copy-start.4 = (bf16[256,512]{1,0:T(8,128)(2,1)S(1)}, bf16[256,512]{1,0:T(8,128)(2,1)}, u32[]{:S(2)}) copy-start(bf16[256,512]{1,0:T(8,128)(2,1)} %gather.1.refs_5_) | copy-start | bytes 786436

commit v6 on v5

--- a/solution.py
+++ b/solution.py
@@ -34,7 +34,13 @@
 def exact(a, b, dims=NN):
     a_high, a_low = a if isinstance(a, tuple) else split_up(a)
     b_high, b_low = b if isinstance(b, tuple) else split_up(b)
-    return dot(a_high, b_high, dims) + (dot(a_high, b_low, dims) + dot(a_low, b_high, dims))
+    if dims == TN:
+        return dot(a_high, b_high, dims) + (
+            dot(a_high, b_low, dims) + dot(a_low, b_high, dims)
+        )
+    n = a_high.shape[0]
+    both = dot(jnp.concatenate([a_high, a_low], axis=0), b_high, dims)
+    return both[:n] + (both[n:] + dot(a_high, b_low, dims))
 
 
 def exchange(parts, axis, groups=None):
@@ -192,6 +198,12 @@
     for mine, there, out in zip(refs[:count], refs[count : 2 * count], refs[2 * count :]):
         for h in range(out.shape[1] // DH):
             out[:, head_cols(h)] = stacked(ids_ref, (mine, there), h)
+
+
+def stack_turned_body(ids_ref, q_ref, g_ref, q_there, g_there, q_out, g_out):
+    for h in range(q_out.shape[1] // DH):
+        q_out[:, head_cols(h)] = stacked(ids_ref, (q_ref, q_there), h)
+        g_out[head_cols(h)] = jnp.transpose(stacked(ids_ref, (g_ref, g_there), h))
 
 
 def context_body(land_ref, k_ref, v_ref, out_ref):
@@ -294,21 +306,26 @@
         exp_ref[h, tok:] = jnp.broadcast_to(shift, (16, M)).astype(BF16)
 
 
+def gain_column(ids_ref, gain_ref, h):
+    row = jnp.broadcast_to(gain_ref[:, own_head(ids_ref, h)], (8, DH))
+    return jnp.transpose(row)[:, 0:1]
+
+
 def output_body(ids_ref, kone_ref, mix_ref, g_ref, gain_ref, out_ref, sum_ref):
     heads, tok, _ = kone_ref.shape
-    squares = jnp.zeros((tok, DH), F32)
-    slopes = jnp.zeros((tok, DH), F32)
+    squares = jnp.zeros((DH, tok), F32)
+    slopes = jnp.zeros((DH, tok), F32)
     for h in range(heads):
-        out = dot(kone_ref[h], mix_ref[h], NT)
-        out_ref[:, head_cols(h)] = out
-        grad = g_ref[:, head_cols(h)].astype(F32)
+        out = dot(mix_ref[h], kone_ref[h], NT)
+        out_ref[head_cols(h)] = out
+        scaled = g_ref[head_cols(h)].astype(F32) * gain_column(ids_ref, gain_ref, h)
         squares = squares + out * out
-        slopes = slopes + grad * gain_ref[:, own_head(ids_ref, h)] * out
-    high, low = split_up(jnp.concatenate([squares, slopes], axis=0))
-    ones = jnp.ones((8, DH), BF16)
-    row = (dot(ones, high, NT) + dot(ones, low, NT))[0:1]
+        slopes = slopes + scaled * out
     both = rows_of(
-        swap_blocks(ids_ref, row[:, :tok], 1), swap_blocks(ids_ref, row[:, tok:], 1)
+        *[
+            swap_blocks(ids_ref, jnp.sum(part, axis=0, keepdims=True), 1)
+            for part in (squares, slopes)
+        ]
     )
     for place in range(sum_ref.shape[0]):
         sum_ref[place] = both[:2]
@@ -328,12 +345,7 @@
         total = total + sum_ref[place]
     root_inv = lax.rsqrt(total[0:1] / features + EPS)
     slope = total[1:2] * root_inv / features
-    columns = jnp.transpose(
-        rows_of(
-            swap_blocks(ids_ref, root_inv, 1), swap_blocks(ids_ref, root_inv * slope, 1)
-        )
-    )
-    return columns[:, 0:1], columns[:, 1:2]
+    return swap_blocks(ids_ref, root_inv, 1), swap_blocks(ids_ref, root_inv * slope, 1)
 
 
 def output_grad(factors, out, grad, gain):
@@ -347,11 +359,12 @@
     cols = DH // per_head
     factors = token_factors(ids_ref, sum_ref, heads * DH * sum_ref.shape[0])
     for h in range(heads):
-        out = out_ref[:, head_cols(h)]
-        grad = g_ref[:, head_cols(h)].astype(F32)
-        gain = gain_ref[:, own_head(ids_ref, h)]
-        g_mixing = dot(output_grad(factors, out, grad, gain), kone_ref[h], TN)
-        gain_sum = jnp.sum(grad * (out * factors[0]), axis=0, keepdims=True)
+        out = out_ref[head_cols(h)]
+        grad = g_ref[head_cols(h)].astype(F32)
+        gain = gain_column(ids_ref, gain_ref, h)
+        g_mixing = dot(output_grad(factors, out, grad, gain), kone_ref[h])
+        gain_sum = jnp.sum(grad * (out * factors[0]), axis=1, keepdims=True)
+        gain_sum = jnp.transpose(jnp.broadcast_to(gain_sum, (DH, DH)))[0:1]
         tail = rows_of(*high_low(gain_sum))
         for j in range(per_head):
             part_ref[h * per_head + j] = jnp.concatenate(
@@ -367,14 +380,14 @@
     tok = mine_ref.shape[1]
     factors = token_factors(ids_ref, sum_ref, heads * DH * sum_ref.shape[0])
     for h in range(heads):
-        out = out_ref[:, head_cols(h)]
-        grad = g_ref[:, head_cols(h)].astype(F32)
-        gain = gain_ref[:, own_head(ids_ref, h)]
-        normed = (out * factors[0] * gain).astype(BF16)
+        out = out_ref[head_cols(h)]
+        grad = g_ref[head_cols(h)].astype(F32)
+        gain = gain_column(ids_ref, gain_ref, h)
+        normed = jnp.transpose(out * factors[0] * gain).astype(BF16)
         mine_ref[0, :, head_cols(h)] = normed[:tok]
         other_ref[0, :, head_cols(h)] = normed[tok:]
         kone = kernel_one(q_ref, land_ref, h)
-        g_kernel = dot(output_grad(factors, out, grad, gain), mix_ref[h])
+        g_kernel = dot(output_grad(factors, out, grad, gain), mix_ref[h], TN)
         inner = jnp.sum(kone * g_kernel, axis=1, keepdims=True)
         g_score = (kone * (g_kernel - inner)).astype(BF16)
         query = dot(g_score, land_ref[:, head_cols(heads + h)]) * SCALE
@@ -601,6 +614,7 @@
     units = shape(heads, 2 * tok, M, dtype=BF16)
 
     both_b = shape(2 * tok, half, dtype=BF16)
+    turned_b = shape(half, 2 * tok, dtype=BF16)
     (own,) = call(
         means_body, [shape(n_ctx, land_dev, 2 * half, dtype=BF16)], queries, keys_in,
         far_in=(0, 1), far_out=(0,), vmem=MOST_VMEM, flops=10**6, name="landmark_means",
@@ -624,7 +638,7 @@
         got, inverse, flops=10**8, name="mixing",
     )
     qs, grads = call(
-        stack_body, [both_b, both_b], ids, queries, out_grad, q_there, g_there,
+        stack_turned_body, [both_b, turned_b], ids, queries, out_grad, q_there, g_there,
         scalars=1, after=(parts,), flops=10**6, name="stack_qg",
     )
     kone, exp_local = call(
@@ -634,7 +648,7 @@
     mixing = exchange(parts, "ctx", same_core).reshape(heads, DH, M)
 
     output, sums = call(
-        output_body, [shape(2 * tok, half), shape(2 * n_head, 2, 2 * tok)],
+        output_body, [shape(half, 2 * tok), shape(2 * n_head, 2, 2 * tok)],
         ids, kone, mixing, grads, gain, scalars=1, flops=10**8, name="output",
     )
     sums = exchange(sums, ("ctx", "head"), same_chip)

time: 108 us -> 108 us (level)
  Pallas kernels: 26.2 us -> 25.1 us
where the time goes in v6:
time: 108 us; the launch traced here: 107 us
  starting transfers between devices  32.9 us (30%)
  Pallas kernels  25.1 us (23%)
  waiting for transfers between devices  22 us (20%)
  blocking collectives  17.4 us (16%)
  local copies, waits for them, and re-layouts  8.22 us (8%)
    all_to_all x6, starting transfers between devices, exchange(): return lax.all_to_all(parts, axis, 0, 0, axis_index_groups=groups)  25.7 us
    pallas_call x16, Pallas kernels, call(): pl.pallas_call(whole, out_shape=outs, in_specs=in_specs, out_specs=[space...  25.1 us
    all_to_all x6, waiting for transfers between devices, exchange(): return lax.all_to_all(parts, axis, 0, 0, axis_index_groups=groups)  22 us
    all_to_all x1, blocking collectives, exchange(): return lax.all_to_all(parts, axis, 0, 0, axis_index_groups=groups)  17.4 us
    unnamed x30, local copies, waits for them, and re-layouts  8.22 us
    ppermute x4, starting transfers between devices, on_device(): lax.ppermute(x, 'ctx', swap)  4.03 us
    ppermute x1, starting transfers between devices, on_device(): passed_there = lax.ppermute(passed, 'ctx', swap)  3.19 us
  transfers between devices with their start and end apart: 12, of which 6 were waited for; matrix products, arithmetic and copies ran while one was open for 0% of the time, Pallas kernels for 16%

profile of v6, /device:TPU:1, one launch (start us, length us, event | category | flops | bytes accessed | tf_op | source)
XLA Modules:
  0.0 106.7 jit_solution(1133858026914197223)
XLA Ops:
  0.6 1.9 %landmark_means.1.refs_5_ = bf16[32,8,512]{2,1,0:T(8,128)(2,1)} custom-call(bf16[256,512]{1,0:T(8,128)(2,1)} %refs_1_.6, bf16[256,512]{1,0:T(8,128)(2,1)} %refs_1_.7), custom_call_target="tpu_custom_call" | custom-call | flops 1000000 | bytes 786432 | tf_op jit(solution)/shard_map/landmark_means/pallas_call | solution.py:165
  2.5 3.3 %collective-permute-start.2 = (bf16[256,512]{1,0:T(8,128)(2,1)}, bf16[256,512]{1,0:T(8,128)(2,1)S(1)}, u32[]{:S(2)}, u32[]{:S(2)}) collective-permute-start(bf16[256,512]{1,0:T(8,128)(2,1)} %refs_1_.7), channel_id=1, source_target_pairs={{0,8},{8,0},{16,24},{24,16},{32,40},{40,32},{48,56},{56,48},{64,72... | collective-permute-start | bytes 786440 | tf_op jit(solution)/shard_map/ppermute | solution.py:623
  6.0 5.8 %all-to-all-start = ((bf16[32,8,512]{2,1,0:T(8,128)(2,1)}), bf16[32,8,512]{2,1,0:T(8,128)(2,1)S(1)}, u32[]{:S(2)}, u32[]{:S(2)}) async-start(bf16[32,8,512]{2,1,0:T(8,128)(2,1)} %landmark_means.1.refs_5_), calls=%async_computation | async-start | bytes 524288 | tf_op jit(solution)/shard_map/all_to_all | solution.py:47
  12.4 0.9 copy-done
  13.4 0.9 copy-done.1
  14.3 0.9 copy-done.5
  15.9 4.8 %all-to-all-done = bf16[32,8,512]{2,1,0:T(8,128)(2,1)S(1)} async-done(((bf16[32,8,512]{2,1,0:T(8,128)(2,1)}), bf16[32,8,512]{2,1,0:T(8,128)(2,1)S(1)}, u32[]{:S(2)}, u32[]{:S(2)}) %all-to-all-start) | async-done | bytes 262176 | tf_op jit(solution)/shard_map/all_to_all | solution.py:47
  20.7 1.6 %local_context.1.refs_2_ = bf16[16,40,128]{2,1,0:T(8,128)(2,1)} custom-call(bf16[256,512]{1,0:T(8,128)(2,1)S(1)} %bitcast.7, bf16[512,256]{1,0:T(8,128)(2,1)S(1)} %get-tuple-element.38.refs_1_.refs_2_, bf16[512,256]{1,0:T(8,128)(2,1)S(1)} %get-tuple-element.39.refs_2_.refs_3_), custom_call_target="tpu_custom_call" | custom-call | flops 100000000 | bytes 950272 | tf_op jit(solution)/shard_map/local_context/pallas_call | solution.py:165
  22.4 3.5 %all-to-all-start.1 = ((bf16[16,40,128]{2,1,0:T(8,128)(2,1)}), bf16[16,40,128]{2,1,0:T(8,128)(2,1)S(1)}, u32[]{:S(2)}, u32[]{:S(2)}) async-start(bf16[16,40,128]{2,1,0:T(8,128)(2,1)} %local_context.1.refs_2_), calls=%async_computation.1 | async-start | bytes 327680 | tf_op jit(solution)/shard_map/all_to_all | solution.py:47
  25.9 3.1 %inverse.1 = (f32[256,256]{1,0:T(8,128)S(1)}, f32[256,256]{1,0:T(8,128)S(1)}, f32[7,256,256]{2,1,0:T(8,128)S(1)}) custom-call(s32[2]{0:T(128)S(1)} %pad_add_fusion.refs_0_, bf16[256,512]{1,0:T(8,128)(2,1)S(1)} %bitcast.8, bf16[16,40,128]{2,1,0:T(8,128)(2,1)} %local_context.1.refs_2_), custom_call_target="tpu_custom_call" | custom-call | flops 3000000000 | bytes 2621448 | tf_op jit(solution)/shard_map/inverse/pallas_call | solution.py:165
  29.1 1.2 %copy-done.11 = f32[7,256,256]{2,1,0:T(8,128)} copy-done((f32[7,256,256]{2,1,0:T(8,128)}, f32[7,256,256]{2,1,0:T(8,128)S(1)}, u32[]{:S(2)}) %copy-start.11) | copy-done | bytes 1835032
  30.3 2.5 %all-to-all-done.1.refs_0_ = bf16[16,40,128]{2,1,0:T(8,128)(2,1)S(1)} async-done(((bf16[16,40,128]{2,1,0:T(8,128)(2,1)}), bf16[16,40,128]{2,1,0:T(8,128)(2,1)S(1)}, u32[]{:S(2)}, u32[]{:S(2)}) %all-to-all-start.1) | async-done | bytes 163872 | tf_op jit(solution)/shard_map/all_to_all | solution.py:47
  33.7 4.1 %all-to-all-start.2 = ((bf16[16,16,256]{2,1,0:T(8,128)(2,1)}), bf16[16,16,256]{2,1,0:T(8,128)(2,1)S(1)}, u32[]{:S(2)}, u32[]{:S(2)}) async-start(bf16[16,16,256]{2,1,0:T(8,128)(2,1)} %get-tuple-element.41.refs_5_.refs_3_), calls=%async_computation.2 | async-start | bytes 262144 | tf_op jit(solution)/shard_map/all_to_all | solution.py:47
  39.4 5.2 %all-to-all-done.2 = bf16[16,16,256]{2,1,0:T(8,128)(2,1)S(1)} async-done(((bf16[16,16,256]{2,1,0:T(8,128)(2,1)}), bf16[16,16,256]{2,1,0:T(8,128)(2,1)S(1)}, u32[]{:S(2)}, u32[]{:S(2)}) %all-to-all-start.2) | async-done | bytes 131104 | tf_op jit(solution)/shard_map/all_to_all | solution.py:47
  45.5 17.4 %all_to_all.35.refs_1_ = f32[16,2,512]{2,1,0:T(2,128)S(1)} all-to-all(f32[16,2,512]{2,1,0:T(2,128)S(1)} %get-tuple-element.45), channel_id=1, replica_groups={{0,1,2,3,4,5,6,7,8,9,10,11,12,13,14,15},{16,17,18,19,20,21,22,23,24,25,..., dimensions={0} | all-to-all | bytes 131072 | tf_op jit(solution)/shard_map/all_to_all | solution.py:47
  63.0 1.7 %norm.1.refs_8_ = bf16[16,40,128]{2,1,0:T(8,128)(2,1)} custom-call(s32[2]{0:T(128)S(1)} %pad_add_fusion.refs_0_, f32[16,2,512]{2,1,0:T(2,128)S(1)} %all_to_all.35.refs_1_, f32[256,512]{1,0:T(8,128)S(1)} %get-tuple-element.46.refs_2_, bf16[256,512]{1,0:T(8,128)(2,1)S(1)} %get-tuple-element.44.refs_3_, f32[1,512]{1,0:T(1,128)S(1)} %bitcast.16, ...), custom_call_target="tpu_custom_call" | custom-call | flops 100000000 | bytes 1542152 | tf_op jit(solution)/shard_map/norm/pallas_call | solution.py:165
  64.6 3.5 %all-to-all-start.4 = ((bf16[16,40,128]{2,1,0:T(8,128)(2,1)}), bf16[16,40,128]{2,1,0:T(8,128)(2,1)S(1)}, u32[]{:S(2)}, u32[]{:S(2)}) async-start(bf16[16,40,128]{2,1,0:T(8,128)(2,1)} %norm.1.refs_8_), calls=%async_computation.4 | async-start | bytes 327680 | tf_op jit(solution)/shard_map/all_to_all | solution.py:47
  68.2 0.9 copy-done.10
  69.1 2.1 %kernel_one_back.1 = (bf16[2,256,256]{2,1,0:T(8,128)(2,1)S(1)}, bf16[2,256,256]{2,1,0:T(8,128)(2,1)S(1)}, f32[256,256]{1,0:T(8,128)S(1)}) custom-call(s32[2]{0:T(128)S(1)} %pad_add_fusion.refs_0_, f32[16,2,512]{2,1,0:T(2,128)S(1)} %all_to_all.35.refs_1_, f32[256,512]{1,0:T(8,128)S(1)} %get-tuple-element.46.refs_2_, ...), custom_call_target="tpu_custom_call" | custom-call | flops 2000000000 | bytes 2295816 | tf_op jit(solution)/shard_map/kernel_one_back/pallas_call | solution.py:165
  71.9 3.1 %all-to-all-done.4.refs_0_ = bf16[16,40,128]{2,1,0:T(8,128)(2,1)S(1)} async-done(((bf16[16,40,128]{2,1,0:T(8,128)(2,1)}), bf16[16,40,128]{2,1,0:T(8,128)(2,1)S(1)}, u32[]{:S(2)}, u32[]{:S(2)}) %all-to-all-start.4) | async-done | bytes 163872 | tf_op jit(solution)/shard_map/all_to_all | solution.py:47
  75.9 3.6 %all-to-all-start.5 = ((bf16[16,40,128]{2,1,0:T(8,128)(2,1)}), bf16[16,40,128]{2,1,0:T(8,128)(2,1)S(1)}, u32[]{:S(2)}, u32[]{:S(2)}) async-start(bf16[16,40,128]{2,1,0:T(8,128)(2,1)} %get-tuple-element.51.refs_6_), calls=%async_computation.5 | async-start | bytes 327680 | tf_op jit(solution)/shard_map/all_to_all | solution.py:47
  79.5 1.5 %copy-done.12 = f32[7,256,256]{2,1,0:T(8,128)S(1)} copy-done((f32[7,256,256]{2,1,0:T(8,128)S(1)}, f32[7,256,256]{2,1,0:T(8,128)}, u32[]{:S(2)}) %copy-start.12) | copy-done | bytes 1835032
  81.0 0.9 copy-done.14
  82.0 2.9 %inverse_back.1.refs_4_ = f32[256,512]{1,0:T(8,128)S(1)} custom-call(s32[2]{0:T(128)S(1)} %pad_add_fusion.refs_0_, f32[7,256,256]{2,1,0:T(8,128)S(1)} %copy-done.12, f32[24,256]{1,0:T(8,128)S(1)} %get-tuple-element.50.refs_2_, f32[16,256]{1,0:T(8,128)S(1)} %get-tuple-element.54.refs_3_, bf16[256,512]{1,0:T(8,128)(2,1)S(1)} %bitcast.11, ...), custom_call_target="tpu_custom_call" | custom-call | flops 5000000000 | bytes 2924552 | tf_op jit(solution)/shard_map/inverse_back/pallas_call | solution.py:165
  84.9 1.5 %all-to-all-done.5.refs_0_ = bf16[16,40,128]{2,1,0:T(8,128)(2,1)S(1)} async-done(((bf16[16,40,128]{2,1,0:T(8,128)(2,1)}), bf16[16,40,128]{2,1,0:T(8,128)(2,1)S(1)}, u32[]{:S(2)}, u32[]{:S(2)}) %all-to-all-start.5) | async-done | bytes 163872 | tf_op jit(solution)/shard_map/all_to_all | solution.py:47
  86.4 1.4 %landmarks_back.1 = (bf16[256,512]{1,0:T(8,128)(2,1)}, bf16[1152,128]{1,0:T(8,128)(2,1)}) custom-call(bf16[16,40,128]{2,1,0:T(8,128)(2,1)S(1)} %all-to-all-done.5.refs_0_, bf16[2,528,256]{2,1,0:T(8,128)(2,1)S(1)} %get-tuple-element.52.refs_1_, bf16[512,256]{1,0:T(8,128)(2,1)S(1)} %get-tuple-element.38.refs_1_.refs_2_, ...), custom_call_target="tpu_custom_call" | custom-call | flops 100000000 | bytes 2572288 | tf_op jit(solution)/shard_map/landmarks_back/pallas_call | solution.py:165
  87.8 3.2 %collective-permute-start.5 = (bf16[1152,128]{1,0:T(8,128)(2,1)}, bf16[1152,128]{1,0:T(8,128)(2,1)S(1)}, u32[]{:S(2)}, u32[]{:S(2)}) collective-permute-start(bf16[1152,128]{1,0:T(8,128)(2,1)} %get-tuple-element.57.refs_3_), channel_id=1, source_target_pairs={{0,8},{8,0},{16,24},{24,16},{32,40},{40,32},{48,56},{56,48},{64,72... | collective-permute-start | bytes 884744 | tf_op jit(solution)/shard_map/ppermute | solution.py:681
  91.0 5.3 %all-to-all-start.6 = ((bf16[32,8,512]{2,1,0:T(8,128)(2,1)}), bf16[32,8,512]{2,1,0:T(8,128)(2,1)S(1)}, u32[]{:S(2)}, u32[]{:S(2)}) async-start(bf16[32,8,512]{2,1,0:T(8,128)(2,1)} %bitcast.5), calls=%async_computation.6 | async-start | bytes 524288 | tf_op jit(solution)/shard_map/all_to_all | solution.py:47
  96.3 1.3 %gather.1.refs_5_ = bf16[256,512]{1,0:T(8,128)(2,1)} custom-call(s32[2]{0:T(128)S(1)} %pad_add_fusion.refs_0_, bf16[2,256,256]{2,1,0:T(8,128)(2,1)S(1)} %get-tuple-element.47.refs_1_.refs_2_, bf16[2,256,256]{2,1,0:T(8,128)(2,1)S(1)} %collective-permute-done.4.refs_2_.refs_3_, bf16[256,512]{1,0:T(8,128)(2,1)} %get-tuple-element.56.refs_3_.refs_5_), custom_call_target="tpu_custom_call" | custom-call | flops 1000000 | bytes 786440 | tf_op jit(solution)/shard_map/gather/pallas_call | solution.py:165
  97.6 2.8 %kernel_three_back.1 = (bf16[256,512]{1,0:T(8,128)(2,1)}, f32[256,512]{1,0:T(8,128)S(1)}, f32[1,512]{1,0:T(1,128)}) custom-call(s32[2]{0:T(128)S(1)} %pad_add_fusion.refs_0_, bf16[256,512]{1,0:T(8,128)(2,1)S(1)} %copy-done.2, bf16[256,512]{1,0:T(8,128)(2,1)S(1)} %copy-done.6, bf16[1152,128]{1,0:T(8,128)(2,1)} %get-tuple-element.57.refs_3_, ...), custom_call_target="tpu_custom_call" | custom-call | flops 2000000000 | bytes 1902600 | tf_op jit(solution)/shard_map/kernel_three_back/pallas_call | solution.py:165
  100.4 4.9 %all-to-all-done.6.refs_1_ = bf16[32,8,512]{2,1,0:T(8,128)(2,1)S(1)} async-done(((bf16[32,8,512]{2,1,0:T(8,128)(2,1)}), bf16[32,8,512]{2,1,0:T(8,128)(2,1)S(1)}, u32[]{:S(2)}, u32[]{:S(2)}) %all-to-all-start.6) | async-done | bytes 262176 | tf_op jit(solution)/shard_map/all_to_all | solution.py:47
  105.3 1.4 %finish.1 = (bf16[256,512]{1,0:T(8,128)(2,1)}, bf16[256,512]{1,0:T(8,128)(2,1)}) custom-call(s32[2]{0:T(128)S(1)} %pad_add_fusion.refs_0_, bf16[32,8,512]{2,1,0:T(8,128)(2,1)S(1)} %all-to-all-done.6.refs_1_, bf16[2,256,256]{2,1,0:T(8,128)(2,1)S(1)} %get-tuple-element.47.refs_1_.refs_2_, bf16[2,256,256]{2,1,0:T(8,128)(2,1)S(1)} %collective-permute-done.4.refs_2_.refs_3_, ...), custom_call_target="tpu_custom_call" | custom-call | flops 1000000 | bytes 1835016 | tf_op jit(solution)/shard_map/finish/pallas_call | solution.py:165
  (40 shorter events, 6.4 us)
Async XLA Ops:
  2.5 9.9 %collective-permute-start.2 = (bf16[256,512]{1,0:T(8,128)(2,1)}, bf16[256,512]{1,0:T(8,128)(2,1)S(1)}, u32[]{:S(2)}, u32[]{:S(2)}) collective-permute-start(bf16[256,512]{1,0:T(8,128)(2,1)} %refs_1_.7), channel_id=1, source_target_pairs={{0,8},{8,0},{16,24},{24,16},{32,40},{40,32},{48,56},{56,48},{64,72... | collective-permute-start | bytes 786440 | tf_op jit(solution)/shard_map/ppermute | solution.py:623
  5.9 6.5 %collective-permute-start.3 = (bf16[256,512]{1,0:T(8,128)(2,1)}, bf16[256,512]{1,0:T(8,128)(2,1)S(1)}, u32[]{:S(2)}, u32[]{:S(2)}) collective-permute-start(bf16[256,512]{1,0:T(8,128)(2,1)} %refs_2_.5), channel_id=1, source_target_pairs={{0,8},{8,0},{16,24},{24,16},{32,40},{40,32},{48,56},{56,48},{64,72... | collective-permute-start | bytes 786440 | tf_op jit(solution)/shard_map/ppermute | solution.py:623
  6.0 14.8 %all-to-all-start = ((bf16[32,8,512]{2,1,0:T(8,128)(2,1)}), bf16[32,8,512]{2,1,0:T(8,128)(2,1)S(1)}, u32[]{:S(2)}, u32[]{:S(2)}) async-start(bf16[32,8,512]{2,1,0:T(8,128)(2,1)} %landmark_means.1.refs_5_), calls=%async_computation | async-start | bytes 524288 | tf_op jit(solution)/shard_map/all_to_all | solution.py:47
  11.7 26.0 %collective-permute-start = (bf16[256,512]{1,0:T(8,128)(2,1)}, bf16[256,512]{1,0:T(8,128)(2,1)S(1)}, u32[]{:S(2)}, u32[]{:S(2)}) collective-permute-start(bf16[256,512]{1,0:T(8,128)(2,1)} %refs_1_.6), channel_id=1, source_target_pairs={{0,8},{8,0},{16,24},{24,16},{32,40},{40,32},{48,56},{56,48},{64,72... | collective-permute-start | bytes 786440 | tf_op jit(solution)/shard_map/ppermute | solution.py:623
  12.1 25.7 %collective-permute-start.1 = (bf16[256,512]{1,0:T(8,128)(2,1)}, bf16[256,512]{1,0:T(8,128)(2,1)S(1)}, u32[]{:S(2)}, u32[]{:S(2)}) collective-permute-start(bf16[256,512]{1,0:T(8,128)(2,1)} %refs_2_.4), channel_id=1, source_target_pairs={{0,8},{8,0},{16,24},{24,16},{32,40},{40,32},{48,56},{56,48},{64,72... | collective-permute-start | bytes 786440 | tf_op jit(solution)/shard_map/ppermute | solution.py:623
  12.4 1.0 copy-start
  13.4 0.9 copy-start.1
  14.3 0.9 copy-start.5
  22.4 10.4 %all-to-all-start.1 = ((bf16[16,40,128]{2,1,0:T(8,128)(2,1)}), bf16[16,40,128]{2,1,0:T(8,128)(2,1)S(1)}, u32[]{:S(2)}, u32[]{:S(2)}) async-start(bf16[16,40,128]{2,1,0:T(8,128)(2,1)} %local_context.1.refs_2_), calls=%async_computation.1 | async-start | bytes 327680 | tf_op jit(solution)/shard_map/all_to_all | solution.py:47
  25.9 11.9 %copy-start.3 = (bf16[256,512]{1,0:T(8,128)(2,1)S(1)}, bf16[256,512]{1,0:T(8,128)(2,1)}, u32[]{:S(2)}) copy-start(bf16[256,512]{1,0:T(8,128)(2,1)} %refs_1_.6) | copy-start | bytes 786436
  25.9 11.9 %copy-start.7 = (bf16[256,512]{1,0:T(8,128)(2,1)S(1)}, bf16[256,512]{1,0:T(8,128)(2,1)}, u32[]{:S(2)}) copy-start(bf16[256,512]{1,0:T(8,128)(2,1)} %refs_2_.4) | copy-start | bytes 786436
  29.0 1.3 %copy-start.11 = (f32[7,256,256]{2,1,0:T(8,128)}, f32[7,256,256]{2,1,0:T(8,128)S(1)}, u32[]{:S(2)}) copy-start(f32[7,256,256]{2,1,0:T(8,128)S(1)} %get-tuple-element.53.refs_1_) | copy-start | bytes 5505028
  33.7 10.9 %all-to-all-start.2 = ((bf16[16,16,256]{2,1,0:T(8,128)(2,1)}), bf16[16,16,256]{2,1,0:T(8,128)(2,1)S(1)}, u32[]{:S(2)}, u32[]{:S(2)}) async-start(bf16[16,16,256]{2,1,0:T(8,128)(2,1)} %get-tuple-element.41.refs_5_.refs_3_), calls=%async_computation.2 | async-start | bytes 262144 | tf_op jit(solution)/shard_map/all_to_all | solution.py:47
  38.5 0.9 copy-start.9
  38.5 6.1 %copy-start.8 = (f32[512]{0:T(512)S(1)}, f32[512]{0:T(512)}, u32[]{:S(2)}) copy-start(f32[512]{0:T(512)} %param.8) | copy-start | bytes 6148
  64.6 10.4 %all-to-all-start.4 = ((bf16[16,40,128]{2,1,0:T(8,128)(2,1)}), bf16[16,40,128]{2,1,0:T(8,128)(2,1)S(1)}, u32[]{:S(2)}, u32[]{:S(2)}) async-start(bf16[16,40,128]{2,1,0:T(8,128)(2,1)} %norm.1.refs_8_), calls=%async_computation.4 | async-start | bytes 327680 | tf_op jit(solution)/shard_map/all_to_all | solution.py:47
  68.2 1.0 copy-start.10
  71.2 0.7 copy-start.13
  75.9 10.5 %all-to-all-start.5 = ((bf16[16,40,128]{2,1,0:T(8,128)(2,1)}), bf16[16,40,128]{2,1,0:T(8,128)(2,1)S(1)}, u32[]{:S(2)}, u32[]{:S(2)}) async-start(bf16[16,40,128]{2,1,0:T(8,128)(2,1)} %get-tuple-element.51.refs_6_), calls=%async_computation.5 | async-start | bytes 327680 | tf_op jit(solution)/shard_map/all_to_all | solution.py:47
  79.5 1.5 %copy-start.12 = (f32[7,256,256]{2,1,0:T(8,128)S(1)}, f32[7,256,256]{2,1,0:T(8,128)}, u32[]{:S(2)}) copy-start(f32[7,256,256]{2,1,0:T(8,128)} %copy-done.11) | copy-start | bytes 5505028
  81.0 0.9 copy-start.14
  84.9 12.7 %copy-start.2 = (bf16[256,512]{1,0:T(8,128)(2,1)S(1)}, bf16[256,512]{1,0:T(8,128)(2,1)}, u32[]{:S(2)}) copy-start(bf16[256,512]{1,0:T(8,128)(2,1)} %refs_1_.7) | copy-start | bytes 786436
  84.9 12.7 %copy-start.6 = (bf16[256,512]{1,0:T(8,128)(2,1)S(1)}, bf16[256,512]{1,0:T(8,128)(2,1)}, u32[]{:S(2)}) copy-start(bf16[256,512]{1,0:T(8,128)(2,1)} %refs_2_.5) | copy-start | bytes 786436
  87.8 9.8 %collective-permute-start.5 = (bf16[1152,128]{1,0:T(8,128)(2,1)}, bf16[1152,128]{1,0:T(8,128)(2,1)S(1)}, u32[]{:S(2)}, u32[]{:S(2)}) collective-permute-start(bf16[1152,128]{1,0:T(8,128)(2,1)} %get-tuple-element.57.refs_3_), channel_id=1, source_target_pairs={{0,8},{8,0},{16,24},{24,16},{32,40},{40,32},{48,56},{56,48},{64,72... | collective-permute-start | bytes 884744 | tf_op jit(solution)/shard_map/ppermute | solution.py:681
  91.0 5.3 %collective-permute-start.4 = (bf16[2,256,256]{2,1,0:T(8,128)(2,1)S(1)}, bf16[2,256,256]{2,1,0:T(8,128)(2,1)S(1)}, u32[]{:S(2)}, u32[]{:S(2)}) collective-permute-start(bf16[2,256,256]{2,1,0:T(8,128)(2,1)S(1)} %get-tuple-element.48.refs_3_), channel_id=1, source_target_pairs={{0,8},{8,0},{16,24},{24,16},{32,40},{40,32},{48,56},{56,48},{64,72... | collective-permute-start | bytes 786440 | tf_op jit(solution)/shard_map/ppermute | solution.py:680
  91.0 14.3 %all-to-all-start.6 = ((bf16[32,8,512]{2,1,0:T(8,128)(2,1)}), bf16[32,8,512]{2,1,0:T(8,128)(2,1)S(1)}, u32[]{:S(2)}, u32[]{:S(2)}) async-start(bf16[32,8,512]{2,1,0:T(8,128)(2,1)} %bitcast.5), calls=%async_computation.6 | async-start | bytes 524288 | tf_op jit(solution)/shard_map/all_to_all | solution.py:47
  97.6 7.7 %copy-start.4 = (bf16[256,512]{1,0:T(8,128)(2,1)S(1)}, bf16[256,512]{1,0:T(8,128)(2,1)}, u32[]{:S(2)}) copy-start(bf16[256,512]{1,0:T(8,128)(2,1)} %gather.1.refs_5_) | copy-start | bytes 786436

commit v7 on v6

--- a/solution.py
+++ b/solution.py
@@ -394,7 +394,7 @@
         mine_ref[1, :, head_cols(h)] = query[:tok].astype(BF16)
         other_ref[1, :, head_cols(h)] = query[tok:].astype(BF16)
         queries = q_ref[:, head_cols(h)]
-        keyland_ref[:, head_cols(h)] = dot(g_score, queries, TN) * SCALE
+        keyland_ref[:, head_cols(h)] = (dot(g_score, queries, TN) * SCALE).astype(BF16)
 
 
 def grad_context_body(got_ref, inv_ref, kept_ref, out_ref, g_ref):
@@ -421,7 +421,7 @@
     g_ref[...] = g_mixing
 
 
-def inverse_back_body(ids_ref, inv_ref, kept_ref, g_ref, land_ref, keyland_ref, out_ref):
+def inverse_back_body(ids_ref, inv_ref, kept_ref, g_ref, land_ref, out_ref):
     half = land_ref.shape[1] // 2
     at = pl.multiple_of(ids_ref[1] * DH, DH)
     lq = land_ref[:, pl.ds(at, DH)]
@@ -451,13 +451,10 @@
         d_x + jnp.transpose(d_x), ktwo_s
     )
     g_score = ktwo * (d_ktwo - jnp.sum(ktwo * d_ktwo, axis=1, keepdims=True))
-    out_ref[:, :half] = jnp.zeros((M, half), F32)
-    out_ref[:, half:] = keyland_ref[...]
+    out_ref[...] = jnp.zeros((M, 2 * half), F32)
     high, low = split_up(g_score)
     out_ref[:, pl.ds(at, DH)] = (dot(high, lk) + dot(low, lk)) * SCALE
-    out_ref[:, pl.ds(at + half, DH)] = keyland_ref[:, pl.ds(at, DH)] + (
-        (dot(high, lq, TN) + dot(low, lq, TN)) * SCALE
-    )
+    out_ref[:, pl.ds(at + half, DH)] = (dot(high, lq, TN) + dot(low, lq, TN)) * SCALE
 
 
 def unpacked(got, h, heads):
@@ -481,7 +478,7 @@
 
 
 def queryland_body(
-    got_ref, exp_ref, k_ref, v_ref, extra_ref, land_ref, out_ref, pass_ref
+    got_ref, exp_ref, k_ref, v_ref, extra_ref, keyland_ref, land_ref, out_ref, pass_ref
 ):
     heads = exp_ref.shape[0]
     half = heads * DH
@@ -495,7 +492,7 @@
         g_score = (exp_three * (dot(vals, g_weighted) + g_totals)).astype(BF16)
         queryland = dot(g_score, keys, TN) * SCALE
         out_ref[:, head_cols(h)] = (queryland + extra_ref[:, head_cols(h)]).astype(BF16)
-    out_ref[:, half:] = extra_ref[:, half:].astype(BF16)
+    out_ref[:, half:] = (extra_ref[:, half:] + keyland_ref[...].astype(F32)).astype(BF16)
     count, rows, _ = got_ref.shape
     for place in range(count):
         pass_ref[place * rows : (place + 1) * rows] = got_ref[place]
@@ -658,7 +655,7 @@
     )
     got = exchange(parts, "ctx", same_core)
     mine, other, keyland = call(
-        query_body, [pair, pair, shape(M, half)],
+        query_body, [pair, pair, shape(M, half, dtype=BF16)],
         ids, sums, output, grads, gain, mixing, qs, land,
         scalars=1, after=(parts,), flops=2 * 10**9, name="kernel_one_back",
     )
@@ -668,13 +665,13 @@
     )
     got = exchange(parts, "ctx", same_core)
     (extra,) = call(
-        inverse_back_body, [shape(M, 2 * half)], ids, chain, kept, g_mixing, land, keyland,
+        inverse_back_body, [shape(M, 2 * half)], ids, chain, kept, g_mixing, land,
         scalars=1, after=(parts,), flops=5 * 10**9, name="inverse_back",
     )
     both, passed = call(
         queryland_body,
         [shape(M, 2 * half, dtype=BF16), shape(chips * (2 * cols + 8) + heads * M, DH, dtype=BF16)],
-        got, exp_local, keys, vals, extra, land, flops=10**8, name="landmarks_back",
+        got, exp_local, keys, vals, extra, keyland, land, flops=10**8, name="landmarks_back",
     )
     landed = exchange(both.reshape(n_ctx, land_dev, 2 * half), "ctx")
     there = lax.ppermute(other, "ctx", swap)

time: 108 us -> 107 us (level)
  waiting for transfers between devices: 22 us -> 23.7 us
  local copies, waits for them, and re-layouts: 8.22 us -> 6.57 us
    all_to_all x6, waiting for transfers between devices: 22 us -> 23.7 us  [exchange(): return lax.all_to_all(parts, axis, 0, 0, axis_index_groups=groups)]
    unnamed x30 -> x26, local copies, waits for them, and re-layouts: 8.22 us -> 6.57 us
where the time goes in v7:
time: 107 us; the launch traced here: 106 us
  starting transfers between devices  32 us (30%)
  Pallas kernels  25.1 us (23%)
  waiting for transfers between devices  23.7 us (22%)
  blocking collectives  17.4 us (16%)
  local copies, waits for them, and re-layouts  6.57 us (6%)
    pallas_call x16, Pallas kernels, call(): pl.pallas_call(whole, out_shape=outs, in_specs=in_specs, out_specs=[space...  25.1 us
    all_to_all x6, starting transfers between devices, exchange(): return lax.all_to_all(parts, axis, 0, 0, axis_index_groups=groups)  24.8 us
    all_to_all x6, waiting for transfers between devices, exchange(): return lax.all_to_all(parts, axis, 0, 0, axis_index_groups=groups)  23.7 us
    all_to_all x1, blocking collectives, exchange(): return lax.all_to_all(parts, axis, 0, 0, axis_index_groups=groups)  17.4 us
    unnamed x26, local copies, waits for them, and re-layouts  6.57 us
    ppermute x4, starting transfers between devices, on_device(): lax.ppermute(x, 'ctx', swap)  4.03 us
    ppermute x1, starting transfers between devices, on_device(): passed_there = lax.ppermute(passed, 'ctx', swap)  3.19 us
  transfers between devices with their start and end apart: 12, of which 6 were waited for; matrix products, arithmetic and copies ran while one was open for 0% of the time, Pallas kernels for 16%

profile of v7, /device:TPU:1, one launch (start us, length us, event | category | flops | bytes accessed | tf_op | source)
XLA Modules:
  0.0 105.8 jit_solution(14526363462087231704)
XLA Ops:
  0.6 1.9 %landmark_means.1.refs_5_ = bf16[32,8,512]{2,1,0:T(8,128)(2,1)} custom-call(bf16[256,512]{1,0:T(8,128)(2,1)} %refs_1_.6, bf16[256,512]{1,0:T(8,128)(2,1)} %refs_1_.7), custom_call_target="tpu_custom_call" | custom-call | flops 1000000 | bytes 786432 | tf_op jit(solution)/shard_map/landmark_means/pallas_call | solution.py:165
  2.5 3.3 %collective-permute-start.2 = (bf16[256,512]{1,0:T(8,128)(2,1)}, bf16[256,512]{1,0:T(8,128)(2,1)S(1)}, u32[]{:S(2)}, u32[]{:S(2)}) collective-permute-start(bf16[256,512]{1,0:T(8,128)(2,1)} %refs_1_.7), channel_id=1, source_target_pairs={{0,8},{8,0},{16,24},{24,16},{32,40},{40,32},{48,56},{56,48},{64,72... | collective-permute-start | bytes 786440 | tf_op jit(solution)/shard_map/ppermute | solution.py:620
  6.0 5.8 %all-to-all-start = ((bf16[32,8,512]{2,1,0:T(8,128)(2,1)}), bf16[32,8,512]{2,1,0:T(8,128)(2,1)S(1)}, u32[]{:S(2)}, u32[]{:S(2)}) async-start(bf16[32,8,512]{2,1,0:T(8,128)(2,1)} %landmark_means.1.refs_5_), calls=%async_computation | async-start | bytes 524288 | tf_op jit(solution)/shard_map/all_to_all | solution.py:47
  12.4 0.9 copy-done
  13.4 0.9 copy-done.1
  14.3 0.9 copy-done.5
  15.9 4.8 %all-to-all-done = bf16[32,8,512]{2,1,0:T(8,128)(2,1)S(1)} async-done(((bf16[32,8,512]{2,1,0:T(8,128)(2,1)}), bf16[32,8,512]{2,1,0:T(8,128)(2,1)S(1)}, u32[]{:S(2)}, u32[]{:S(2)}) %all-to-all-start) | async-done | bytes 262176 | tf_op jit(solution)/shard_map/all_to_all | solution.py:47
  20.7 1.6 %local_context.1.refs_2_ = bf16[16,40,128]{2,1,0:T(8,128)(2,1)} custom-call(bf16[256,512]{1,0:T(8,128)(2,1)S(1)} %bitcast.7, bf16[512,256]{1,0:T(8,128)(2,1)S(1)} %get-tuple-element.38.refs_1_.refs_2_, bf16[512,256]{1,0:T(8,128)(2,1)S(1)} %get-tuple-element.39.refs_2_.refs_3_), custom_call_target="tpu_custom_call" | custom-call | flops 100000000 | bytes 950272 | tf_op jit(solution)/shard_map/local_context/pallas_call | solution.py:165
  22.4 3.5 %all-to-all-start.1 = ((bf16[16,40,128]{2,1,0:T(8,128)(2,1)}), bf16[16,40,128]{2,1,0:T(8,128)(2,1)S(1)}, u32[]{:S(2)}, u32[]{:S(2)}) async-start(bf16[16,40,128]{2,1,0:T(8,128)(2,1)} %local_context.1.refs_2_), calls=%async_computation.1 | async-start | bytes 327680 | tf_op jit(solution)/shard_map/all_to_all | solution.py:47
  25.9 3.1 %inverse.1 = (f32[256,256]{1,0:T(8,128)S(1)}, f32[256,256]{1,0:T(8,128)S(1)}, f32[7,256,256]{2,1,0:T(8,128)S(1)}) custom-call(s32[2]{0:T(128)S(1)} %pad_add_fusion.refs_0_, bf16[256,512]{1,0:T(8,128)(2,1)S(1)} %bitcast.8, bf16[16,40,128]{2,1,0:T(8,128)(2,1)} %local_context.1.refs_2_), custom_call_target="tpu_custom_call" | custom-call | flops 3000000000 | bytes 2621448 | tf_op jit(solution)/shard_map/inverse/pallas_call | solution.py:165
  29.1 1.2 %copy-done.11 = f32[7,256,256]{2,1,0:T(8,128)} copy-done((f32[7,256,256]{2,1,0:T(8,128)}, f32[7,256,256]{2,1,0:T(8,128)S(1)}, u32[]{:S(2)}) %copy-start.11) | copy-done | bytes 1835032
  30.3 2.5 %all-to-all-done.1.refs_0_ = bf16[16,40,128]{2,1,0:T(8,128)(2,1)S(1)} async-done(((bf16[16,40,128]{2,1,0:T(8,128)(2,1)}), bf16[16,40,128]{2,1,0:T(8,128)(2,1)S(1)}, u32[]{:S(2)}, u32[]{:S(2)}) %all-to-all-start.1) | async-done | bytes 163872 | tf_op jit(solution)/shard_map/all_to_all | solution.py:47
  33.7 4.1 %all-to-all-start.2 = ((bf16[16,16,256]{2,1,0:T(8,128)(2,1)}), bf16[16,16,256]{2,1,0:T(8,128)(2,1)S(1)}, u32[]{:S(2)}, u32[]{:S(2)}) async-start(bf16[16,16,256]{2,1,0:T(8,128)(2,1)} %get-tuple-element.41.refs_5_.refs_3_), calls=%async_computation.2 | async-start | bytes 262144 | tf_op jit(solution)/shard_map/all_to_all | solution.py:47
  39.4 5.2 %all-to-all-done.2 = bf16[16,16,256]{2,1,0:T(8,128)(2,1)S(1)} async-done(((bf16[16,16,256]{2,1,0:T(8,128)(2,1)}), bf16[16,16,256]{2,1,0:T(8,128)(2,1)S(1)}, u32[]{:S(2)}, u32[]{:S(2)}) %all-to-all-start.2) | async-done | bytes 131104 | tf_op jit(solution)/shard_map/all_to_all | solution.py:47
  44.6 0.9 output.1
  45.5 17.4 %all_to_all.35.refs_1_ = f32[16,2,512]{2,1,0:T(2,128)S(1)} all-to-all(f32[16,2,512]{2,1,0:T(2,128)S(1)} %get-tuple-element.45), channel_id=1, replica_groups={{0,1,2,3,4,5,6,7,8,9,10,11,12,13,14,15},{16,17,18,19,20,21,22,23,24,25,..., dimensions={0} | all-to-all | bytes 131072 | tf_op jit(solution)/shard_map/all_to_all | solution.py:47
  63.0 1.7 %norm.1.refs_8_ = bf16[16,40,128]{2,1,0:T(8,128)(2,1)} custom-call(s32[2]{0:T(128)S(1)} %pad_add_fusion.refs_0_, f32[16,2,512]{2,1,0:T(2,128)S(1)} %all_to_all.35.refs_1_, f32[256,512]{1,0:T(8,128)S(1)} %get-tuple-element.46.refs_2_, bf16[256,512]{1,0:T(8,128)(2,1)S(1)} %get-tuple-element.44.refs_3_, f32[1,512]{1,0:T(1,128)S(1)} %bitcast.16, ...), custom_call_target="tpu_custom_call" | custom-call | flops 100000000 | bytes 1542152 | tf_op jit(solution)/shard_map/norm/pallas_call | solution.py:165
  64.6 3.5 %all-to-all-start.4 = ((bf16[16,40,128]{2,1,0:T(8,128)(2,1)}), bf16[16,40,128]{2,1,0:T(8,128)(2,1)S(1)}, u32[]{:S(2)}, u32[]{:S(2)}) async-start(bf16[16,40,128]{2,1,0:T(8,128)(2,1)} %norm.1.refs_8_), calls=%async_computation.4 | async-start | bytes 327680 | tf_op jit(solution)/shard_map/all_to_all | solution.py:47
  68.2 0.9 copy-done.10
  69.1 2.1 %kernel_one_back.1 = (bf16[2,256,256]{2,1,0:T(8,128)(2,1)S(1)}, bf16[2,256,256]{2,1,0:T(8,128)(2,1)S(1)}, bf16[256,256]{1,0:T(8,128)(2,1)S(1)}) custom-call(s32[2]{0:T(128)S(1)} %pad_add_fusion.refs_0_, f32[16,2,512]{2,1,0:T(2,128)S(1)} %all_to_all.35.refs_1_, f32[256,512]{1,0:T(8,128)S(1)} %get-tuple-element.46.refs_2_, ...), custom_call_target="tpu_custom_call" | custom-call | flops 2000000000 | bytes 2164744 | tf_op jit(solution)/shard_map/kernel_one_back/pallas_call | solution.py:165
  71.2 3.8 %all-to-all-done.4.refs_0_ = bf16[16,40,128]{2,1,0:T(8,128)(2,1)S(1)} async-done(((bf16[16,40,128]{2,1,0:T(8,128)(2,1)}), bf16[16,40,128]{2,1,0:T(8,128)(2,1)S(1)}, u32[]{:S(2)}, u32[]{:S(2)}) %all-to-all-start.4) | async-done | bytes 163872 | tf_op jit(solution)/shard_map/all_to_all | solution.py:47
  75.9 3.6 %all-to-all-start.5 = ((bf16[16,40,128]{2,1,0:T(8,128)(2,1)}), bf16[16,40,128]{2,1,0:T(8,128)(2,1)S(1)}, u32[]{:S(2)}, u32[]{:S(2)}) async-start(bf16[16,40,128]{2,1,0:T(8,128)(2,1)} %get-tuple-element.51.refs_5_), calls=%async_computation.5 | async-start | bytes 327680 | tf_op jit(solution)/shard_map/all_to_all | solution.py:47
  79.5 1.5 %copy-done.12 = f32[7,256,256]{2,1,0:T(8,128)S(1)} copy-done((f32[7,256,256]{2,1,0:T(8,128)S(1)}, f32[7,256,256]{2,1,0:T(8,128)}, u32[]{:S(2)}) %copy-start.12) | copy-done | bytes 1835032
  81.0 2.9 %inverse_back.1.refs_4_ = f32[256,512]{1,0:T(8,128)S(1)} custom-call(s32[2]{0:T(128)S(1)} %pad_add_fusion.refs_0_, f32[7,256,256]{2,1,0:T(8,128)S(1)} %copy-done.12, f32[24,256]{1,0:T(8,128)S(1)} %get-tuple-element.50.refs_2_, f32[16,256]{1,0:T(8,128)S(1)} %get-tuple-element.54.refs_3_, bf16[256,512]{1,0:T(8,128)(2,1)S(1)} %bitcast.11, ...), custom_call_target="tpu_custom_call" | custom-call | flops 5000000000 | bytes 2662408 | tf_op jit(solution)/shard_map/inverse_back/pallas_call | solution.py:165
  84.0 2.5 %all-to-all-done.5.refs_0_ = bf16[16,40,128]{2,1,0:T(8,128)(2,1)S(1)} async-done(((bf16[16,40,128]{2,1,0:T(8,128)(2,1)}), bf16[16,40,128]{2,1,0:T(8,128)(2,1)S(1)}, u32[]{:S(2)}, u32[]{:S(2)}) %all-to-all-start.5) | async-done | bytes 163872 | tf_op jit(solution)/shard_map/all_to_all | solution.py:47
  86.4 1.4 %landmarks_back.1 = (bf16[256,512]{1,0:T(8,128)(2,1)}, bf16[1152,128]{1,0:T(8,128)(2,1)}) custom-call(bf16[16,40,128]{2,1,0:T(8,128)(2,1)S(1)} %all-to-all-done.5.refs_0_, bf16[2,528,256]{2,1,0:T(8,128)(2,1)S(1)} %get-tuple-element.52.refs_1_, bf16[512,256]{1,0:T(8,128)(2,1)S(1)} %get-tuple-element.38.refs_1_.refs_2_, ...), custom_call_target="tpu_custom_call" | custom-call | flops 100000000 | bytes 2703360 | tf_op jit(solution)/shard_map/landmarks_back/pallas_call | solution.py:165
  87.8 3.2 %collective-permute-start.5 = (bf16[1152,128]{1,0:T(8,128)(2,1)}, bf16[1152,128]{1,0:T(8,128)(2,1)S(1)}, u32[]{:S(2)}, u32[]{:S(2)}) collective-permute-start(bf16[1152,128]{1,0:T(8,128)(2,1)} %get-tuple-element.57.refs_3_), channel_id=1, source_target_pairs={{0,8},{8,0},{16,24},{24,16},{32,40},{40,32},{48,56},{56,48},{64,72... | collective-permute-start | bytes 884744 | tf_op jit(solution)/shard_map/ppermute | solution.py:678
  91.0 4.3 %all-to-all-start.6 = ((bf16[32,8,512]{2,1,0:T(8,128)(2,1)}), bf16[32,8,512]{2,1,0:T(8,128)(2,1)S(1)}, u32[]{:S(2)}, u32[]{:S(2)}) async-start(bf16[32,8,512]{2,1,0:T(8,128)(2,1)} %bitcast.5), calls=%async_computation.6 | async-start | bytes 524288 | tf_op jit(solution)/shard_map/all_to_all | solution.py:47
  95.4 1.3 %gather.1.refs_5_ = bf16[256,512]{1,0:T(8,128)(2,1)} custom-call(s32[2]{0:T(128)S(1)} %pad_add_fusion.refs_0_, bf16[2,256,256]{2,1,0:T(8,128)(2,1)S(1)} %get-tuple-element.47.refs_1_.refs_2_, bf16[2,256,256]{2,1,0:T(8,128)(2,1)S(1)} %collective-permute-done.4.refs_2_.refs_3_, bf16[256,512]{1,0:T(8,128)(2,1)} %get-tuple-element.56.refs_3_.refs_5_), custom_call_target="tpu_custom_call" | custom-call | flops 1000000 | bytes 786440 | tf_op jit(solution)/shard_map/gather/pallas_call | solution.py:165
  96.6 2.8 %kernel_three_back.1 = (bf16[256,512]{1,0:T(8,128)(2,1)}, f32[256,512]{1,0:T(8,128)S(1)}, f32[1,512]{1,0:T(1,128)}) custom-call(s32[2]{0:T(128)S(1)} %pad_add_fusion.refs_0_, bf16[256,512]{1,0:T(8,128)(2,1)S(1)} %copy-done.2, bf16[256,512]{1,0:T(8,128)(2,1)S(1)} %copy-done.6, bf16[1152,128]{1,0:T(8,128)(2,1)} %get-tuple-element.57.refs_3_, ...), custom_call_target="tpu_custom_call" | custom-call | flops 2000000000 | bytes 1902600 | tf_op jit(solution)/shard_map/kernel_three_back/pallas_call | solution.py:165
  99.4 4.9 %all-to-all-done.6.refs_1_ = bf16[32,8,512]{2,1,0:T(8,128)(2,1)S(1)} async-done(((bf16[32,8,512]{2,1,0:T(8,128)(2,1)}), bf16[32,8,512]{2,1,0:T(8,128)(2,1)S(1)}, u32[]{:S(2)}, u32[]{:S(2)}) %all-to-all-start.6) | async-done | bytes 262176 | tf_op jit(solution)/shard_map/all_to_all | solution.py:47
  104.3 1.4 %finish.1 = (bf16[256,512]{1,0:T(8,128)(2,1)}, bf16[256,512]{1,0:T(8,128)(2,1)}) custom-call(s32[2]{0:T(128)S(1)} %pad_add_fusion.refs_0_, bf16[32,8,512]{2,1,0:T(8,128)(2,1)S(1)} %all-to-all-done.6.refs_1_, bf16[2,256,256]{2,1,0:T(8,128)(2,1)S(1)} %get-tuple-element.47.refs_1_.refs_2_, bf16[2,256,256]{2,1,0:T(8,128)(2,1)S(1)} %collective-permute-done.4.refs_2_.refs_3_, ...), custom_call_target="tpu_custom_call" | custom-call | flops 1000000 | bytes 1835016 | tf_op jit(solution)/shard_map/finish/pallas_call | solution.py:165
  (36 shorter events, 4.8 us)
Async XLA Ops:
  2.5 9.9 %collective-permute-start.2 = (bf16[256,512]{1,0:T(8,128)(2,1)}, bf16[256,512]{1,0:T(8,128)(2,1)S(1)}, u32[]{:S(2)}, u32[]{:S(2)}) collective-permute-start(bf16[256,512]{1,0:T(8,128)(2,1)} %refs_1_.7), channel_id=1, source_target_pairs={{0,8},{8,0},{16,24},{24,16},{32,40},{40,32},{48,56},{56,48},{64,72... | collective-permute-start | bytes 786440 | tf_op jit(solution)/shard_map/ppermute | solution.py:620
  5.9 6.5 %collective-permute-start.3 = (bf16[256,512]{1,0:T(8,128)(2,1)}, bf16[256,512]{1,0:T(8,128)(2,1)S(1)}, u32[]{:S(2)}, u32[]{:S(2)}) collective-permute-start(bf16[256,512]{1,0:T(8,128)(2,1)} %refs_2_.5), channel_id=1, source_target_pairs={{0,8},{8,0},{16,24},{24,16},{32,40},{40,32},{48,56},{56,48},{64,72... | collective-permute-start | bytes 786440 | tf_op jit(solution)/shard_map/ppermute | solution.py:620
  6.0 14.8 %all-to-all-start = ((bf16[32,8,512]{2,1,0:T(8,128)(2,1)}), bf16[32,8,512]{2,1,0:T(8,128)(2,1)S(1)}, u32[]{:S(2)}, u32[]{:S(2)}) async-start(bf16[32,8,512]{2,1,0:T(8,128)(2,1)} %landmark_means.1.refs_5_), calls=%async_computation | async-start | bytes 524288 | tf_op jit(solution)/shard_map/all_to_all | solution.py:47
  11.7 26.0 %collective-permute-start = (bf16[256,512]{1,0:T(8,128)(2,1)}, bf16[256,512]{1,0:T(8,128)(2,1)S(1)}, u32[]{:S(2)}, u32[]{:S(2)}) collective-permute-start(bf16[256,512]{1,0:T(8,128)(2,1)} %refs_1_.6), channel_id=1, source_target_pairs={{0,8},{8,0},{16,24},{24,16},{32,40},{40,32},{48,56},{56,48},{64,72... | collective-permute-start | bytes 786440 | tf_op jit(solution)/shard_map/ppermute | solution.py:620
  12.1 25.7 %collective-permute-start.1 = (bf16[256,512]{1,0:T(8,128)(2,1)}, bf16[256,512]{1,0:T(8,128)(2,1)S(1)}, u32[]{:S(2)}, u32[]{:S(2)}) collective-permute-start(bf16[256,512]{1,0:T(8,128)(2,1)} %refs_2_.4), channel_id=1, source_target_pairs={{0,8},{8,0},{16,24},{24,16},{32,40},{40,32},{48,56},{56,48},{64,72... | collective-permute-start | bytes 786440 | tf_op jit(solution)/shard_map/ppermute | solution.py:620
  12.4 1.0 copy-start
  13.4 0.9 copy-start.1
  14.3 0.9 copy-start.5
  22.4 10.4 %all-to-all-start.1 = ((bf16[16,40,128]{2,1,0:T(8,128)(2,1)}), bf16[16,40,128]{2,1,0:T(8,128)(2,1)S(1)}, u32[]{:S(2)}, u32[]{:S(2)}) async-start(bf16[16,40,128]{2,1,0:T(8,128)(2,1)} %local_context.1.refs_2_), calls=%async_computation.1 | async-start | bytes 327680 | tf_op jit(solution)/shard_map/all_to_all | solution.py:47
  25.9 11.9 %copy-start.3 = (bf16[256,512]{1,0:T(8,128)(2,1)S(1)}, bf16[256,512]{1,0:T(8,128)(2,1)}, u32[]{:S(2)}) copy-start(bf16[256,512]{1,0:T(8,128)(2,1)} %refs_1_.6) | copy-start | bytes 786436
  25.9 11.9 %copy-start.7 = (bf16[256,512]{1,0:T(8,128)(2,1)S(1)}, bf16[256,512]{1,0:T(8,128)(2,1)}, u32[]{:S(2)}) copy-start(bf16[256,512]{1,0:T(8,128)(2,1)} %refs_2_.4) | copy-start | bytes 786436
  29.0 1.3 %copy-start.11 = (f32[7,256,256]{2,1,0:T(8,128)}, f32[7,256,256]{2,1,0:T(8,128)S(1)}, u32[]{:S(2)}) copy-start(f32[7,256,256]{2,1,0:T(8,128)S(1)} %get-tuple-element.53.refs_1_) | copy-start | bytes 5505028
  33.7 10.9 %all-to-all-start.2 = ((bf16[16,16,256]{2,1,0:T(8,128)(2,1)}), bf16[16,16,256]{2,1,0:T(8,128)(2,1)S(1)}, u32[]{:S(2)}, u32[]{:S(2)}) async-start(bf16[16,16,256]{2,1,0:T(8,128)(2,1)} %get-tuple-element.41.refs_5_.refs_3_), calls=%async_computation.2 | async-start | bytes 262144 | tf_op jit(solution)/shard_map/all_to_all | solution.py:47
  38.5 0.9 copy-start.9
  38.5 6.1 %copy-start.8 = (f32[512]{0:T(512)S(1)}, f32[512]{0:T(512)}, u32[]{:S(2)}) copy-start(f32[512]{0:T(512)} %param.8) | copy-start | bytes 6148
  64.6 10.4 %all-to-all-start.4 = ((bf16[16,40,128]{2,1,0:T(8,128)(2,1)}), bf16[16,40,128]{2,1,0:T(8,128)(2,1)S(1)}, u32[]{:S(2)}, u32[]{:S(2)}) async-start(bf16[16,40,128]{2,1,0:T(8,128)(2,1)} %norm.1.refs_8_), calls=%async_computation.4 | async-start | bytes 327680 | tf_op jit(solution)/shard_map/all_to_all | solution.py:47
  68.2 1.0 copy-start.10
  75.9 10.5 %all-to-all-start.5 = ((bf16[16,40,128]{2,1,0:T(8,128)(2,1)}), bf16[16,40,128]{2,1,0:T(8,128)(2,1)S(1)}, u32[]{:S(2)}, u32[]{:S(2)}) async-start(bf16[16,40,128]{2,1,0:T(8,128)(2,1)} %get-tuple-element.51.refs_5_), calls=%async_computation.5 | async-start | bytes 327680 | tf_op jit(solution)/shard_map/all_to_all | solution.py:47
  79.5 1.5 %copy-start.12 = (f32[7,256,256]{2,1,0:T(8,128)S(1)}, f32[7,256,256]{2,1,0:T(8,128)}, u32[]{:S(2)}) copy-start(f32[7,256,256]{2,1,0:T(8,128)} %copy-done.11) | copy-start | bytes 5505028
  86.4 10.2 %copy-start.2 = (bf16[256,512]{1,0:T(8,128)(2,1)S(1)}, bf16[256,512]{1,0:T(8,128)(2,1)}, u32[]{:S(2)}) copy-start(bf16[256,512]{1,0:T(8,128)(2,1)} %refs_1_.7) | copy-start | bytes 786436
  86.4 10.2 %copy-start.6 = (bf16[256,512]{1,0:T(8,128)(2,1)S(1)}, bf16[256,512]{1,0:T(8,128)(2,1)}, u32[]{:S(2)}) copy-start(bf16[256,512]{1,0:T(8,128)(2,1)} %refs_2_.5) | copy-start | bytes 786436
  87.8 8.8 %collective-permute-start.5 = (bf16[1152,128]{1,0:T(8,128)(2,1)}, bf16[1152,128]{1,0:T(8,128)(2,1)S(1)}, u32[]{:S(2)}, u32[]{:S(2)}) collective-permute-start(bf16[1152,128]{1,0:T(8,128)(2,1)} %get-tuple-element.57.refs_3_), channel_id=1, source_target_pairs={{0,8},{8,0},{16,24},{24,16},{32,40},{40,32},{48,56},{56,48},{64,72... | collective-permute-start | bytes 884744 | tf_op jit(solution)/shard_map/ppermute | solution.py:678
  91.0 4.3 %collective-permute-start.4 = (bf16[2,256,256]{2,1,0:T(8,128)(2,1)S(1)}, bf16[2,256,256]{2,1,0:T(8,128)(2,1)S(1)}, u32[]{:S(2)}, u32[]{:S(2)}) collective-permute-start(bf16[2,256,256]{2,1,0:T(8,128)(2,1)S(1)} %get-tuple-element.48.refs_3_), channel_id=1, source_target_pairs={{0,8},{8,0},{16,24},{24,16},{32,40},{40,32},{48,56},{56,48},{64,72... | collective-permute-start | bytes 786440 | tf_op jit(solution)/shard_map/ppermute | solution.py:677
  91.0 13.3 %all-to-all-start.6 = ((bf16[32,8,512]{2,1,0:T(8,128)(2,1)}), bf16[32,8,512]{2,1,0:T(8,128)(2,1)S(1)}, u32[]{:S(2)}, u32[]{:S(2)}) async-start(bf16[32,8,512]{2,1,0:T(8,128)(2,1)} %bitcast.5), calls=%async_computation.6 | async-start | bytes 524288 | tf_op jit(solution)/shard_map/all_to_all | solution.py:47
  96.6 7.7 %copy-start.4 = (bf16[256,512]{1,0:T(8,128)(2,1)S(1)}, bf16[256,512]{1,0:T(8,128)(2,1)}, u32[]{:S(2)}) copy-start(bf16[256,512]{1,0:T(8,128)(2,1)} %gather.1.refs_5_) | copy-start | bytes 786436

commit v8 on v7

--- a/solution.py
+++ b/solution.py
@@ -122,7 +122,7 @@
 
 def call(
     body, outs, *args, scalars=0, far_in=(), far_out=(), after=(), flops=0,
-    vmem=VMEM_BYTES, name
+    vmem=VMEM_BYTES, early=False, name
 ):
     nbytes = sum(a.size * a.dtype.itemsize for a in (*args, *outs))
     n_in, n_after, n_out = len(args), len(after), len(outs)
@@ -145,9 +145,12 @@
             copy.start()
         for copy in loads:
             copy.wait()
-        body(*ins, *results)
-        for copy in stores:
-            copy.start()
+        if early:
+            body(*ins, *results, [copy.start for copy in stores])
+        else:
+            body(*ins, *results)
+            for copy in stores:
+                copy.start()
         for copy in stores:
             copy.wait()
 
@@ -555,7 +558,7 @@
 
 
 def finish_body(
-    ids_ref, got_ref, mine_ref, there_ref, key_ref, query_out, key_out
+    ids_ref, got_ref, mine_ref, there_ref, key_ref, query_out, key_out, send
 ):
     count, land_dev, both = got_ref.shape
     _, tok, half = mine_ref.shape
@@ -578,12 +581,14 @@
                 ).astype(BF16)
 
     by_core(ids_ref, place_halves)
+    send[0]()
     for core in range(2):
         place = slice(core * half, (core + 1) * half)
         for row, span in spans:
             key_out[span, place] = (
                 key_ref[span, place] + lands[core][row : row + 1, half:]
             ).astype(BF16)
+    send[1]()
 
 
 def on_device(queries, keys_in, values, norm_gain, out_grad):
@@ -687,7 +692,7 @@
     )
     query_grad, key_grad = call(
         finish_body, [wide_b, wide_b], ids, landed, mine, there, key_three,
-        scalars=1, after=(normed,), flops=10**6, name="finish",
+        scalars=1, far_out=(0, 1), early=True, after=(normed,), flops=10**6, name="finish",
     )
     return (normed, query_grad, key_grad, value_grad, gain_grad.reshape(width))
 

time: 107 us -> 107 us (level)
  no operation moved by 1% of the time
where the time goes in v8:
time: 107 us; the launch traced here: 106 us
  starting transfers between devices  32 us (30%)
  Pallas kernels  25.1 us (23%)
  waiting for transfers between devices  23.7 us (22%)
  blocking collectives  17.4 us (16%)
  local copies, waits for them, and re-layouts  6.57 us (6%)
    pallas_call x16, Pallas kernels, call(): pl.pallas_call(whole, out_shape=outs, in_specs=in_specs, out_specs=[space...  25.1 us
    all_to_all x6, starting transfers between devices, exchange(): return lax.all_to_all(parts, axis, 0, 0, axis_index_groups=groups)  24.8 us
    all_to_all x6, waiting for transfers between devices, exchange(): return lax.all_to_all(parts, axis, 0, 0, axis_index_groups=groups)  23.7 us
    all_to_all x1, blocking collectives, exchange(): return lax.all_to_all(parts, axis, 0, 0, axis_index_groups=groups)  17.4 us
    unnamed x26, local copies, waits for them, and re-layouts  6.57 us
    ppermute x4, starting transfers between devices, on_device(): lax.ppermute(x, 'ctx', swap)  4.03 us
    ppermute x1, starting transfers between devices, on_device(): passed_there = lax.ppermute(passed, 'ctx', swap)  3.19 us
  transfers between devices with their start and end apart: 12, of which 6 were waited for; matrix products, arithmetic and copies ran while one was open for 0% of the time, Pallas kernels for 16%

profile of v8, /device:TPU:1, one launch (start us, length us, event | category | flops | bytes accessed | tf_op | source)
XLA Modules:
  0.0 105.9 jit_solution(8226939663286240481)
XLA Ops:
  0.6 1.9 %landmark_means.1.refs_5_ = bf16[32,8,512]{2,1,0:T(8,128)(2,1)} custom-call(bf16[256,512]{1,0:T(8,128)(2,1)} %refs_1_.6, bf16[256,512]{1,0:T(8,128)(2,1)} %refs_1_.7), custom_call_target="tpu_custom_call" | custom-call | flops 1000000 | bytes 786432 | tf_op jit(solution)/shard_map/landmark_means/pallas_call | solution.py:168
  2.5 3.3 %collective-permute-start.2 = (bf16[256,512]{1,0:T(8,128)(2,1)}, bf16[256,512]{1,0:T(8,128)(2,1)S(1)}, u32[]{:S(2)}, u32[]{:S(2)}) collective-permute-start(bf16[256,512]{1,0:T(8,128)(2,1)} %refs_1_.7), channel_id=1, source_target_pairs={{0,8},{8,0},{16,24},{24,16},{32,40},{40,32},{48,56},{56,48},{64,72... | collective-permute-start | bytes 786440 | tf_op jit(solution)/shard_map/ppermute | solution.py:625
  6.0 5.8 %all-to-all-start = ((bf16[32,8,512]{2,1,0:T(8,128)(2,1)}), bf16[32,8,512]{2,1,0:T(8,128)(2,1)S(1)}, u32[]{:S(2)}, u32[]{:S(2)}) async-start(bf16[32,8,512]{2,1,0:T(8,128)(2,1)} %landmark_means.1.refs_5_), calls=%async_computation | async-start | bytes 524288 | tf_op jit(solution)/shard_map/all_to_all | solution.py:47
  12.4 0.9 copy-done
  13.4 0.9 copy-done.1
  14.3 0.9 copy-done.5
  15.9 4.8 %all-to-all-done = bf16[32,8,512]{2,1,0:T(8,128)(2,1)S(1)} async-done(((bf16[32,8,512]{2,1,0:T(8,128)(2,1)}), bf16[32,8,512]{2,1,0:T(8,128)(2,1)S(1)}, u32[]{:S(2)}, u32[]{:S(2)}) %all-to-all-start) | async-done | bytes 262176 | tf_op jit(solution)/shard_map/all_to_all | solution.py:47
  20.7 1.6 %local_context.1.refs_2_ = bf16[16,40,128]{2,1,0:T(8,128)(2,1)} custom-call(bf16[256,512]{1,0:T(8,128)(2,1)S(1)} %bitcast.7, bf16[512,256]{1,0:T(8,128)(2,1)S(1)} %get-tuple-element.38.refs_1_.refs_2_, bf16[512,256]{1,0:T(8,128)(2,1)S(1)} %get-tuple-element.39.refs_2_.refs_3_), custom_call_target="tpu_custom_call" | custom-call | flops 100000000 | bytes 950272 | tf_op jit(solution)/shard_map/local_context/pallas_call | solution.py:168
  22.4 3.5 %all-to-all-start.1 = ((bf16[16,40,128]{2,1,0:T(8,128)(2,1)}), bf16[16,40,128]{2,1,0:T(8,128)(2,1)S(1)}, u32[]{:S(2)}, u32[]{:S(2)}) async-start(bf16[16,40,128]{2,1,0:T(8,128)(2,1)} %local_context.1.refs_2_), calls=%async_computation.1 | async-start | bytes 327680 | tf_op jit(solution)/shard_map/all_to_all | solution.py:47
  25.9 3.1 %inverse.1 = (f32[256,256]{1,0:T(8,128)S(1)}, f32[256,256]{1,0:T(8,128)S(1)}, f32[7,256,256]{2,1,0:T(8,128)S(1)}) custom-call(s32[2]{0:T(128)S(1)} %pad_add_fusion.refs_0_, bf16[256,512]{1,0:T(8,128)(2,1)S(1)} %bitcast.8, bf16[16,40,128]{2,1,0:T(8,128)(2,1)} %local_context.1.refs_2_), custom_call_target="tpu_custom_call" | custom-call | flops 3000000000 | bytes 2621448 | tf_op jit(solution)/shard_map/inverse/pallas_call | solution.py:168
  29.1 1.2 %copy-done.11 = f32[7,256,256]{2,1,0:T(8,128)} copy-done((f32[7,256,256]{2,1,0:T(8,128)}, f32[7,256,256]{2,1,0:T(8,128)S(1)}, u32[]{:S(2)}) %copy-start.11) | copy-done | bytes 1835032
  30.3 2.5 %all-to-all-done.1.refs_0_ = bf16[16,40,128]{2,1,0:T(8,128)(2,1)S(1)} async-done(((bf16[16,40,128]{2,1,0:T(8,128)(2,1)}), bf16[16,40,128]{2,1,0:T(8,128)(2,1)S(1)}, u32[]{:S(2)}, u32[]{:S(2)}) %all-to-all-start.1) | async-done | bytes 163872 | tf_op jit(solution)/shard_map/all_to_all | solution.py:47
  33.7 4.1 %all-to-all-start.2 = ((bf16[16,16,256]{2,1,0:T(8,128)(2,1)}), bf16[16,16,256]{2,1,0:T(8,128)(2,1)S(1)}, u32[]{:S(2)}, u32[]{:S(2)}) async-start(bf16[16,16,256]{2,1,0:T(8,128)(2,1)} %get-tuple-element.41.refs_5_.refs_3_), calls=%async_computation.2 | async-start | bytes 262144 | tf_op jit(solution)/shard_map/all_to_all | solution.py:47
  39.4 5.2 %all-to-all-done.2 = bf16[16,16,256]{2,1,0:T(8,128)(2,1)S(1)} async-done(((bf16[16,16,256]{2,1,0:T(8,128)(2,1)}), bf16[16,16,256]{2,1,0:T(8,128)(2,1)S(1)}, u32[]{:S(2)}, u32[]{:S(2)}) %all-to-all-start.2) | async-done | bytes 131104 | tf_op jit(solution)/shard_map/all_to_all | solution.py:47
  44.6 0.9 output.1
  45.5 17.4 %all_to_all.35.refs_1_ = f32[16,2,512]{2,1,0:T(2,128)S(1)} all-to-all(f32[16,2,512]{2,1,0:T(2,128)S(1)} %get-tuple-element.45), channel_id=1, replica_groups={{0,1,2,3,4,5,6,7,8,9,10,11,12,13,14,15},{16,17,18,19,20,21,22,23,24,25,..., dimensions={0} | all-to-all | bytes 131072 | tf_op jit(solution)/shard_map/all_to_all | solution.py:47
  63.0 1.7 %norm.1.refs_8_ = bf16[16,40,128]{2,1,0:T(8,128)(2,1)} custom-call(s32[2]{0:T(128)S(1)} %pad_add_fusion.refs_0_, f32[16,2,512]{2,1,0:T(2,128)S(1)} %all_to_all.35.refs_1_, f32[256,512]{1,0:T(8,128)S(1)} %get-tuple-element.46.refs_2_, bf16[256,512]{1,0:T(8,128)(2,1)S(1)} %get-tuple-element.44.refs_3_, f32[1,512]{1,0:T(1,128)S(1)} %bitcast.16, ...), custom_call_target="tpu_custom_call" | custom-call | flops 100000000 | bytes 1542152 | tf_op jit(solution)/shard_map/norm/pallas_call | solution.py:168
  64.6 3.5 %all-to-all-start.4 = ((bf16[16,40,128]{2,1,0:T(8,128)(2,1)}), bf16[16,40,128]{2,1,0:T(8,128)(2,1)S(1)}, u32[]{:S(2)}, u32[]{:S(2)}) async-start(bf16[16,40,128]{2,1,0:T(8,128)(2,1)} %norm.1.refs_8_), calls=%async_computation.4 | async-start | bytes 327680 | tf_op jit(solution)/shard_map/all_to_all | solution.py:47
  68.2 0.9 copy-done.10
  69.1 2.1 %kernel_one_back.1 = (bf16[2,256,256]{2,1,0:T(8,128)(2,1)S(1)}, bf16[2,256,256]{2,1,0:T(8,128)(2,1)S(1)}, bf16[256,256]{1,0:T(8,128)(2,1)S(1)}) custom-call(s32[2]{0:T(128)S(1)} %pad_add_fusion.refs_0_, f32[16,2,512]{2,1,0:T(2,128)S(1)} %all_to_all.35.refs_1_, f32[256,512]{1,0:T(8,128)S(1)} %get-tuple-element.46.refs_2_, ...), custom_call_target="tpu_custom_call" | custom-call | flops 2000000000 | bytes 2164744 | tf_op jit(solution)/shard_map/kernel_one_back/pallas_call | solution.py:168
  71.2 3.8 %all-to-all-done.4.refs_0_ = bf16[16,40,128]{2,1,0:T(8,128)(2,1)S(1)} async-done(((bf16[16,40,128]{2,1,0:T(8,128)(2,1)}), bf16[16,40,128]{2,1,0:T(8,128)(2,1)S(1)}, u32[]{:S(2)}, u32[]{:S(2)}) %all-to-all-start.4) | async-done | bytes 163872 | tf_op jit(solution)/shard_map/all_to_all | solution.py:47
  75.9 3.6 %all-to-all-start.5 = ((bf16[16,40,128]{2,1,0:T(8,128)(2,1)}), bf16[16,40,128]{2,1,0:T(8,128)(2,1)S(1)}, u32[]{:S(2)}, u32[]{:S(2)}) async-start(bf16[16,40,128]{2,1,0:T(8,128)(2,1)} %get-tuple-element.51.refs_5_), calls=%async_computation.5 | async-start | bytes 327680 | tf_op jit(solution)/shard_map/all_to_all | solution.py:47
  79.5 1.5 %copy-done.12 = f32[7,256,256]{2,1,0:T(8,128)S(1)} copy-done((f32[7,256,256]{2,1,0:T(8,128)S(1)}, f32[7,256,256]{2,1,0:T(8,128)}, u32[]{:S(2)}) %copy-start.12) | copy-done | bytes 1835032
  81.0 2.9 %inverse_back.1.refs_4_ = f32[256,512]{1,0:T(8,128)S(1)} custom-call(s32[2]{0:T(128)S(1)} %pad_add_fusion.refs_0_, f32[7,256,256]{2,1,0:T(8,128)S(1)} %copy-done.12, f32[24,256]{1,0:T(8,128)S(1)} %get-tuple-element.50.refs_2_, f32[16,256]{1,0:T(8,128)S(1)} %get-tuple-element.54.refs_3_, bf16[256,512]{1,0:T(8,128)(2,1)S(1)} %bitcast.11, ...), custom_call_target="tpu_custom_call" | custom-call | flops 5000000000 | bytes 2662408 | tf_op jit(solution)/shard_map/inverse_back/pallas_call | solution.py:168
  84.0 2.5 %all-to-all-done.5.refs_0_ = bf16[16,40,128]{2,1,0:T(8,128)(2,1)S(1)} async-done(((bf16[16,40,128]{2,1,0:T(8,128)(2,1)}), bf16[16,40,128]{2,1,0:T(8,128)(2,1)S(1)}, u32[]{:S(2)}, u32[]{:S(2)}) %all-to-all-start.5) | async-done | bytes 163872 | tf_op jit(solution)/shard_map/all_to_all | solution.py:47
  86.4 1.4 %landmarks_back.1 = (bf16[256,512]{1,0:T(8,128)(2,1)}, bf16[1152,128]{1,0:T(8,128)(2,1)}) custom-call(bf16[16,40,128]{2,1,0:T(8,128)(2,1)S(1)} %all-to-all-done.5.refs_0_, bf16[2,528,256]{2,1,0:T(8,128)(2,1)S(1)} %get-tuple-element.52.refs_1_, bf16[512,256]{1,0:T(8,128)(2,1)S(1)} %get-tuple-element.38.refs_1_.refs_2_, ...), custom_call_target="tpu_custom_call" | custom-call | flops 100000000 | bytes 2703360 | tf_op jit(solution)/shard_map/landmarks_back/pallas_call | solution.py:168
  87.8 3.2 %collective-permute-start.5 = (bf16[1152,128]{1,0:T(8,128)(2,1)}, bf16[1152,128]{1,0:T(8,128)(2,1)S(1)}, u32[]{:S(2)}, u32[]{:S(2)}) collective-permute-start(bf16[1152,128]{1,0:T(8,128)(2,1)} %get-tuple-element.57.refs_3_), channel_id=1, source_target_pairs={{0,8},{8,0},{16,24},{24,16},{32,40},{40,32},{48,56},{56,48},{64,72... | collective-permute-start | bytes 884744 | tf_op jit(solution)/shard_map/ppermute | solution.py:683
  91.0 4.3 %all-to-all-start.6 = ((bf16[32,8,512]{2,1,0:T(8,128)(2,1)}), bf16[32,8,512]{2,1,0:T(8,128)(2,1)S(1)}, u32[]{:S(2)}, u32[]{:S(2)}) async-start(bf16[32,8,512]{2,1,0:T(8,128)(2,1)} %bitcast.5), calls=%async_computation.6 | async-start | bytes 524288 | tf_op jit(solution)/shard_map/all_to_all | solution.py:47
  95.4 1.3 %gather.1.refs_5_ = bf16[256,512]{1,0:T(8,128)(2,1)} custom-call(s32[2]{0:T(128)S(1)} %pad_add_fusion.refs_0_, bf16[2,256,256]{2,1,0:T(8,128)(2,1)S(1)} %get-tuple-element.47.refs_1_.refs_2_, bf16[2,256,256]{2,1,0:T(8,128)(2,1)S(1)} %collective-permute-done.4.refs_2_.refs_3_, bf16[256,512]{1,0:T(8,128)(2,1)} %get-tuple-element.56.refs_3_.refs_5_), custom_call_target="tpu_custom_call" | custom-call | flops 1000000 | bytes 786440 | tf_op jit(solution)/shard_map/gather/pallas_call | solution.py:168
  96.6 2.8 %kernel_three_back.1 = (bf16[256,512]{1,0:T(8,128)(2,1)}, f32[256,512]{1,0:T(8,128)S(1)}, f32[1,512]{1,0:T(1,128)}) custom-call(s32[2]{0:T(128)S(1)} %pad_add_fusion.refs_0_, bf16[256,512]{1,0:T(8,128)(2,1)S(1)} %copy-done.2, bf16[256,512]{1,0:T(8,128)(2,1)S(1)} %copy-done.6, bf16[1152,128]{1,0:T(8,128)(2,1)} %get-tuple-element.57.refs_3_, ...), custom_call_target="tpu_custom_call" | custom-call | flops 2000000000 | bytes 1902600 | tf_op jit(solution)/shard_map/kernel_three_back/pallas_call | solution.py:168
  99.4 4.9 %all-to-all-done.6.refs_1_ = bf16[32,8,512]{2,1,0:T(8,128)(2,1)S(1)} async-done(((bf16[32,8,512]{2,1,0:T(8,128)(2,1)}), bf16[32,8,512]{2,1,0:T(8,128)(2,1)S(1)}, u32[]{:S(2)}, u32[]{:S(2)}) %all-to-all-start.6) | async-done | bytes 262176 | tf_op jit(solution)/shard_map/all_to_all | solution.py:47
  104.3 1.4 %finish.1 = (bf16[256,512]{1,0:T(8,128)(2,1)}, bf16[256,512]{1,0:T(8,128)(2,1)}) custom-call(s32[2]{0:T(128)S(1)} %pad_add_fusion.refs_0_, bf16[32,8,512]{2,1,0:T(8,128)(2,1)S(1)} %all-to-all-done.6.refs_1_, bf16[2,256,256]{2,1,0:T(8,128)(2,1)S(1)} %get-tuple-element.47.refs_1_.refs_2_, bf16[2,256,256]{2,1,0:T(8,128)(2,1)S(1)} %collective-permute-done.4.refs_2_.refs_3_, ...), custom_call_target="tpu_custom_call" | custom-call | flops 1000000 | bytes 1835016 | tf_op jit(solution)/shard_map/finish/pallas_call | solution.py:168
  (36 shorter events, 4.8 us)
Async XLA Ops:
  2.5 9.9 %collective-permute-start.2 = (bf16[256,512]{1,0:T(8,128)(2,1)}, bf16[256,512]{1,0:T(8,128)(2,1)S(1)}, u32[]{:S(2)}, u32[]{:S(2)}) collective-permute-start(bf16[256,512]{1,0:T(8,128)(2,1)} %refs_1_.7), channel_id=1, source_target_pairs={{0,8},{8,0},{16,24},{24,16},{32,40},{40,32},{48,56},{56,48},{64,72... | collective-permute-start | bytes 786440 | tf_op jit(solution)/shard_map/ppermute | solution.py:625
  5.9 6.5 %collective-permute-start.3 = (bf16[256,512]{1,0:T(8,128)(2,1)}, bf16[256,512]{1,0:T(8,128)(2,1)S(1)}, u32[]{:S(2)}, u32[]{:S(2)}) collective-permute-start(bf16[256,512]{1,0:T(8,128)(2,1)} %refs_2_.5), channel_id=1, source_target_pairs={{0,8},{8,0},{16,24},{24,16},{32,40},{40,32},{48,56},{56,48},{64,72... | collective-permute-start | bytes 786440 | tf_op jit(solution)/shard_map/ppermute | solution.py:625
  6.0 14.8 %all-to-all-start = ((bf16[32,8,512]{2,1,0:T(8,128)(2,1)}), bf16[32,8,512]{2,1,0:T(8,128)(2,1)S(1)}, u32[]{:S(2)}, u32[]{:S(2)}) async-start(bf16[32,8,512]{2,1,0:T(8,128)(2,1)} %landmark_means.1.refs_5_), calls=%async_computation | async-start | bytes 524288 | tf_op jit(solution)/shard_map/all_to_all | solution.py:47
  11.7 26.0 %collective-permute-start = (bf16[256,512]{1,0:T(8,128)(2,1)}, bf16[256,512]{1,0:T(8,128)(2,1)S(1)}, u32[]{:S(2)}, u32[]{:S(2)}) collective-permute-start(bf16[256,512]{1,0:T(8,128)(2,1)} %refs_1_.6), channel_id=1, source_target_pairs={{0,8},{8,0},{16,24},{24,16},{32,40},{40,32},{48,56},{56,48},{64,72... | collective-permute-start | bytes 786440 | tf_op jit(solution)/shard_map/ppermute | solution.py:625
  12.1 25.7 %collective-permute-start.1 = (bf16[256,512]{1,0:T(8,128)(2,1)}, bf16[256,512]{1,0:T(8,128)(2,1)S(1)}, u32[]{:S(2)}, u32[]{:S(2)}) collective-permute-start(bf16[256,512]{1,0:T(8,128)(2,1)} %refs_2_.4), channel_id=1, source_target_pairs={{0,8},{8,0},{16,24},{24,16},{32,40},{40,32},{48,56},{56,48},{64,72... | collective-permute-start | bytes 786440 | tf_op jit(solution)/shard_map/ppermute | solution.py:625
  12.4 1.0 copy-start
  13.4 0.9 copy-start.1
  14.3 0.9 copy-start.5
  22.4 10.4 %all-to-all-start.1 = ((bf16[16,40,128]{2,1,0:T(8,128)(2,1)}), bf16[16,40,128]{2,1,0:T(8,128)(2,1)S(1)}, u32[]{:S(2)}, u32[]{:S(2)}) async-start(bf16[16,40,128]{2,1,0:T(8,128)(2,1)} %local_context.1.refs_2_), calls=%async_computation.1 | async-start | bytes 327680 | tf_op jit(solution)/shard_map/all_to_all | solution.py:47
  25.9 11.9 %copy-start.3 = (bf16[256,512]{1,0:T(8,128)(2,1)S(1)}, bf16[256,512]{1,0:T(8,128)(2,1)}, u32[]{:S(2)}) copy-start(bf16[256,512]{1,0:T(8,128)(2,1)} %refs_1_.6) | copy-start | bytes 786436
  25.9 11.9 %copy-start.7 = (bf16[256,512]{1,0:T(8,128)(2,1)S(1)}, bf16[256,512]{1,0:T(8,128)(2,1)}, u32[]{:S(2)}) copy-start(bf16[256,512]{1,0:T(8,128)(2,1)} %refs_2_.4) | copy-start | bytes 786436
  29.0 1.3 %copy-start.11 = (f32[7,256,256]{2,1,0:T(8,128)}, f32[7,256,256]{2,1,0:T(8,128)S(1)}, u32[]{:S(2)}) copy-start(f32[7,256,256]{2,1,0:T(8,128)S(1)} %get-tuple-element.53.refs_1_) | copy-start | bytes 5505028
  33.7 10.9 %all-to-all-start.2 = ((bf16[16,16,256]{2,1,0:T(8,128)(2,1)}), bf16[16,16,256]{2,1,0:T(8,128)(2,1)S(1)}, u32[]{:S(2)}, u32[]{:S(2)}) async-start(bf16[16,16,256]{2,1,0:T(8,128)(2,1)} %get-tuple-element.41.refs_5_.refs_3_), calls=%async_computation.2 | async-start | bytes 262144 | tf_op jit(solution)/shard_map/all_to_all | solution.py:47
  38.5 0.9 copy-start.9
  38.5 6.1 %copy-start.8 = (f32[512]{0:T(512)S(1)}, f32[512]{0:T(512)}, u32[]{:S(2)}) copy-start(f32[512]{0:T(512)} %param.8) | copy-start | bytes 6148
  64.6 10.4 %all-to-all-start.4 = ((bf16[16,40,128]{2,1,0:T(8,128)(2,1)}), bf16[16,40,128]{2,1,0:T(8,128)(2,1)S(1)}, u32[]{:S(2)}, u32[]{:S(2)}) async-start(bf16[16,40,128]{2,1,0:T(8,128)(2,1)} %norm.1.refs_8_), calls=%async_computation.4 | async-start | bytes 327680 | tf_op jit(solution)/shard_map/all_to_all | solution.py:47
  68.2 1.0 copy-start.10
  75.9 10.5 %all-to-all-start.5 = ((bf16[16,40,128]{2,1,0:T(8,128)(2,1)}), bf16[16,40,128]{2,1,0:T(8,128)(2,1)S(1)}, u32[]{:S(2)}, u32[]{:S(2)}) async-start(bf16[16,40,128]{2,1,0:T(8,128)(2,1)} %get-tuple-element.51.refs_5_), calls=%async_computation.5 | async-start | bytes 327680 | tf_op jit(solution)/shard_map/all_to_all | solution.py:47
  79.5 1.5 %copy-start.12 = (f32[7,256,256]{2,1,0:T(8,128)S(1)}, f32[7,256,256]{2,1,0:T(8,128)}, u32[]{:S(2)}) copy-start(f32[7,256,256]{2,1,0:T(8,128)} %copy-done.11) | copy-start | bytes 5505028
  86.4 10.2 %copy-start.2 = (bf16[256,512]{1,0:T(8,128)(2,1)S(1)}, bf16[256,512]{1,0:T(8,128)(2,1)}, u32[]{:S(2)}) copy-start(bf16[256,512]{1,0:T(8,128)(2,1)} %refs_1_.7) | copy-start | bytes 786436
  86.4 10.2 %copy-start.6 = (bf16[256,512]{1,0:T(8,128)(2,1)S(1)}, bf16[256,512]{1,0:T(8,128)(2,1)}, u32[]{:S(2)}) copy-start(bf16[256,512]{1,0:T(8,128)(2,1)} %refs_2_.5) | copy-start | bytes 786436
  87.8 8.8 %collective-permute-start.5 = (bf16[1152,128]{1,0:T(8,128)(2,1)}, bf16[1152,128]{1,0:T(8,128)(2,1)S(1)}, u32[]{:S(2)}, u32[]{:S(2)}) collective-permute-start(bf16[1152,128]{1,0:T(8,128)(2,1)} %get-tuple-element.57.refs_3_), channel_id=1, source_target_pairs={{0,8},{8,0},{16,24},{24,16},{32,40},{40,32},{48,56},{56,48},{64,72... | collective-permute-start | bytes 884744 | tf_op jit(solution)/shard_map/ppermute | solution.py:683
  91.0 4.3 %collective-permute-start.4 = (bf16[2,256,256]{2,1,0:T(8,128)(2,1)S(1)}, bf16[2,256,256]{2,1,0:T(8,128)(2,1)S(1)}, u32[]{:S(2)}, u32[]{:S(2)}) collective-permute-start(bf16[2,256,256]{2,1,0:T(8,128)(2,1)S(1)} %get-tuple-element.48.refs_3_), channel_id=1, source_target_pairs={{0,8},{8,0},{16,24},{24,16},{32,40},{40,32},{48,56},{56,48},{64,72... | collective-permute-start | bytes 786440 | tf_op jit(solution)/shard_map/ppermute | solution.py:682
  91.0 13.3 %all-to-all-start.6 = ((bf16[32,8,512]{2,1,0:T(8,128)(2,1)}), bf16[32,8,512]{2,1,0:T(8,128)(2,1)S(1)}, u32[]{:S(2)}, u32[]{:S(2)}) async-start(bf16[32,8,512]{2,1,0:T(8,128)(2,1)} %bitcast.5), calls=%async_computation.6 | async-start | bytes 524288 | tf_op jit(solution)/shard_map/all_to_all | solution.py:47
  96.6 7.7 %copy-start.4 = (bf16[256,512]{1,0:T(8,128)(2,1)S(1)}, bf16[256,512]{1,0:T(8,128)(2,1)}, u32[]{:S(2)}) copy-start(bf16[256,512]{1,0:T(8,128)(2,1)} %gather.1.refs_5_) | copy-start | bytes 786436
